TPU v7x, 256 devices: a whole 4x4x8 slice. The times are simulated.
256 devices in a mesh: grp: 8 (over x, core), dev: 32 (over y, z).
Axes of the slice: x: 4, y: 4, z: 8, core: 2. Of those that a mesh axis runs over, the one named last changes fastest.
Arguments:
- queries: bfloat16 [1024, 16, 4096], P(('grp', 'dev')), may hold values from -25.849872 to 25.849872
- own_keys: bfloat16 [1024, 16, 1024], P(('grp', 'dev')), may hold values from -18 to 18
- own_values: bfloat16 [1024, 16, 1024], P(('grp', 'dev')), may hold values from -48 to 48
- prefix_keys: bfloat16 [1024, 1024], P('grp'), may hold values from -6 to 6
- prefix_values: bfloat16 [1024, 1024], P('grp'), may hold values from -48 to 48
- passage_keys: bfloat16 [32, 512, 1024], P('dev'), may hold values from -6 to 6
- passage_values: bfloat16 [32, 512, 1024], P('dev'), may hold values from -48 to 48
- retrieval: int32 [1024, 8], P(('grp', 'dev')), may hold values from 0 to 31, all different within a row; in each aligned block of 4 rows (0 to 3, 4 to 7, ...) at most 2 rows name the same one
- location: int32 [32], replicated, may hold values from 0 to 31, each once
Outputs:
- attended: bfloat16 [1024, 16, 4096], P(('grp', 'dev'))
Inputs may be any that keep to these rules, and one draw needn't show every extreme that they name: `retrieval`: each response names 8 different passages. The 4 responses of one device name one passage at most 2 times together, and on some devices some passage exactly 2 times. `location`: each position is taken by exactly one passage.
All inputs are finite; a program needn't handle non-finite values.
Results may differ from a plain program's by a relative error of at most 0.004.
Values may be sent and summed in bfloat16 or wider, within the bound.
No kernel may reach another device: no remote copies, remote signals or barrier semaphores. Data moves between devices by JAX's collectives and lax.ppermute only.
A program may use at most 192 MiB of HBM per device.

v0:
```python
import math

import jax
import jax.numpy as jnp
from jax import lax
from jax.sharding import PartitionSpec as P

HEADS = 32
KEY_VALUE_HEADS = 8
HEAD_WIDTH = 128
TOPK = 8


def softmax_part(scores, values, form):
    maxima = jnp.max(scores, axis=-1)
    weights = jnp.exp(scores - maxima[..., None])
    totals = jnp.sum(weights, axis=-1)
    mixed = jnp.einsum(
        form, weights.astype(jnp.bfloat16), values, preferred_element_type=jnp.float32
    )
    return (mixed / totals[..., None], maxima + jnp.log(totals))


def block_attend(grid, keys, values, scale):
    rows = grid.shape[0]
    block = math.gcd(rows, 512)
    key_grid = keys.reshape(-1, KEY_VALUE_HEADS, HEAD_WIDTH)
    value_grid = values.reshape(-1, KEY_VALUE_HEADS, HEAD_WIDTH)

    def one_block(portion):
        scores = (
            jnp.einsum("tkgd,skd->tkgs", portion, key_grid, preferred_element_type=jnp.float32)
            * scale
        )
        return softmax_part(scores, value_grid, "tkgs,skd->tkgd")

    blocks = grid.reshape((rows // block, block) + grid.shape[1:])
    mixed, level = lax.map(one_block, blocks)
    return (mixed.reshape(grid.shape), level.reshape(grid.shape[:-1]))


def per_device(
    queries,
    own_keys,
    own_values,
    prefix_keys,
    prefix_values,
    passage_keys,
    passage_values,
    retrieval,
    location,
):
    query_group = HEADS // KEY_VALUE_HEADS
    scale = 1.0 / math.sqrt(HEAD_WIDTH)
    resp, response_tokens, width = queries.shape
    tokens = resp * response_tokens
    grid = queries.reshape(tokens, KEY_VALUE_HEADS, query_group, HEAD_WIDTH)
    own_scores = (
        jnp.einsum(
            "rtkgd,rskd->rtkgs",
            queries.reshape(resp, response_tokens, KEY_VALUE_HEADS, query_group, HEAD_WIDTH),
            own_keys.reshape(resp, response_tokens, KEY_VALUE_HEADS, HEAD_WIDTH),
            preferred_element_type=jnp.float32,
        )
        * scale
    )
    causal = jnp.arange(response_tokens)[:, None] >= jnp.arange(response_tokens)[None, :]
    own_scores = jnp.where(causal[None, :, None, None, :], own_scores, -jnp.inf)
    own_out, own_lse = softmax_part(
        own_scores,
        own_values.reshape(resp, response_tokens, KEY_VALUE_HEADS, HEAD_WIDTH),
        "rtkgs,rskd->rtkgd",
    )
    maxima = jnp.full((tokens, KEY_VALUE_HEADS, query_group), -jnp.inf, jnp.float32)
    totals = jnp.zeros((tokens, KEY_VALUE_HEADS, query_group), jnp.float32)
    mixed = jnp.zeros((tokens, KEY_VALUE_HEADS, query_group, HEAD_WIDTH), jnp.float32)
    key_grid = lax.all_gather(prefix_keys, "grp", axis=0, tiled=True).reshape(
        -1, KEY_VALUE_HEADS, HEAD_WIDTH
    )
    value_grid = lax.all_gather(prefix_values, "grp", axis=0, tiled=True).reshape(
        -1, KEY_VALUE_HEADS, HEAD_WIDTH
    )
    scores = (
        jnp.einsum("tkgd,skd->tkgs", grid, key_grid, preferred_element_type=jnp.float32) * scale
    )
    newmax = jnp.max(scores, axis=-1)
    shrink = jnp.exp(maxima - newmax)
    weights = jnp.exp(scores - newmax[..., None])
    totals = totals * shrink + jnp.sum(weights, axis=-1)
    mixed = mixed * shrink[..., None] + jnp.einsum(
        "tkgs,skd->tkgd",
        weights.astype(jnp.bfloat16),
        value_grid,
        preferred_element_type=jnp.float32,
    )
    maxima, totals, mixed = (newmax, totals, mixed)
    pre_out = mixed / totals[..., None]
    pre_lse = maxima + jnp.log(totals)
    device_total = lax.axis_size("dev")
    largest_count = min(resp, max(2, 2 * resp * TOPK // device_total))
    slot_total = device_total * largest_count
    passages = location.shape[0]
    passage_ids = jnp.arange(passages, dtype=jnp.int32)
    flat_ids = retrieval.reshape(-1)
    requests = flat_ids.shape[0]
    owners = jnp.sum(
        jnp.where(flat_ids[:, None] == passage_ids[None, :], location[None, :], 0), axis=1
    )
    order = jnp.arange(requests, dtype=jnp.int32)
    earlier = (owners[:, None] == owners[None, :]) & (order[None, :] < order[:, None])
    ranks = jnp.sum(earlier.astype(jnp.int32), axis=1)
    slots = owners * largest_count + ranks
    local_keys = passage_keys[0]
    local_values = passage_values[0]
    seen_queries, seen_lists = (
        lax.all_gather(queries, "dev", axis=0, tiled=True),
        lax.all_gather(retrieval, "dev", axis=0, tiled=True),
    )
    seen_queries = seen_queries.reshape(device_total, resp, response_tokens, width)
    seen_lists = seen_lists.reshape(device_total, requests)
    seen_owner = jnp.sum(
        jnp.where(seen_lists[:, :, None] == passage_ids[None, None, :], location[None, None, :], 0),
        axis=2,
    )
    mine = seen_owner == lax.axis_index("dev")
    seen_rank = jnp.cumsum(mine.astype(jnp.int32), axis=1) - 1
    seen_hits = mine[:, None, :] & (
        seen_rank[:, None, :] == jnp.arange(largest_count, dtype=jnp.int32)[None, :, None]
    )
    seen_source = jnp.sum(jnp.where(seen_hits, order[None, None, :] // TOPK, 0), axis=2)
    seen_filled = jnp.any(seen_hits, axis=2)
    picked = jnp.take_along_axis(seen_queries, seen_source[:, :, None, None], axis=1)
    arrived = jnp.where(seen_filled[:, :, None, None], picked, jnp.zeros((), jnp.bfloat16))
    senders = arrived.shape[0]
    count = arrived.shape[1]
    arrived_grid = arrived.reshape(-1, KEY_VALUE_HEADS, query_group, HEAD_WIDTH)
    block_out, block_lse = block_attend(arrived_grid, local_keys, local_values, scale)
    block_out = block_out.reshape(senders, count, response_tokens, width).astype(jnp.bfloat16)
    block_lse = block_lse.reshape(senders, count, response_tokens, HEADS)
    returned_out = lax.all_to_all(block_out, "dev", split_axis=0, concat_axis=0, tiled=True)
    returned_lse = lax.all_to_all(block_lse, "dev", split_axis=0, concat_axis=0, tiled=True)
    slot_lookup_table = slots.reshape(resp, TOPK)
    selected_output = returned_out.reshape(
        slot_total, response_tokens, KEY_VALUE_HEADS, query_group, HEAD_WIDTH
    )[slot_lookup_table].astype(jnp.float32)
    selected_log_normalizer = returned_lse.reshape(
        slot_total, response_tokens, KEY_VALUE_HEADS, query_group
    )[slot_lookup_table]
    pre_out = pre_out.reshape(resp, response_tokens, KEY_VALUE_HEADS, query_group, HEAD_WIDTH)
    pre_lse = pre_lse.reshape(resp, response_tokens, KEY_VALUE_HEADS, query_group)
    top_level = jnp.maximum(jnp.maximum(pre_lse, own_lse), jnp.max(selected_log_normalizer, axis=1))
    total = (
        jnp.exp(pre_lse - top_level)
        + jnp.exp(own_lse - top_level)
        + jnp.sum(jnp.exp(selected_log_normalizer - top_level[:, None]), axis=1)
    )
    level = top_level + jnp.log(total)
    result = (
        jnp.exp(pre_lse - level)[..., None] * pre_out
        + jnp.exp(own_lse - level)[..., None] * own_out
    )
    result = result + jnp.sum(
        jnp.exp(selected_log_normalizer - level[:, None])[..., None] * selected_output, axis=1
    )
    return result.reshape(resp, response_tokens, width).astype(jnp.bfloat16)


def solution(mesh):
    placed = (
        P(("grp", "dev"), None, None),
        P(("grp", "dev"), None, None),
        P(("grp", "dev"), None, None),
        P("grp", None),
        P("grp", None),
        P("dev", None, None),
        P("dev", None, None),
        P(("grp", "dev"), None),
        P(),
    )
    return jax.shard_map(
        per_device,
        mesh=mesh,
        in_specs=placed,
        out_specs=P(("grp", "dev"), None, None),
        check_vma=False,
    )
```

profile of v0, /device:TPU:1, one launch (start us, length us, event | category | flops | bytes accessed | tf_op | source)
XLA Modules:
  0.0 551.7 jit_solution(14876546210618163699)
XLA Ops:
  8.1 43.3 %all-gather = s32[32,4,8]{2,1,0:T(4,128)S(1)} all-gather(s32[1,4,8]{2,1,0:T(4,128)} %bitcast.165), channel_id=1, replica_groups=mesh['grp'=8,'dev'=32] {'dev'}, dimensions={0}, use_global_device_ids=true | all-gather | bytes 4224 | tf_op jit(solution)/shard_map/all_gather | solution.py:117
  51.6 1.4 select_reduce_fusion
  54.4 1.5 copy.205
  56.5 1.5 copy.206
  58.8 95.6 %all-gather.7.cloned.1.call-done = bf16[128,16,4096]{2,1,0:T(8,128)(2,1)} async-done(((bf16[4,16,4096]{2,1,0:T(8,128)(2,1)}), bf16[128,16,4096]{2,1,0:T(8,128)(2,1)}) %all-gather.7.cloned.1.call-update) | async-done | bytes 16777232 | tf_op jit(solution)/shard_map/all_gather | solution.py:116
  154.4 11.6 %gather_fusion.2 = bf16[64,16,4096]{2,1,0:T(8,128)(2,1)} fusion(bf16[32,4,16,4096]{3,2,1,0:T(8,128)(2,1)} %bitcast.156, s32[64]{0:T(128)S(1)} %reshape.338), kind=kCustom, calls=%fused_computation.2 | custom fusion | bytes 16777728 | tf_op jit(solution)/shard_map/jit(take_along_axis)/gather | solution.py:132
  166.0 14.3 %gather.13 = bf16[2,512,8,4,128]{4,3,2,1,0:T(4,128)(2,1)} reshape(bf16[64,16,4096]{2,1,0:T(8,128)(2,1)} %gather_fusion.2) | data formatting | bytes 16777216 | tf_op jit(solution)/shard_map/jit(take_along_axis)/gather | solution.py:132
  180.2 8.5 %select_select_fusion = bf16[2,512,8,4,128]{4,3,2,1,0:T(4,128)(2,1)} fusion(bf16[2,512,8,4,128]{4,3,2,1,0:T(4,128)(2,1)} %gather.13, pred[2,512]{1,0:T(4,128)(4,1)S(1)} %broadcast_in_dim.144, pred[2,512]{1,0:T(4,128)(4,1)S(1)} %broadcast_in_dim.139), kind=kLoop, calls=%fused_computation.25 | loop fusion | flops 8388608 | bytes 16779264 | tf_op jit(solution)/shard_map/jit(_where)/select_n | solution.py:133
  188.8 94.7 %while.12 = (s32[]{:T(128)}, bf16[2,512,8,4,128]{4,1,3,2,0:T(8,128)(2,1)}, f32[2,512,8,4]{1,0,3,2:T(2,128)S(1)}, bf16[2,512,8,4,128]{4,3,2,1,0:T(4,128)(2,1)}, b...) while((s32[]{:T(128)}, ...), condition=%wide.region_11.12_spmd, body=%wide.region_8.11_spmd.sunk | while | flops 4364156928 | bytes 124519000 | solution.py:38
  188.8 3.6 constant_dynamic-slice_fusion.2
  192.4 13.6 %bitcast_reduce_fusion.4 = (f32[512,8,4]{0,2,1:T(4,128)S(1)}, f32[8,512,4,512]{1,3,2,0:T(8,128)}) fusion(bf16[512,8,128]{2,0,1:T(8,128)(2,1)S(1)} %get-tuple-element.161, bf16[1,512,8,4,128]{4,3,2,1,0:T(4,128)(2,1)S(1)} %constant_dynamic-slice_fusion.2), kind=kOutput, calls=%fused_computation.4.clone.1 | convolution fusion | flops 2164244480 | bytes 38862848 | tf_op jit(solution)/shard_map/while/body/eval_jaxpr/tkgd,skd->tkgs/dot_general | solution.py:32
  206.0 13.6 %fusion.71 = f32[512,8,4]{0,2,1:T(4,128)S(1)} fusion(f32[8,512,4,512]{1,3,2,0:T(8,128)} %get-tuple-element.139, f32[512,8,4]{0,2,1:T(4,128)S(1)} %get-tuple-element.140), kind=kLoop, calls=%fused_computation.6.clone.1 | loop fusion | flops 25149440 | bytes 33685504 | tf_op jit(solution)/shard_map/while/body/eval_jaxpr/reduce_sum | solution.py:17
  220.3 15.9 %bitcast_dynamic-update-slice_fusion.2 = bf16[2,512,8,4,128]{4,1,3,2,0:T(8,128)(2,1)} fusion(bf16[2,512,8,4,128]{4,1,3,2,0:T(8,128)(2,1)} %get-tuple-element.150, s32[]{:T(128)} %get-tuple-element.149, f32[512,8,4]{0,2,1:T(4,128)S(1)} %fusion.71, f32[8,512,4,512]{1,3,2,0:T(8,128)} %get-tuple-element.139, f32[512,8,4]{0,2,1:T(4,128)S(1)} %get-tuple-element.140, ...), kind=kOutput, calls=%fused_computation.11.clone.1 | convolution fusion | flops 2174746624 | bytes 43123200 | tf_op jit(solution)/shard_map/while/body/eval_jaxpr/tkgs,skd->tkgd/dot_general | solution.py:18
  236.1 3.6 constant_dynamic-slice_fusion.2
  239.8 13.6 %bitcast_reduce_fusion.4 = (f32[512,8,4]{0,2,1:T(4,128)S(1)}, f32[8,512,4,512]{1,3,2,0:T(8,128)}) fusion(bf16[512,8,128]{2,0,1:T(8,128)(2,1)S(1)} %get-tuple-element.161, bf16[1,512,8,4,128]{4,3,2,1,0:T(4,128)(2,1)S(1)} %constant_dynamic-slice_fusion.2), kind=kOutput, calls=%fused_computation.4.clone.1 | convolution fusion | flops 2164244480 | bytes 38862848 | tf_op jit(solution)/shard_map/while/body/eval_jaxpr/tkgd,skd->tkgs/dot_general | solution.py:32
  253.3 13.6 %fusion.71 = f32[512,8,4]{0,2,1:T(4,128)S(1)} fusion(f32[8,512,4,512]{1,3,2,0:T(8,128)} %get-tuple-element.139, f32[512,8,4]{0,2,1:T(4,128)S(1)} %get-tuple-element.140), kind=kLoop, calls=%fused_computation.6.clone.1 | loop fusion | flops 25149440 | bytes 33685504 | tf_op jit(solution)/shard_map/while/body/eval_jaxpr/reduce_sum | solution.py:17
  267.6 15.8 %bitcast_dynamic-update-slice_fusion.2 = bf16[2,512,8,4,128]{4,1,3,2,0:T(8,128)(2,1)} fusion(bf16[2,512,8,4,128]{4,1,3,2,0:T(8,128)(2,1)} %get-tuple-element.150, s32[]{:T(128)} %get-tuple-element.149, f32[512,8,4]{0,2,1:T(4,128)S(1)} %fusion.71, f32[8,512,4,512]{1,3,2,0:T(8,128)} %get-tuple-element.139, f32[512,8,4]{0,2,1:T(4,128)S(1)} %get-tuple-element.140, ...), kind=kOutput, calls=%fused_computation.11.clone.1 | convolution fusion | flops 2174746624 | bytes 43123200 | tf_op jit(solution)/shard_map/while/body/eval_jaxpr/tkgs,skd->tkgd/dot_general | solution.py:18
  286.4 5.3 all-to-all-start
  291.8 12.2 %copy.225 = bf16[2,512,8,4,128]{4,3,2,1,0:T(4,128)(2,1)} copy(bf16[2,512,8,4,128]{4,1,3,2,0:T(8,128)(2,1)} %get-tuple-element.39) | data formatting | bytes 16777216 | tf_op jit(solution)/shard_map/convert_element_type | solution.py:138
  303.9 14.5 %convert_element_type.39 = bf16[32,2,16,4096]{3,2,1,0:T(8,128)(2,1)} reshape(bf16[2,512,8,4,128]{4,3,2,1,0:T(4,128)(2,1)} %copy.225) | data formatting | bytes 16777216 | tf_op jit(solution)/shard_map/convert_element_type | solution.py:138
  318.5 9.5 %all-to-all-start.1 = ((bf16[32,2,16,4096]{3,2,1,0:T(8,128)(2,1)}), bf16[32,2,16,4096]{3,2,1,0:T(8,128)(2,1)}, u32[]{:S(2)}, u32[]{:S(2)}) async-start(bf16[32,2,16,4096]{3,2,1,0:T(8,128)(2,1)} %convert_element_type.39), calls=%async_computation.1 | async-start | bytes 16777216 | tf_op jit(solution)/shard_map/all_to_all | solution.py:140
  333.1 29.3 %all-gather.5.cloned.1.call-done = bf16[1024,1024]{0,1:T(8,128)(2,1)} async-done(((bf16[128,1024]{0,1:T(8,128)(2,1)}), bf16[1024,1024]{0,1:T(8,128)(2,1)}) %all-gather.5.cloned.1.call-update) | async-done | bytes 2097168 | tf_op jit(solution)/shard_map/all_gather | solution.py:77
  362.4 6.1 %bitcast_reduce_fusion.1 = (f32[64,8,4]{0,2,1:T(4,128)S(1)}, f32[8,1024,64,4]{1,2,3,0:T(8,128)}) fusion(bf16[1024,8,128,1]{0,2,3,1:T(8,128)(2,1)} %bitcast.159, bf16[64,8,4,128]{3,2,1,0:T(4,128)(2,1)S(1)} %reshape.313), kind=kOutput, calls=%fused_computation.23 | convolution fusion | flops 541063168 | bytes 11018240 | tf_op jit(solution)/shard_map/tkgd,skd->tkgs/dot_general | solution.py:84
  368.6 4.6 fusion.16
  373.3 21.1 %all-gather.9.cloned.1.call-done = bf16[1024,1024]{0,1:T(8,128)(2,1)} async-done(((bf16[128,1024]{0,1:T(8,128)(2,1)}), bf16[1024,1024]{0,1:T(8,128)(2,1)}) %all-gather.9.cloned.1.call-update) | async-done | bytes 2097168 | tf_op jit(solution)/shard_map/all_gather | solution.py:80
  394.5 6.0 %fusion.34 = f32[64,8,4,128]{3,0,2,1:T(8,128)} fusion(bf16[1024,8,128,1]{0,2,3,1:T(8,128)(2,1)} %bitcast.166, f32[8,1024,64,4]{1,2,3,0:T(8,128)} %get-tuple-element.97, f32[64,8,4]{0,2,1:T(4,128)S(1)} %get-tuple-element.96, f32[64,8,4]{0,2,1:T(4,128)S(1)} %get-tuple-element.95, f32[64,8,4]{0,2,1:T(4,128)S(1)} %get-tuple-element.94), kind=kOutput, calls=%fused_computation.44 | convolution fusion | flops 543686656 | bytes 11558912 | tf_op jit(solution)/shard_map/tkgs,skd->tkgd/dot_general | solution.py:90
  404.9 2.6 copy.224
  408.2 102.4 %all-to-all-done.1 = bf16[32,2,16,4096]{3,2,1,0:T(8,128)(2,1)} async-done(((bf16[32,2,16,4096]{3,2,1,0:T(8,128)(2,1)}), bf16[32,2,16,4096]{3,2,1,0:T(8,128)(2,1)}, u32[]{:S(2)}, u32[]{:S(2)}) %all-to-all-start.1) | async-done | bytes 8388640 | tf_op jit(solution)/shard_map/all_to_all | solution.py:140
  510.6 14.3 %reshape.321 = bf16[64,16,8,4,128]{4,3,2,1,0:T(4,128)(2,1)} reshape(bf16[32,2,16,4096]{3,2,1,0:T(8,128)(2,1)} %all-to-all-done.1) | data formatting | bytes 16777216 | tf_op jit(solution)/shard_map/reshape | solution.py:143
  524.9 9.1 %gather_fusion.1 = bf16[32,16,8,4,128]{4,3,2,1,0:T(4,128)(2,1)} fusion(bf16[64,16,8,4,128]{4,3,2,1,0:T(4,128)(2,1)} %reshape.321, s32[1024]{0:T(1024)S(1)} %pad_clamp_fusion), kind=kCustom, calls=%fused_computation.1 | custom fusion | bytes 8388736 | tf_op jit(solution)/shard_map/gather | solution.py:143
  534.1 6.4 %fusion.13 = f32[4,16,8,4,128]{4,3,2,1,0:T(4,128)S(1)} fusion(f32[4,8,16,8,4]{4,3,2,1,0:T(8,128)S(1)} %copy.224, bf16[32,16,8,4,128]{4,3,2,1,0:T(4,128)(2,1)} %gather_fusion.1), kind=kLoop, calls=%fused_computation.21 | loop fusion | flops 6029312 | bytes 5308416 | tf_op jit(solution)/shard_map/reduce_sum | solution.py:162
  540.5 2.3 fusion.33
  (93 shorter events, 19.5 us)
Async XLA Ops:
  7.4 147.0 %all-gather.7.cloned.1.call-start = ((), (), s32[]{:S(2)}) async-start(), calls=%async_computation.3 | async-start | bytes 17301504 | tf_op jit(solution)/shard_map/all_gather | solution.py:116
  286.4 32.0 %all-to-all-start = ((f32[32,1,1024]{2,1,0:T(1,128)}), f32[32,1,1024]{2,1,0:T(1,128)S(1)}, u32[]{:S(2)}, u32[]{:S(2)}) async-start(f32[32,1,1024]{2,1,0:T(1,128)} %reshape.359), calls=%async_computation | async-start | bytes 262144 | tf_op jit(solution)/shard_map/all_to_all | solution.py:141
  318.4 9.6 %copy-start.1 = (bf16[128,1024]{1,0:T(8,128)(2,1)S(1)}, bf16[128,1024]{1,0:T(8,128)(2,1)}, u32[]{:S(2)}) copy-start(bf16[128,1024]{1,0:T(8,128)(2,1)} %param.14) | copy-start | bytes 786436
  318.4 10.5 %copy-start.2 = (bf16[128,1024]{1,0:T(8,128)(2,1)S(1)}, bf16[128,1024]{1,0:T(8,128)(2,1)}, u32[]{:S(2)}) copy-start(bf16[128,1024]{1,0:T(8,128)(2,1)} %param.15) | copy-start | bytes 786436
  318.4 11.4 %copy-start.6 = (s32[4,8]{1,0:T(4,128)S(1)}, s32[4,8]{1,0:T(4,128)}, u32[]{:S(2)}) copy-start(s32[4,8]{1,0:T(4,128)} %param.18) | copy-start | bytes 388
  318.4 11.5 %copy-start = (bf16[4,16,4096]{2,1,0:T(8,128)(2,1)S(1)}, bf16[4,16,4096]{2,1,0:T(8,128)(2,1)}, u32[]{:S(2)}) copy-start(bf16[4,16,4096]{2,1,0:T(8,128)(2,1)} %param.11) | copy-start | bytes 1572868
  318.4 12.3 %copy-start.7 = (s32[32]{0:T(128)S(1)}, s32[32]{0:T(128)}, u32[]{:S(2)}) copy-start(s32[32]{0:T(128)} %param.19) | copy-start | bytes 388
  318.5 12.8 %copy-start.3 = (bf16[4,16,1024]{2,1,0:T(8,128)(2,1)S(1)}, bf16[4,16,1024]{2,1,0:T(8,128)(2,1)}, u32[]{:S(2)}) copy-start(bf16[4,16,1024]{2,1,0:T(8,128)(2,1)} %param.12) | copy-start | bytes 393220
  318.5 12.8 %copy-start.4 = (bf16[4,16,1024]{2,1,0:T(8,128)(2,1)S(1)}, bf16[4,16,1024]{2,1,0:T(8,128)(2,1)}, u32[]{:S(2)}) copy-start(bf16[4,16,1024]{2,1,0:T(8,128)(2,1)} %param.13) | copy-start | bytes 393220
  318.5 192.1 %all-to-all-start.1 = ((bf16[32,2,16,4096]{3,2,1,0:T(8,128)(2,1)}), bf16[32,2,16,4096]{3,2,1,0:T(8,128)(2,1)}, u32[]{:S(2)}, u32[]{:S(2)}) async-start(bf16[32,2,16,4096]{3,2,1,0:T(8,128)(2,1)} %convert_element_type.39), calls=%async_computation.1 | async-start | bytes 16777216 | tf_op jit(solution)/shard_map/all_to_all | solution.py:140
  328.0 34.4 %all-gather.5.cloned.1.call-start = ((), (), s32[]{:S(2)}) async-start(), calls=%async_computation.2 | async-start | bytes 2359296 | tf_op jit(solution)/shard_map/all_gather | solution.py:77
  328.9 65.6 %all-gather.9.cloned.1.call-start = ((), (), s32[]{:S(2)}) async-start(), calls=%async_computation.4 | async-start | bytes 2359296 | tf_op jit(solution)/shard_map/all_gather | solution.py:80
  524.9 15.6 %copy-start.5 = (f32[4,16,8,4]{1,3,2,0:T(4,128)S(1)}, f32[4,16,8,4]{1,3,2,0:T(4,128)}, u32[]{:S(2)}) copy-start(f32[4,16,8,4]{1,3,2,0:T(4,128)} %copy.216) | copy-start | bytes 24580
Sparse Core Ops, SparseCore 0:
  10.8 143.5 all-gather.6
Sparse Core Ops, SparseCore 1:
  330.3 32.1 all-gather.4
  364.1 30.3 all-gather.8
where the time goes:
time: 559 us; the launch traced here: 552 us
  waiting for transfers between devices  249 us (45%)
  local copies, waits for them, and re-layouts  102 us (18%)
  matrix products  74.6 us (13%)
  other arithmetic  51.9 us (9%)
  blocking collectives  43.3 us (8%)
  between operations  15.3 us (3%)
  starting transfers between devices  14.9 us (3%)
    all_to_all x1, waiting for transfers between devices, per_device(): lax.all_to_all(block_out, 'dev', split_axis=0, concat_axis=0, tiled=True)  102 us
    all_gather x1, waiting for transfers between devices, per_device(): lax.all_gather(queries, 'dev', axis=0, tiled=True)  95.6 us
    all_gather x1, blocking collectives, per_device(): lax.all_gather(retrieval, 'dev', axis=0, tiled=True)  43.3 us
    dot_general x3, matrix products, softmax_part(): jnp.einsum(form, weights.astype(jnp.bfloat16), values, preferred_element_...  34 us
    all_gather x1, waiting for transfers between devices, per_device(): lax.all_gather(prefix_keys, 'grp', axis=0, tiled=True)  29.3 us
    reduce_sum x3, other arithmetic, softmax_part(): totals = jnp.sum(weights, axis=-1)  27.5 us
    dot_general x2, matrix products, one_block(): jnp.einsum('tkgd,skd->tkgs', portion, key_grid, preferred_element_type=jn...  27.1 us
    convert_element_type x2, local copies, waits for them, and re-layouts, per_device(): block_out.reshape(senders, count, response_tokens, width)  26.7 us
  transfers between devices with their start and end apart: 5, of which 4 were waited for; matrix products, arithmetic and copies ran while one was open for 11% of the time, Pallas kernels for 0%

commit v1 on v0

v1 whole, which is shorter than its diff:
```python
import functools
import math

import jax
import jax.numpy as jnp
from jax import lax
from jax.experimental import pallas as pl
from jax.experimental.pallas import tpu as pltpu
from jax.sharding import PartitionSpec as P

HEADS = 32
KV = 8
D = 128
TOPK = 8
NX, NC, NY, NZ = 4, 2, 4, 8
AXES = ("grp", "dev")
RESP = 4
T = 16
GROUP = HEADS // KV
ROWS = GROUP * T
NR = 8 * RESP
SLOTS = NR + 1
BATCH = 4
COEF = math.log2(math.e) / math.sqrt(D)


def index_of(x, c, y, z):
    return ((x % NX) * NC + c) * (NY * NZ) + (y % NY) * NZ + z % NZ


def moves(to):
    places = [
        (x, c, y, z) for x in range(NX) for c in range(NC) for y in range(NY) for z in range(NZ)
    ]
    return [(index_of(*p), index_of(*to(*p))) for p in places]


def send(block, to):
    return lax.ppermute(block, AXES, moves(to))


def y_by(step):
    return lambda x, c, y, z: (x, c, y + step, z)


def z_by(step):
    return lambda x, c, y, z: (x, c, y, z + step)


def other_core(x, c, y, z):
    return (x, 1 - c, y, z)


def head_groups():
    return [
        [index_of(x, c, 2 * high + low, z) for x in range(NX) for low in range(2)]
        for c in range(NC)
        for high in range(2)
        for z in range(NZ)
    ]


def nt(a, b):
    return lax.dot_general(a, b, (((1,), (1,)), ((), ())), preferred_element_type=jnp.float32)


def first_kernel(got_ref, theirs_ref, q_ref, acc_ref, m_ref, keys, values):
    for s in range(8):
        at = pl.ds(s * 64, 64)
        keys[at, :] = got_ref[s, :, 768:896]
        values[at, 0:D] = got_ref[s, :, 896:1024]
        at = pl.ds(512 + s * 64, 64)
        keys[at, :] = theirs_ref[s, :, 0:D]
        values[at, 0:D] = theirs_ref[s, :, D : 2 * D]
    values[:, D:] = jnp.ones((1024, D), jnp.bfloat16)
    q_ref[NR * ROWS :, :] = jnp.zeros((ROWS, D), jnp.bfloat16)
    m_ref[NR * ROWS :, :] = jnp.zeros((ROWS, D), jnp.float32)
    acc_ref[NR * ROWS :, :] = jnp.zeros((ROWS, 2 * D), jnp.float32)
    row = lax.broadcasted_iota(jnp.int32, (RESP * ROWS, RESP * T), 0)
    col = lax.broadcasted_iota(jnp.int32, (RESP * ROWS, RESP * T), 1)
    seen = (row // ROWS == col // T) & (row % T >= col % T)

    @pl.loop(0, 8)
    def _(s):
        base = pl.multiple_of(s * (RESP * ROWS), RESP * ROWS)
        q = jnp.concatenate(
            [
                got_ref[s, a * T : (a + 1) * T, g * D : (g + 1) * D]
                for a in range(RESP)
                for g in range(GROUP)
            ],
            axis=0,
        )
        q_ref[pl.ds(base, RESP * ROWS), :] = q
        own = jnp.where(seen, nt(q, got_ref[s, :, 512:640]), -jnp.inf)
        far = nt(q, keys[...])
        top = jnp.maximum(
            jnp.max(far, axis=1, keepdims=True), jnp.max(own, axis=1, keepdims=True)
        )
        m = jnp.broadcast_to(top * COEF, (RESP * ROWS, D))
        p = jnp.concatenate(
            [
                jnp.exp2(far[:, j * D : (j + 1) * D] * COEF - m).astype(jnp.bfloat16)
                for j in range(8)
            ],
            axis=1,
        )
        po = jnp.exp2(own * COEF - m[:, : RESP * T]).astype(jnp.bfloat16)
        vo = jnp.concatenate(
            [got_ref[s, :, 640:768], jnp.ones((RESP * T, D), jnp.bfloat16)], axis=1
        )
        acc = jnp.dot(p, values[...], preferred_element_type=jnp.float32)
        acc = acc + jnp.dot(po, vo, preferred_element_type=jnp.float32)
        m_ref[pl.ds(base, RESP * ROWS), :] = m
        acc_ref[pl.ds(base, RESP * ROWS), :] = acc


def first_call(got, theirs):
    n = SLOTS * ROWS
    return pl.pallas_call(
        first_kernel,
        out_shape=(
            jax.ShapeDtypeStruct((n, D), jnp.bfloat16),
            jax.ShapeDtypeStruct((n, 2 * D), jnp.float32),
            jax.ShapeDtypeStruct((n, D), jnp.float32),
        ),
        in_specs=[pl.BlockSpec(memory_space=pltpu.VMEM)] * 2,
        out_specs=(pl.BlockSpec(memory_space=pltpu.VMEM),) * 3,
        scratch_shapes=[
            pltpu.VMEM((1024, D), jnp.bfloat16),
            pltpu.VMEM((1024, 2 * D), jnp.bfloat16),
        ],
        compiler_params=pltpu.CompilerParams(vmem_limit_bytes=24 * 1024 * 1024),
        cost_estimate=pl.CostEstimate(
            flops=4 * 2048 * 1088 * D, bytes_accessed=6 * 1024 * 1024, transcendentals=2048 * 1088
        ),
        name="prefix_and_own",
    )(got, theirs)


def passage_kernel(counts, last, places_ref, count_ref, list_ref, q_ref, acc_in, m_in, *rest):
    blocks = rest[: 2 * len(counts)]
    if last:
        out_ref, acc, m, values = rest[2 * len(counts) :]
    else:
        acc, m, values = rest[2 * len(counts) :]
    acc[...] = acc_in[...]
    m[...] = m_in[...]
    values[:, D:] = jnp.ones((512, D), jnp.bfloat16)
    first = 0
    for number, count in enumerate(counts):
        mine, theirs = blocks[2 * number], blocks[2 * number + 1]

        @pl.loop(0, count)
        def _(i, mine=mine, theirs=theirs, first=first):
            place = places_ref[first + i]
            values[0:256, 0:D] = mine[i, :, D:]
            values[256:512, 0:D] = theirs[i, :, D:]

            @pl.loop(0, (count_ref[place] + BATCH - 1) // BATCH)
            def _(b):
                at = [
                    pl.ds(pl.multiple_of(list_ref[place, b * BATCH + k] * ROWS, ROWS), ROWS)
                    for k in range(BATCH)
                ]
                q = jnp.concatenate([q_ref[a, :] for a in at], axis=0)
                sc = [nt(q, mine[i, :, 0:D]), nt(q, theirs[i, :, 0:D])]
                top = jnp.maximum(
                    jnp.max(sc[0], axis=1, keepdims=True), jnp.max(sc[1], axis=1, keepdims=True)
                )
                old = jnp.concatenate([m[a, :] for a in at], axis=0)
                new = jnp.maximum(old, top * COEF)
                shrink = jnp.exp2(old - new)
                p = jnp.concatenate(
                    [
                        jnp.exp2(h[:, j * D : (j + 1) * D] * COEF - new).astype(jnp.bfloat16)
                        for h in sc
                        for j in range(2)
                    ],
                    axis=1,
                )
                mixed = jnp.dot(p, values[...], preferred_element_type=jnp.float32)
                for k, a in enumerate(at):
                    part = slice(k * ROWS, (k + 1) * ROWS)
                    m[a, :] = new[part]
                    acc[a, 0:D] = acc[a, 0:D] * shrink[part] + mixed[part, 0:D]
                    acc[a, D:] = acc[a, D:] * shrink[part] + mixed[part, D:]

        first += count
    if last:

        @pl.loop(0, NR)
        def _(r):
            at = pl.ds(pl.multiple_of(r * ROWS, ROWS), ROWS)
            o = (acc[at, 0:D] / acc[at, D:]).astype(jnp.bfloat16)
            for g in range(GROUP):
                out_ref[pl.ds(pl.multiple_of(r * T, T), T), g * D : (g + 1) * D] = o[
                    g * T : (g + 1) * T
                ]


def passage_call(places, counts_of, lists, q, acc, m, pairs, last):
    n = SLOTS * ROWS
    counts = tuple(mine.shape[0] for mine, _ in pairs)
    total = sum(counts)
    state = (jax.ShapeDtypeStruct((n, 2 * D), jnp.float32), jax.ShapeDtypeStruct((n, D), jnp.float32))
    scratch = [pltpu.VMEM((512, 2 * D), jnp.bfloat16)]
    if last:
        out_shape = (jax.ShapeDtypeStruct((NR * T, GROUP * D), jnp.bfloat16),)
        scratch = [pltpu.VMEM((n, 2 * D), jnp.float32), pltpu.VMEM((n, D), jnp.float32)] + scratch
        aliases = {}
    else:
        out_shape = state
        aliases = {4: 0, 5: 1}
    vmem = pl.BlockSpec(memory_space=pltpu.VMEM)
    smem = pl.BlockSpec(memory_space=pltpu.SMEM)
    return pl.pallas_call(
        functools.partial(passage_kernel, counts, last),
        out_shape=out_shape,
        in_specs=[smem] * 3 + [vmem] * (3 + 2 * len(counts)),
        out_specs=(vmem,) * len(out_shape),
        scratch_shapes=scratch,
        input_output_aliases=aliases,
        compiler_params=pltpu.CompilerParams(vmem_limit_bytes=28 * 1024 * 1024),
        cost_estimate=pl.CostEstimate(
            flops=4 * total * 10 * ROWS * 512 * D,
            bytes_accessed=6 * 1024 * 1024,
            transcendentals=total * 10 * ROWS * 512,
        ),
        name="passages",
    )(places, counts_of, lists, q, acc, m, *[a for pair in pairs for a in pair])


def per_device(
    queries,
    own_keys,
    own_values,
    prefix_keys,
    prefix_values,
    passage_keys,
    passage_values,
    retrieval,
    location,
):
    grp, dev = lax.axis_index("grp"), lax.axis_index("dev")
    x, c, y, z = grp // NC, grp % NC, dev // NZ, dev % NZ
    low = y % 2

    def two_heads(cache):
        return lax.dynamic_slice(cache[0], (c * 256, x * 2 * D), (256, 2 * D))

    k2, v2 = two_heads(passage_keys), two_heads(passage_values)
    even = jnp.concatenate([k2[:, :D], v2[:, :D]], axis=1)
    odd = jnp.concatenate([k2[:, D:], v2[:, D:]], axis=1)
    kept = jnp.where(low == 0, even, odd)
    given = jnp.where(low == 0, odd, even)
    column = jnp.stack(
        [kept, send(given, y_by(1)), send(given, y_by(-1)), send(kept, y_by(2))]
    )
    column_ys = [y, y - 1, y + 1, y + 2]

    def by_head(rows, width):
        return rows.reshape(64, KV, width).transpose(1, 0, 2)

    def prefix_part(rows):
        return by_head(lax.dynamic_slice(rows, (low * 64, 0), (64, KV * D)), D)

    ids = jnp.zeros((RESP, T, D), jnp.bfloat16)
    ids = ids.at[:, :, :TOPK].set(retrieval.astype(jnp.bfloat16)[:, None, :])
    parcel = jnp.concatenate(
        [
            by_head(queries, GROUP * D),
            by_head(own_keys, D),
            by_head(own_values, D),
            prefix_part(prefix_keys),
            prefix_part(prefix_values),
            jnp.broadcast_to(ids.reshape(1, 64, D), (KV, 64, D)),
        ],
        axis=2,
    )
    got = lax.all_to_all(parcel, AXES, 0, 0, tiled=True, axis_index_groups=head_groups())
    theirs = send(got[:, :, 768:1024], other_core)

    chosen = got[:, :, 1024 : 1024 + TOPK].reshape(NR, T, TOPK)[:, 0].astype(jnp.int32)
    here = location[None, None, :] == jnp.arange(32)[:, None, None]
    at_place = jnp.sum(jnp.where(here, jnp.arange(32)[None, None, :], 0), axis=2)
    reads = jnp.any(chosen[None] == at_place[:, :, None], axis=2)
    ranks = jnp.sum(
        (reads[:, None, :] & (jnp.arange(NR)[None, :] < jnp.arange(NR)[:, None])[None]), axis=2
    )
    hit = reads[:, None, :] & (ranks[:, None, :] == jnp.arange(NR)[None, :, None])
    lists = jnp.sum(jnp.where(hit, jnp.arange(NR)[None, None, :] - NR, 0), axis=2) + NR
    lists = lists.astype(jnp.int32)
    counts_of = jnp.sum(reads, axis=1).astype(jnp.int32)

    q, acc, m = first_call(got, theirs)

    def places_of(offset, ys):
        return jnp.stack([(yy % NY) * NZ + (z + offset) % NZ for yy in ys]).astype(jnp.int32)

    def passages(chunks, acc, m, last=False):
        places = jnp.concatenate([places_of(offset, ys) for offset, ys, _ in chunks])
        pairs = [(block, send(block, other_core)) for _, _, block in chunks]
        return passage_call(places, counts_of, lists, q, acc, m, pairs, last)

    acc, m = passages([(0, column_ys, column)], acc, m)
    up = down = column
    for step in range(1, 4):
        up, down = send(up, z_by(1)), send(down, z_by(-1))
        acc, m = passages([(-step, column_ys, up), (step, column_ys, down)], acc, m)
    up, down = send(up[:2], z_by(1)), send(down[2:], z_by(-1))
    (out,) = passages([(4, column_ys[:2], up), (4, column_ys[2:], down)], acc, m, True)

    out = out.reshape(KV, 64, GROUP * D)
    home = lax.all_to_all(out, AXES, 0, 0, tiled=True, axis_index_groups=head_groups())
    return home.transpose(1, 0, 2).reshape(RESP, T, HEADS * D)


def solution(mesh):
    placed = (
        P(("grp", "dev"), None, None),
        P(("grp", "dev"), None, None),
        P(("grp", "dev"), None, None),
        P("grp", None),
        P("grp", None),
        P("dev", None, None),
        P("dev", None, None),
        P(("grp", "dev"), None),
        P(),
    )
    return jax.shard_map(
        per_device,
        mesh=mesh,
        in_specs=placed,
        out_specs=P(("grp", "dev"), None, None),
        check_vma=False,
    )
```

time: 559 us -> 137 us (0.25); the launches traced: 552 us -> 137 us
  waiting for transfers between devices: 249 us -> 21 us
  local copies, waits for them, and re-layouts: 102 us -> 7.56 us
  matrix products: 74.6 us -> 0 us
  Pallas kernels: 0 us -> 56.6 us
  other arithmetic: 51.9 us -> 1.94 us
  blocking collectives: 43.3 us -> 12.5 us
  starting transfers between devices: 14.9 us -> 36.9 us
  between operations: 15.3 us -> 0.3 us
    all_gather x3 -> x0, waiting for transfers between devices: 146 us -> none  [the longest x1 95.6 us: per_device(): lax.all_gather(queries, 'dev', axis=0, tiled=True)]
    all_to_all x2 -> x1, waiting for transfers between devices: 102 us -> 0.01 us  [per_device(): lax.all_to_all(parcel, AXES, 0, 0, tiled=True, axis_index_groups=head_gro...]
    dot_general x8 -> x0, matrix products: 74.6 us -> none  [the longest x3 34 us: softmax_part(): jnp.einsum(form, weights.astype(jnp.bfloat16), values, preferred_element_...]
    pallas_call x0 -> x6, Pallas kernels: none -> 56.6 us  [the longest x5 49.1 us: passage_call(): pl.pallas_call(functools.partial(passage_kernel, counts, last), out_shape...]
    all_gather x1 -> x0, blocking collectives: 43.3 us -> none  [per_device(): lax.all_gather(retrieval, 'dev', axis=0, tiled=True)]
    reduce_sum x10 -> x4, other arithmetic: 40.6 us -> 1.45 us  [the longest x1 0.62 us: per_device(): jnp.sum(reads[:, None, :] & (jnp.arange(NR)[None, :] < jnp.arange(NR)[:,...]
    gather x6 -> x0, local copies, waits for them, and re-layouts: 36.1 us -> none  [the longest x4 26.1 us: per_device(): jnp.take_along_axis(seen_queries, seen_source[:, :, None, None], axis=1)]
    ppermute x0 -> x21, starting transfers between devices: none -> 32.8 us  [send(): return lax.ppermute(block, AXES, moves(to))]
  transfers between devices with their start and end apart: 5 -> 22, of which waited for: 4 -> 6; matrix products, arithmetic and copies ran while one was open for 11% -> 5% of each run, Pallas kernels for 0% -> 37%
where the time goes in v1:
time: 137 us
  Pallas kernels  56.6 us (41%)
  starting transfers between devices  36.9 us (27%)
  waiting for transfers between devices  21 us (15%)
  blocking collectives  12.5 us (9%)
  local copies, waits for them, and re-layouts  7.56 us (6%)
  other arithmetic  1.94 us (1%)
    pallas_call x5, Pallas kernels, passage_call(): pl.pallas_call(functools.partial(passage_kernel, counts, last), out_shape...  49.1 us
    ppermute x21, starting transfers between devices, send(): return lax.ppermute(block, AXES, moves(to))  32.8 us
    ppermute x21, waiting for transfers between devices, send(): return lax.ppermute(block, AXES, moves(to))  21 us
    all_to_all x1, blocking collectives, per_device(): lax.all_to_all(out, AXES, 0, 0, tiled=True, axis_index_groups=head_groups())  12.5 us
    pallas_call x1, Pallas kernels, first_call(): pl.pallas_call(first_kernel, out_shape=(jax.ShapeDtypeStruct((n, D), jnp....  7.55 us
    all_to_all x1, starting transfers between devices, per_device(): lax.all_to_all(parcel, AXES, 0, 0, tiled=True, axis_index_groups=head_gro...  4.15 us
    unnamed x23, local copies, waits for them, and re-layouts  4.01 us
  transfers between devices with their start and end apart: 22, of which 6 were waited for; matrix products, arithmetic and copies ran while one was open for 5% of the time, Pallas kernels for 37%

profile of v1, /device:TPU:1, one launch (start us, length us, event | category | flops | bytes accessed | tf_op | source)
XLA Modules:
  0.0 136.9 jit_solution(7673433670661658933)
XLA Ops:
  0.0 1.0 dynamic-slice_bitcast_fusion
  1.2 3.6 %collective-permute-start.2 = (bf16[256,256]{1,0:T(8,128)(2,1)S(1)}, bf16[256,256]{1,0:T(8,128)(2,1)S(1)}, u32[]{:S(2)}, u32[]{:S(2)}) collective-permute-start(bf16[256,256]{1,0:T(8,128)(2,1)S(1)} %get-tuple-element.39), channel_id=1, source_target_pairs={{0,24},{1,25},{2,26},{3,27},{4,28},{5,29},{6,30},{7,31},{8,0},{9,1... | collective-permute-start | bytes 393224 | tf_op jit(solution)/shard_map/ppermute | solution.py:39
  4.9 1.6 %collective-permute-start.3 = (bf16[256,256]{1,0:T(8,128)(2,1)S(1)}, bf16[256,256]{1,0:T(8,128)(2,1)S(1)}, u32[]{:S(2)}, u32[]{:S(2)}) collective-permute-start(bf16[256,256]{1,0:T(8,128)(2,1)S(1)} %get-tuple-element.40), channel_id=1, source_target_pairs={{0,16},{1,17},{2,18},{3,19},{4,20},{5,21},{6,22},{7,23},{8,24},{9,... | collective-permute-start | bytes 393224 | tf_op jit(solution)/shard_map/ppermute | solution.py:39
  6.7 1.0 bitcast_dynamic-update-slice_fusion
  7.8 0.7 bitcast_dynamic-update-slice_fusion.2
  8.5 0.7 bitcast_dynamic-update-slice_fusion.1
  10.6 1.0 collective-permute-done.3
  11.6 1.9 %collective-permute-done.1 = bf16[256,256]{1,0:T(8,128)(2,1)S(1)} collective-permute-done((bf16[256,256]{1,0:T(8,128)(2,1)S(1)}, bf16[256,256]{1,0:T(8,128)(2,1)S(1)}, u32[]{:S(2)}, u32[]{:S(2)}) %collective-permute-start.1) | collective-permute-done | bytes 131104 | tf_op jit(solution)/shard_map/ppermute | solution.py:39
  13.6 1.7 %collective-permute-start.5 = (bf16[4,256,256]{2,1,0:T(8,128)(2,1)S(1)}, bf16[4,256,256]{2,1,0:T(8,128)(2,1)S(1)}, u32[]{:S(2)}, u32[]{:S(2)}) collective-permute-start(bf16[4,256,256]{2,1,0:T(8,128)(2,1)S(1)} %pad_maximum_fusion.rest_0_), channel_id=1, source_target_pairs={{0,1},{1,2},{2,3},{3,4},{4,5},{5,6},{6,7},{7,0},{8,9},{9,10},{10,1... | collective-permute-start | bytes 1572872 | tf_op jit(solution)/shard_map/ppermute | solution.py:39
  15.3 4.0 %collective-permute-start.7 = (bf16[4,256,256]{2,1,0:T(8,128)(2,1)S(1)}, bf16[4,256,256]{2,1,0:T(8,128)(2,1)}, u32[]{:S(2)}, u32[]{:S(2)}) collective-permute-start(bf16[4,256,256]{2,1,0:T(8,128)(2,1)S(1)} %pad_maximum_fusion.rest_0_), channel_id=1, source_target_pairs={{0,7},{1,0},{2,1},{3,2},{4,3},{5,4},{6,5},{7,6},{8,15},{9,8},{10,9... | collective-permute-start | bytes 1572872 | tf_op jit(solution)/shard_map/ppermute | solution.py:39
  19.3 0.7 broadcast_dynamic-update-slice_fusion
  20.0 4.2 %all-to-all-start = ((bf16[8,64,1152]{2,1,0:T(8,128)(2,1)}), bf16[8,64,1152]{2,1,0:T(8,128)(2,1)S(1)}, u32[]{:S(2)}, u32[]{:S(2)}) async-start(bf16[8,64,1152]{2,1,0:T(8,128)(2,1)} %broadcast_dynamic-update-slice_fusion), calls=%async_computation | async-start | bytes 2359296 | tf_op jit(solution)/shard_map/all_to_all | solution.py:281
  24.1 6.0 %collective-permute-done.5.rest_0_ = bf16[4,256,256]{2,1,0:T(8,128)(2,1)S(1)} collective-permute-done((bf16[4,256,256]{2,1,0:T(8,128)(2,1)S(1)}, bf16[4,256,256]{2,1,0:T(8,128)(2,1)S(1)}, u32[]{:S(2)}, u32[]{:S(2)}) %collective-permute-start.5) | collective-permute-done | bytes 524320 | tf_op jit(solution)/shard_map/ppermute | solution.py:39
  30.4 2.7 %collective-permute-start.11 = (bf16[4,256,256]{2,1,0:T(8,128)(2,1)}, bf16[4,256,256]{2,1,0:T(8,128)(2,1)}, u32[]{:S(2)}, u32[]{:S(2)}) collective-permute-start(bf16[4,256,256]{2,1,0:T(8,128)(2,1)} %collective-permute-done.7.rest_2_), channel_id=1, source_target_pairs={{0,7},{1,0},{2,1},{3,2},{4,3},{5,4},{6,5},{7,6},{8,15},{9,8},{10,9... | collective-permute-start | bytes 1572872 | tf_op jit(solution)/shard_map/ppermute | solution.py:39
  33.2 2.6 %collective-permute-start.4 = (bf16[4,256,256]{2,1,0:T(8,128)(2,1)S(1)}, bf16[4,256,256]{2,1,0:T(8,128)(2,1)}, u32[]{:S(2)}, u32[]{:S(2)}) collective-permute-start(bf16[4,256,256]{2,1,0:T(8,128)(2,1)S(1)} %pad_maximum_fusion.rest_0_), channel_id=1, source_target_pairs={{0,32},{1,33},{2,34},{3,35},{4,36},{5,37},{6,38},{7,39},{8,40},{9,... | collective-permute-start | bytes 1572872 | tf_op jit(solution)/shard_map/ppermute | solution.py:39
  36.0 6.9 %collective-permute-done.9.rest_0_ = bf16[4,256,256]{2,1,0:T(8,128)(2,1)} collective-permute-done((bf16[4,256,256]{2,1,0:T(8,128)(2,1)S(1)}, bf16[4,256,256]{2,1,0:T(8,128)(2,1)}, u32[]{:S(2)}, u32[]{:S(2)}) %collective-permute-start.9) | collective-permute-done | bytes 524320 | tf_op jit(solution)/shard_map/ppermute | solution.py:39
  43.0 2.9 %collective-permute-start.6 = (bf16[4,256,256]{2,1,0:T(8,128)(2,1)S(1)}, bf16[4,256,256]{2,1,0:T(8,128)(2,1)}, u32[]{:S(2)}, u32[]{:S(2)}) collective-permute-start(bf16[4,256,256]{2,1,0:T(8,128)(2,1)S(1)} %collective-permute-done.5.rest_0_), channel_id=1, source_target_pairs={{0,32},{1,33},{2,34},{3,35},{4,36},{5,37},{6,38},{7,39},{8,40},{9,... | collective-permute-start | bytes 1572872 | tf_op jit(solution)/shard_map/ppermute | solution.py:39
  46.0 3.0 %collective-permute-start.15 = (bf16[4,256,256]{2,1,0:T(8,128)(2,1)}, bf16[4,256,256]{2,1,0:T(8,128)(2,1)S(1)}, u32[]{:S(2)}, u32[]{:S(2)}) collective-permute-start(bf16[4,256,256]{2,1,0:T(8,128)(2,1)} %collective-permute-done.11.rest_2_), channel_id=1, source_target_pairs={{0,7},{1,0},{2,1},{3,2},{4,3},{5,4},{6,5},{7,6},{8,15},{9,8},{10,9... | collective-permute-start | bytes 1572872 | tf_op jit(solution)/shard_map/ppermute | solution.py:39
  49.1 0.7 collective-permute-start.10
  50.7 4.2 %collective-permute-done.13.rest_0_ = bf16[4,256,256]{2,1,0:T(8,128)(2,1)S(1)} collective-permute-done((bf16[4,256,256]{2,1,0:T(8,128)(2,1)}, bf16[4,256,256]{2,1,0:T(8,128)(2,1)S(1)}, u32[]{:S(2)}, u32[]{:S(2)}) %collective-permute-start.13) | collective-permute-done | bytes 524320 | tf_op jit(solution)/shard_map/ppermute | solution.py:39
  54.9 3.8 %collective-permute-start = (bf16[8,64,256]{2,1,0:T(8,128)(2,1)S(1)}, bf16[8,64,256]{2,1,0:T(8,128)(2,1)S(1)}, u32[]{:S(2)}, u32[]{:S(2)}) collective-permute-start(bf16[8,64,256]{2,1,0:T(8,128)(2,1)S(1)} %slice.59), channel_id=1, source_target_pairs={{0,32},{1,33},{2,34},{3,35},{4,36},{5,37},{6,38},{7,39},{8,40},{9,... | collective-permute-start | bytes 786440 | tf_op jit(solution)/shard_map/ppermute | solution.py:39
  59.3 1.0 collective-permute-done.15.rest_2_
  60.3 1.2 collective-permute-start.12
  61.7 3.4 %collective-permute-start.19 = (bf16[2,256,256]{2,1,0:T(8,128)(2,1)S(1)}, bf16[2,256,256]{2,1,0:T(8,128)(2,1)S(1)}, u32[]{:S(2)}, u32[]{:S(2)}) collective-permute-start(bf16[2,256,256]{2,1,0:T(8,128)(2,1)S(1)} %slice.65), channel_id=1, source_target_pairs={{0,7},{1,0},{2,1},{3,2},{4,3},{5,4},{6,5},{7,6},{8,15},{9,8},{10,9... | collective-permute-start | bytes 786440 | tf_op jit(solution)/shard_map/ppermute | solution.py:39
  65.7 7.5 %prefix_and_own.1 = (bf16[2112,128]{1,0:T(8,128)(2,1)S(1)}, f32[2112,256]{1,0:T(8,128)S(1)}, f32[2112,128]{1,0:T(8,128)S(1)}) custom-call(bf16[8,64,1152]{2,1,0:T(8,128)(2,1)S(1)} %all-to-all-done.got_ref, bf16[8,64,256]{2,1,0:T(8,128)(2,1)S(1)} %collective-permute-done.theirs_ref), custom_call_target="tpu_custom_call" | custom-call | flops 1140850688 | bytes 6291456 | tf_op jit(solution)/shard_map/prefix_and_own/pallas_call | solution.py:120
  73.2 6.1 %passages.5 = (f32[2112,256]{1,0:T(8,128)S(1)}, f32[2112,128]{1,0:T(8,128)S(1)}) custom-call(s32[4]{0:T(128)S(1)} %pad_add_fusion.1.places_ref, s32[32]{0:T(128)S(1)} %convert_reduce_fusion.1.count_ref, s32[32,32]{1,0:T(8,128)S(1)} %broadcast_add_fusion.list_ref, ...), custom_call_target="tpu_custom_call", output_to_operand_aliasing={{0}: (4, {}), {1}: (5, {})} | custom-call | flops 671088640 | bytes 6291456 | tf_op jit(solution)/shard_map/passages/pallas_call | solution.py:217
  80.0 13.3 %passages.6 = (f32[2112,256]{1,0:T(8,128)S(1)}, f32[2112,128]{1,0:T(8,128)S(1)}) custom-call(s32[8]{0:T(128)S(1)} %concatenate.53.places_ref, s32[32]{0:T(128)S(1)} %convert_reduce_fusion.1.count_ref, s32[32,32]{1,0:T(8,128)S(1)} %broadcast_add_fusion.list_ref, ...), custom_call_target="tpu_custom_call", output_to_operand_aliasing={{0}: (4, {}), {1}: (5, {})} | custom-call | flops 1342177280 | bytes 6291456 | tf_op jit(solution)/shard_map/passages/pallas_call | solution.py:217
  93.2 12.0 %passages.7 = (f32[2112,256]{1,0:T(8,128)S(1)}, f32[2112,128]{1,0:T(8,128)S(1)}) custom-call(s32[8]{0:T(128)S(1)} %concatenate.52.places_ref, s32[32]{0:T(128)S(1)} %convert_reduce_fusion.1.count_ref, s32[32,32]{1,0:T(8,128)S(1)} %broadcast_add_fusion.list_ref, ...), custom_call_target="tpu_custom_call", output_to_operand_aliasing={{0}: (4, {}), {1}: (5, {})} | custom-call | flops 1342177280 | bytes 6291456 | tf_op jit(solution)/shard_map/passages/pallas_call | solution.py:217
  105.3 11.6 %passages.8 = (f32[2112,256]{1,0:T(8,128)S(1)}, f32[2112,128]{1,0:T(8,128)S(1)}) custom-call(s32[8]{0:T(128)S(1)} %concatenate.51.places_ref, s32[32]{0:T(128)S(1)} %convert_reduce_fusion.1.count_ref, s32[32,32]{1,0:T(8,128)S(1)} %broadcast_add_fusion.list_ref, ...), custom_call_target="tpu_custom_call", output_to_operand_aliasing={{0}: (4, {}), {1}: (5, {})} | custom-call | flops 1342177280 | bytes 6291456 | tf_op jit(solution)/shard_map/passages/pallas_call | solution.py:217
  116.9 6.1 %passages.9 = bf16[512,512]{1,0:T(8,128)(2,1)S(1)} custom-call(s32[4]{0:T(128)S(1)} %pad_add_fusion.places_ref, s32[32]{0:T(128)S(1)} %convert_reduce_fusion.1.count_ref, s32[32,32]{1,0:T(8,128)S(1)} %broadcast_add_fusion.list_ref, bf16[2112,128]{1,0:T(8,128)(2,1)S(1)} %get-tuple-element.28.q_ref, f32[2112,256]{1,0:T(8,128)S(1)} %get-tuple-element.37.acc_in, ...), custom_call_target="tpu_custom_call" | custom-call | flops 671088640 | bytes 6291456 | tf_op jit(solution)/shard_map/passages/pallas_call | solution.py:217
  123.0 12.5 %all_to_all.10 = bf16[8,64,512]{2,1,0:T(8,128)(2,1)S(1)} all-to-all(bf16[8,64,512]{2,1,0:T(8,128)(2,1)S(1)} %bitcast.87), channel_id=1, replica_groups={{0,8,64,72,128,136,192,200},{1,9,65,73,129,137,193,201},{2,10,66,74,130..., dimensions={0} | all-to-all | bytes 1048576 | tf_op jit(solution)/shard_map/all_to_all | solution.py:315
  135.8 1.0 reshape.192
  (73 shorter events, 5.7 us)
Async XLA Ops:
  0.0 6.5 %copy-start = (bf16[4,16,4096]{2,1,0:T(8,128)(2,1)S(1)}, bf16[4,16,4096]{2,1,0:T(8,128)(2,1)}, u32[]{:S(2)}) copy-start(bf16[4,16,4096]{2,1,0:T(8,128)(2,1)} %param.11) | copy-start | bytes 1572868
  1.2 6.5 %copy-start.1 = (bf16[4,16,1024]{2,1,0:T(8,128)(2,1)S(1)}, bf16[4,16,1024]{2,1,0:T(8,128)(2,1)}, u32[]{:S(2)}) copy-start(bf16[4,16,1024]{2,1,0:T(8,128)(2,1)} %param.12) | copy-start | bytes 393220
  1.2 10.4 %collective-permute-start.2 = (bf16[256,256]{1,0:T(8,128)(2,1)S(1)}, bf16[256,256]{1,0:T(8,128)(2,1)S(1)}, u32[]{:S(2)}, u32[]{:S(2)}) collective-permute-start(bf16[256,256]{1,0:T(8,128)(2,1)S(1)} %get-tuple-element.39), channel_id=1, source_target_pairs={{0,24},{1,25},{2,26},{3,27},{4,28},{5,29},{6,30},{7,31},{8,0},{9,1... | collective-permute-start | bytes 393224 | tf_op jit(solution)/shard_map/ppermute | solution.py:39
  4.9 8.6 %collective-permute-start.1 = (bf16[256,256]{1,0:T(8,128)(2,1)S(1)}, bf16[256,256]{1,0:T(8,128)(2,1)S(1)}, u32[]{:S(2)}, u32[]{:S(2)}) collective-permute-start(bf16[256,256]{1,0:T(8,128)(2,1)S(1)} %get-tuple-element.39), channel_id=1, source_target_pairs={{0,8},{1,9},{2,10},{3,11},{4,12},{5,13},{6,14},{7,15},{8,16},{9,17... | collective-permute-start | bytes 393224 | tf_op jit(solution)/shard_map/ppermute | solution.py:39
  4.9 6.7 %collective-permute-start.3 = (bf16[256,256]{1,0:T(8,128)(2,1)S(1)}, bf16[256,256]{1,0:T(8,128)(2,1)S(1)}, u32[]{:S(2)}, u32[]{:S(2)}) collective-permute-start(bf16[256,256]{1,0:T(8,128)(2,1)S(1)} %get-tuple-element.40), channel_id=1, source_target_pairs={{0,16},{1,17},{2,18},{3,19},{4,20},{5,21},{6,22},{7,23},{8,24},{9,... | collective-permute-start | bytes 393224 | tf_op jit(solution)/shard_map/ppermute | solution.py:39
  6.5 1.2 copy-start.2
  6.7 2.5 %copy-start.3 = (bf16[128,1024]{1,0:T(8,128)(2,1)S(1)}, bf16[128,1024]{1,0:T(8,128)(2,1)}, u32[]{:S(2)}) copy-start(bf16[128,1024]{1,0:T(8,128)(2,1)} %param.15) | copy-start | bytes 786436
  6.7 2.5 %copy-start.4 = (bf16[128,1024]{1,0:T(8,128)(2,1)S(1)}, bf16[128,1024]{1,0:T(8,128)(2,1)}, u32[]{:S(2)}) copy-start(bf16[128,1024]{1,0:T(8,128)(2,1)} %param.14) | copy-start | bytes 786436
  7.7 2.9 %copy-start.5 = (s32[4,8]{1,0:T(4,128)S(1)}, s32[4,8]{1,0:T(4,128)}, u32[]{:S(2)}) copy-start(s32[4,8]{1,0:T(4,128)} %param.18) | copy-start | bytes 388
  13.6 16.6 %collective-permute-start.5 = (bf16[4,256,256]{2,1,0:T(8,128)(2,1)S(1)}, bf16[4,256,256]{2,1,0:T(8,128)(2,1)S(1)}, u32[]{:S(2)}, u32[]{:S(2)}) collective-permute-start(bf16[4,256,256]{2,1,0:T(8,128)(2,1)S(1)} %pad_maximum_fusion.rest_0_), channel_id=1, source_target_pairs={{0,1},{1,2},{2,3},{3,4},{4,5},{5,6},{6,7},{7,0},{8,9},{9,10},{10,1... | collective-permute-start | bytes 1572872 | tf_op jit(solution)/shard_map/ppermute | solution.py:39
  15.3 15.1 %collective-permute-start.7 = (bf16[4,256,256]{2,1,0:T(8,128)(2,1)S(1)}, bf16[4,256,256]{2,1,0:T(8,128)(2,1)}, u32[]{:S(2)}, u32[]{:S(2)}) collective-permute-start(bf16[4,256,256]{2,1,0:T(8,128)(2,1)S(1)} %pad_maximum_fusion.rest_0_), channel_id=1, source_target_pairs={{0,7},{1,0},{2,1},{3,2},{4,3},{5,4},{6,5},{7,6},{8,15},{9,8},{10,9... | collective-permute-start | bytes 1572872 | tf_op jit(solution)/shard_map/ppermute | solution.py:39
  20.0 15.9 %copy-start.6 = (s32[32]{0:T(128)S(1)}, s32[32]{0:T(128)}, u32[]{:S(2)}) copy-start(s32[32]{0:T(128)} %param.19) | copy-start | bytes 388
  20.0 26.0 %all-to-all-start = ((bf16[8,64,1152]{2,1,0:T(8,128)(2,1)}), bf16[8,64,1152]{2,1,0:T(8,128)(2,1)S(1)}, u32[]{:S(2)}, u32[]{:S(2)}) async-start(bf16[8,64,1152]{2,1,0:T(8,128)(2,1)} %broadcast_dynamic-update-slice_fusion), calls=%async_computation | async-start | bytes 2359296 | tf_op jit(solution)/shard_map/all_to_all | solution.py:281
  30.1 12.8 %collective-permute-start.9 = (bf16[4,256,256]{2,1,0:T(8,128)(2,1)S(1)}, bf16[4,256,256]{2,1,0:T(8,128)(2,1)}, u32[]{:S(2)}, u32[]{:S(2)}) collective-permute-start(bf16[4,256,256]{2,1,0:T(8,128)(2,1)S(1)} %collective-permute-done.5.rest_0_), channel_id=1, source_target_pairs={{0,1},{1,2},{2,3},{3,4},{4,5},{5,6},{6,7},{7,0},{8,9},{9,10},{10,1... | collective-permute-start | bytes 1572872 | tf_op jit(solution)/shard_map/ppermute | solution.py:39
  30.4 15.6 %collective-permute-start.11 = (bf16[4,256,256]{2,1,0:T(8,128)(2,1)}, bf16[4,256,256]{2,1,0:T(8,128)(2,1)}, u32[]{:S(2)}, u32[]{:S(2)}) collective-permute-start(bf16[4,256,256]{2,1,0:T(8,128)(2,1)} %collective-permute-done.7.rest_2_), channel_id=1, source_target_pairs={{0,7},{1,0},{2,1},{3,2},{4,3},{5,4},{6,5},{7,6},{8,15},{9,8},{10,9... | collective-permute-start | bytes 1572872 | tf_op jit(solution)/shard_map/ppermute | solution.py:39
  33.2 16.0 %collective-permute-start.4 = (bf16[4,256,256]{2,1,0:T(8,128)(2,1)S(1)}, bf16[4,256,256]{2,1,0:T(8,128)(2,1)}, u32[]{:S(2)}, u32[]{:S(2)}) collective-permute-start(bf16[4,256,256]{2,1,0:T(8,128)(2,1)S(1)} %pad_maximum_fusion.rest_0_), channel_id=1, source_target_pairs={{0,32},{1,33},{2,34},{3,35},{4,36},{5,37},{6,38},{7,39},{8,40},{9,... | collective-permute-start | bytes 1572872 | tf_op jit(solution)/shard_map/ppermute | solution.py:39
  42.9 12.0 %collective-permute-start.13 = (bf16[4,256,256]{2,1,0:T(8,128)(2,1)}, bf16[4,256,256]{2,1,0:T(8,128)(2,1)S(1)}, u32[]{:S(2)}, u32[]{:S(2)}) collective-permute-start(bf16[4,256,256]{2,1,0:T(8,128)(2,1)} %collective-permute-done.9.rest_0_), channel_id=1, source_target_pairs={{0,1},{1,2},{2,3},{3,4},{4,5},{5,6},{6,7},{7,0},{8,9},{9,10},{10,1... | collective-permute-start | bytes 1572872 | tf_op jit(solution)/shard_map/ppermute | solution.py:39
  43.0 18.6 %collective-permute-start.6 = (bf16[4,256,256]{2,1,0:T(8,128)(2,1)S(1)}, bf16[4,256,256]{2,1,0:T(8,128)(2,1)}, u32[]{:S(2)}, u32[]{:S(2)}) collective-permute-start(bf16[4,256,256]{2,1,0:T(8,128)(2,1)S(1)} %collective-permute-done.5.rest_0_), channel_id=1, source_target_pairs={{0,32},{1,33},{2,34},{3,35},{4,36},{5,37},{6,38},{7,39},{8,40},{9,... | collective-permute-start | bytes 1572872 | tf_op jit(solution)/shard_map/ppermute | solution.py:39
  45.9 15.8 %collective-permute-start.8 = (bf16[4,256,256]{2,1,0:T(8,128)(2,1)}, bf16[4,256,256]{2,1,0:T(8,128)(2,1)}, u32[]{:S(2)}, u32[]{:S(2)}) collective-permute-start(bf16[4,256,256]{2,1,0:T(8,128)(2,1)} %collective-permute-done.7.rest_2_), channel_id=1, source_target_pairs={{0,32},{1,33},{2,34},{3,35},{4,36},{5,37},{6,38},{7,39},{8,40},{9,... | collective-permute-start | bytes 1572872 | tf_op jit(solution)/shard_map/ppermute | solution.py:39
  46.0 14.2 %collective-permute-start.15 = (bf16[4,256,256]{2,1,0:T(8,128)(2,1)}, bf16[4,256,256]{2,1,0:T(8,128)(2,1)S(1)}, u32[]{:S(2)}, u32[]{:S(2)}) collective-permute-start(bf16[4,256,256]{2,1,0:T(8,128)(2,1)} %collective-permute-done.11.rest_2_), channel_id=1, source_target_pairs={{0,7},{1,0},{2,1},{3,2},{4,3},{5,4},{6,5},{7,6},{8,15},{9,8},{10,9... | collective-permute-start | bytes 1572872 | tf_op jit(solution)/shard_map/ppermute | solution.py:39
  49.1 16.2 %collective-permute-start.10 = (bf16[4,256,256]{2,1,0:T(8,128)(2,1)}, bf16[4,256,256]{2,1,0:T(8,128)(2,1)S(1)}, u32[]{:S(2)}, u32[]{:S(2)}) collective-permute-start(bf16[4,256,256]{2,1,0:T(8,128)(2,1)} %collective-permute-done.9.rest_0_), channel_id=1, source_target_pairs={{0,32},{1,33},{2,34},{3,35},{4,36},{5,37},{6,38},{7,39},{8,40},{9,... | collective-permute-start | bytes 1572872 | tf_op jit(solution)/shard_map/ppermute | solution.py:39
  54.9 10.2 %collective-permute-start = (bf16[8,64,256]{2,1,0:T(8,128)(2,1)S(1)}, bf16[8,64,256]{2,1,0:T(8,128)(2,1)S(1)}, u32[]{:S(2)}, u32[]{:S(2)}) collective-permute-start(bf16[8,64,256]{2,1,0:T(8,128)(2,1)S(1)} %slice.59), channel_id=1, source_target_pairs={{0,32},{1,33},{2,34},{3,35},{4,36},{5,37},{6,38},{7,39},{8,40},{9,... | collective-permute-start | bytes 786440 | tf_op jit(solution)/shard_map/ppermute | solution.py:39
  60.3 33.0 %collective-permute-start.12 = (bf16[4,256,256]{2,1,0:T(8,128)(2,1)}, bf16[4,256,256]{2,1,0:T(8,128)(2,1)S(1)}, u32[]{:S(2)}, u32[]{:S(2)}) collective-permute-start(bf16[4,256,256]{2,1,0:T(8,128)(2,1)} %collective-permute-done.11.rest_2_), channel_id=1, source_target_pairs={{0,32},{1,33},{2,34},{3,35},{4,36},{5,37},{6,38},{7,39},{8,40},{9,... | collective-permute-start | bytes 1572872 | tf_op jit(solution)/shard_map/ppermute | solution.py:39
  61.6 17.8 %collective-permute-start.17 = (bf16[2,256,256]{2,1,0:T(8,128)(2,1)S(1)}, bf16[2,256,256]{2,1,0:T(8,128)(2,1)S(1)}, u32[]{:S(2)}, u32[]{:S(2)}) collective-permute-start(bf16[2,256,256]{2,1,0:T(8,128)(2,1)S(1)} %slice.64), channel_id=1, source_target_pairs={{0,1},{1,2},{2,3},{3,4},{4,5},{5,6},{6,7},{7,0},{8,9},{9,10},{10,1... | collective-permute-start | bytes 786440 | tf_op jit(solution)/shard_map/ppermute | solution.py:39
  61.7 18.1 %collective-permute-start.19 = (bf16[2,256,256]{2,1,0:T(8,128)(2,1)S(1)}, bf16[2,256,256]{2,1,0:T(8,128)(2,1)S(1)}, u32[]{:S(2)}, u32[]{:S(2)}) collective-permute-start(bf16[2,256,256]{2,1,0:T(8,128)(2,1)S(1)} %slice.65), channel_id=1, source_target_pairs={{0,7},{1,0},{2,1},{3,2},{4,3},{5,4},{6,5},{7,6},{8,15},{9,8},{10,9... | collective-permute-start | bytes 786440 | tf_op jit(solution)/shard_map/ppermute | solution.py:39
  65.1 40.2 %collective-permute-start.14 = (bf16[4,256,256]{2,1,0:T(8,128)(2,1)S(1)}, bf16[4,256,256]{2,1,0:T(8,128)(2,1)S(1)}, u32[]{:S(2)}, u32[]{:S(2)}) collective-permute-start(bf16[4,256,256]{2,1,0:T(8,128)(2,1)S(1)} %collective-permute-done.13.rest_0_), channel_id=1, source_target_pairs={{0,32},{1,33},{2,34},{3,35},{4,36},{5,37},{6,38},{7,39},{8,40},{9,... | collective-permute-start | bytes 1572872 | tf_op jit(solution)/shard_map/ppermute | solution.py:39
  65.3 39.9 %collective-permute-start.16 = (bf16[4,256,256]{2,1,0:T(8,128)(2,1)S(1)}, bf16[4,256,256]{2,1,0:T(8,128)(2,1)S(1)}, u32[]{:S(2)}, u32[]{:S(2)}) collective-permute-start(bf16[4,256,256]{2,1,0:T(8,128)(2,1)S(1)} %collective-permute-done.15.rest_2_), channel_id=1, source_target_pairs={{0,32},{1,33},{2,34},{3,35},{4,36},{5,37},{6,38},{7,39},{8,40},{9,... | collective-permute-start | bytes 1572872 | tf_op jit(solution)/shard_map/ppermute | solution.py:39
  79.4 37.5 %collective-permute-start.18 = (bf16[2,256,256]{2,1,0:T(8,128)(2,1)S(1)}, bf16[2,256,256]{2,1,0:T(8,128)(2,1)S(1)}, u32[]{:S(2)}, u32[]{:S(2)}) collective-permute-start(bf16[2,256,256]{2,1,0:T(8,128)(2,1)S(1)} %collective-permute-done.17.rest_0_), channel_id=1, source_target_pairs={{0,32},{1,33},{2,34},{3,35},{4,36},{5,37},{6,38},{7,39},{8,40},{9,... | collective-permute-start | bytes 786440 | tf_op jit(solution)/shard_map/ppermute | solution.py:39
  79.7 37.2 %collective-permute-start.20 = (bf16[2,256,256]{2,1,0:T(8,128)(2,1)S(1)}, bf16[2,256,256]{2,1,0:T(8,128)(2,1)S(1)}, u32[]{:S(2)}, u32[]{:S(2)}) collective-permute-start(bf16[2,256,256]{2,1,0:T(8,128)(2,1)S(1)} %collective-permute-done.19.rest_2_), channel_id=1, source_target_pairs={{0,32},{1,33},{2,34},{3,35},{4,36},{5,37},{6,38},{7,39},{8,40},{9,... | collective-permute-start | bytes 786440 | tf_op jit(solution)/shard_map/ppermute | solution.py:39

commit v2 on v1

v2 whole, which is shorter than its diff:
```python
import functools
import math

import jax
import jax.numpy as jnp
from jax import lax
from jax.experimental import pallas as pl
from jax.experimental.pallas import tpu as pltpu
from jax.sharding import PartitionSpec as P

HEADS = 32
KV = 8
D = 128
TOPK = 8
NX, NC, NY, NZ = 4, 2, 4, 8
AXES = ("grp", "dev")
RESP = 4
T = 16
GROUP = HEADS // KV
ROWS = GROUP * T
NR = 8 * RESP
SLOTS = NR + 1
BATCH = 8
PLACES = 32
COEF = math.log2(math.e) / math.sqrt(D)


def index_of(x, c, y, z):
    return ((x % NX) * NC + c) * (NY * NZ) + (y % NY) * NZ + z % NZ


def moves(to):
    places = [
        (x, c, y, z) for x in range(NX) for c in range(NC) for y in range(NY) for z in range(NZ)
    ]
    return [(index_of(*p), index_of(*to(*p))) for p in places]


def send(block, to):
    return lax.ppermute(block, AXES, moves(to))


def after(block, *earlier):
    return lax.optimization_barrier((block, *earlier))[0]


def y_by(step):
    return lambda x, c, y, z: (x, c, y + step, z)


def z_by(step):
    return lambda x, c, y, z: (x, c, y, z + step)


def other_core(x, c, y, z):
    return (x, 1 - c, y, z)


def head_groups():
    return [
        [index_of(x, c, 2 * high + low, z) for x in range(NX) for low in range(2)]
        for c in range(NC)
        for high in range(2)
        for z in range(NZ)
    ]


def any_turn(i):
    return jnp.where(i < 2, -i, i - 1)


def early_turn(i):
    return -i


def late_turn(i):
    return i + 1


def nt(a, b):
    return lax.dot_general(a, b, (((1,), (1,)), ((), ())), preferred_element_type=jnp.float32)


def parcel_kernel(
    low_ref, q_hbm, ok_hbm, ov_hbm, pk_hbm, pv_hbm, ids_ref, out_ref, q, ok, ov, pk, pv, sems
):
    rows = pl.ds(pl.multiple_of(low_ref[0] * 64, 64), 64)
    pairs = [(ok_hbm, ok), (ov_hbm, ov), (pk_hbm.at[rows, :], pk), (pv_hbm.at[rows, :], pv)]
    copies = [pltpu.make_async_copy(*pair, sems.at[k]) for k, pair in enumerate(pairs + [(q_hbm, q)])]
    for copy in copies:
        copy.start()
    for h in range(KV):
        out_ref[h, :, 1024:1152] = ids_ref[...]
    for k, source in enumerate((ok, ov, pk, pv)):
        copies[k].wait()
        for h in range(KV):
            out_ref[h, :, 512 + k * D : 512 + (k + 1) * D] = source[:, h * D : (h + 1) * D]
    copies[4].wait()
    for h in range(KV):
        out_ref[h, :, 0:512] = q[:, h * 512 : (h + 1) * 512]


def parcel_call(low, queries, own_keys, own_values, prefix_keys, prefix_values, ids):
    anywhere = pl.BlockSpec(memory_space=pl.ANY)
    vmem = pl.BlockSpec(memory_space=pltpu.VMEM)
    return pl.pallas_call(
        parcel_kernel,
        out_shape=jax.ShapeDtypeStruct((KV, 64, 1152), jnp.bfloat16),
        in_specs=[pl.BlockSpec(memory_space=pltpu.SMEM)] + [anywhere] * 5 + [vmem],
        out_specs=vmem,
        scratch_shapes=[pltpu.VMEM((64, HEADS * D), jnp.bfloat16)]
        + [pltpu.VMEM((64, KV * D), jnp.bfloat16)] * 4
        + [pltpu.SemaphoreType.DMA((5,))],
        compiler_params=pltpu.CompilerParams(vmem_limit_bytes=8 * 1024 * 1024),
        cost_estimate=pl.CostEstimate(flops=0, bytes_accessed=6 * 1024 * 1024, transcendentals=0),
        name="parcel",
    )(
        low.reshape(1),
        queries.reshape(64, HEADS * D),
        own_keys.reshape(64, KV * D),
        own_values.reshape(64, KV * D),
        prefix_keys,
        prefix_values,
        ids,
    )


def first_kernel(
    ids_ref, at_ref, got_ref, theirs_ref, q_ref, acc_ref, m_ref, count_ref, list_ref, keys, values
):
    for s in range(8):
        at = pl.ds(s * 64, 64)
        keys[at, :] = got_ref[s, :, 768:896]
        values[at, 0:D] = got_ref[s, :, 896:1024]
        at = pl.ds(512 + s * 64, 64)
        keys[at, :] = theirs_ref[s, :, 0:D]
        values[at, 0:D] = theirs_ref[s, :, D : 2 * D]
    values[:, D:] = jnp.ones((1024, D), jnp.bfloat16)
    q_ref[NR * ROWS :, :] = jnp.zeros((ROWS, D), jnp.bfloat16)
    m_ref[NR * ROWS :, :] = jnp.zeros((ROWS, D), jnp.float32)
    acc_ref[NR * ROWS :, :] = jnp.zeros((ROWS, 2 * D), jnp.float32)
    for p in range(PLACES + 1):
        count_ref[p] = 0
    row = lax.broadcasted_iota(jnp.int32, (RESP * ROWS, RESP * T), 0)
    col = lax.broadcasted_iota(jnp.int32, (RESP * ROWS, RESP * T), 1)
    seen = (row // ROWS == col // T) & (row % T >= col % T)

    @pl.loop(0, 4)
    def _(pair):
        for k in range(8 * TOPK):
            r = pair * 8 + k // TOPK
            place = at_ref[ids_ref[r, k % TOPK]]
            rank = count_ref[place]
            list_ref[place, rank] = r
            count_ref[place] = rank + 1
        two = [pair * 2, pair * 2 + 1]
        q = [
            jnp.concatenate(
                [
                    got_ref[s, a * T : (a + 1) * T, g * D : (g + 1) * D]
                    for a in range(RESP)
                    for g in range(GROUP)
                ],
                axis=0,
            )
            for s in two
        ]
        own = [
            jnp.where(seen, nt(q[i], got_ref[s, :, 512:640]), -jnp.inf) for i, s in enumerate(two)
        ]
        far = [nt(q[i], keys[...]) for i in range(2)]
        m = []
        for i in range(2):
            top = jnp.maximum(
                jnp.max(far[i], axis=1, keepdims=True), jnp.max(own[i], axis=1, keepdims=True)
            )
            m.append(jnp.broadcast_to(top * COEF, (RESP * ROWS, D)))
        for i, s in enumerate(two):
            at = pl.ds(pl.multiple_of(s * (RESP * ROWS), RESP * ROWS), RESP * ROWS)
            p = jnp.concatenate(
                [
                    jnp.exp2(far[i][:, j * D : (j + 1) * D] * COEF - m[i]).astype(jnp.bfloat16)
                    for j in range(8)
                ],
                axis=1,
            )
            po = jnp.exp2(own[i] * COEF - m[i][:, : RESP * T]).astype(jnp.bfloat16)
            vo = jnp.concatenate(
                [got_ref[s, :, 640:768], jnp.ones((RESP * T, D), jnp.bfloat16)], axis=1
            )
            acc = jnp.dot(p, values[...], preferred_element_type=jnp.float32)
            q_ref[at, :] = q[i]
            m_ref[at, :] = m[i]
            acc_ref[at, :] = acc + jnp.dot(po, vo, preferred_element_type=jnp.float32)


def first_call(ids, location, got, theirs):
    n = SLOTS * ROWS
    vmem = pl.BlockSpec(memory_space=pltpu.VMEM)
    smem = pl.BlockSpec(memory_space=pltpu.SMEM)
    return pl.pallas_call(
        first_kernel,
        out_shape=(
            jax.ShapeDtypeStruct((n, D), jnp.bfloat16),
            jax.ShapeDtypeStruct((n, 2 * D), jnp.float32),
            jax.ShapeDtypeStruct((n, D), jnp.float32),
            jax.ShapeDtypeStruct((PLACES + 1,), jnp.int32),
            jax.ShapeDtypeStruct((PLACES + 1, NR), jnp.int32),
        ),
        in_specs=[smem] * 2 + [vmem] * 2,
        out_specs=(vmem,) * 3 + (smem,) * 2,
        scratch_shapes=[
            pltpu.VMEM((1024, D), jnp.bfloat16),
            pltpu.VMEM((1024, 2 * D), jnp.bfloat16),
        ],
        compiler_params=pltpu.CompilerParams(vmem_limit_bytes=16 * 1024 * 1024),
        cost_estimate=pl.CostEstimate(
            flops=8 * 2048 * 1088 * D, bytes_accessed=6 * 1024 * 1024, transcendentals=2048 * 1088
        ),
        name="prefix_and_own",
    )(ids, location, got, theirs)


def passage_kernel(steps, counts, last, spot_ref, count_ref, list_ref, q_ref, acc_in, m_in, *rest):
    blocks = rest[:4]
    if last:
        out_ref, acc, m = rest[4:]
    else:
        acc, m = rest[4:]
    acc[...] = acc_in[...]
    m[...] = m_in[...]
    ones = jnp.ones((256, D), jnp.bfloat16)

    def place_of(s, i):
        turn = steps[s][1](i)
        return ((spot_ref[0] + turn) & (NY - 1)) * NZ + ((spot_ref[1] + steps[s][0]) & (NZ - 1))

    def batches(s):
        total = 0
        for i in range(counts[s]):
            count = count_ref[place_of(s, i)]
            total = total + jnp.maximum((count + BATCH - 1) // BATCH, 1)
        return total

    def step(_, carry):
        at, sc, keep = [], [], []
        ahead = []
        for s, (i, b) in enumerate(carry):
            i_here = jnp.minimum(i, counts[s] - 1)
            place = jnp.where(i < counts[s], place_of(s, i_here), PLACES)
            count = count_ref[place]
            rows = [
                jnp.where(b * BATCH + k < count, list_ref[place, b * BATCH + k], NR)
                for k in range(BATCH)
            ]
            at.append([pl.ds(pl.multiple_of(r * ROWS, ROWS), ROWS) for r in rows])
            full = (b + 1) * BATCH >= count
            ahead.append((i + full.astype(jnp.int32), jnp.where(full, 0, b + 1)))
            q = jnp.concatenate([q_ref[a, :] for a in at[s]], axis=0)
            here = [blocks[2 * s], blocks[2 * s + 1]]
            sc.append([nt(q, h[i_here, :, 0:D]) for h in here])
            keep.append([jnp.concatenate([h[i_here, :, D:], ones], axis=1) for h in here])
        new, shrink = [], []
        for s in range(2):
            top = jnp.maximum(
                jnp.max(sc[s][0], axis=1, keepdims=True), jnp.max(sc[s][1], axis=1, keepdims=True)
            )
            old = jnp.concatenate([m[a, :] for a in at[s]], axis=0)
            new.append(jnp.maximum(old, top * COEF))
            shrink.append(jnp.exp2(old - new[s]))
            for k, a in enumerate(at[s]):
                m[a, :] = new[s][k * ROWS : (k + 1) * ROWS]
        mixed = []
        for s in range(2):
            mixed.append(0)
            for h in range(2):
                p = jnp.concatenate(
                    [
                        jnp.exp2(sc[s][h][:, j * D : (j + 1) * D] * COEF - new[s]).astype(
                            jnp.bfloat16
                        )
                        for j in range(2)
                    ],
                    axis=1,
                )
                mixed[s] = mixed[s] + jnp.dot(p, keep[s][h], preferred_element_type=jnp.float32)
        for s in range(2):
            for k, a in enumerate(at[s]):
                part = slice(k * ROWS, (k + 1) * ROWS)
                acc[a, 0:D] = acc[a, 0:D] * shrink[s][part] + mixed[s][part, 0:D]
                acc[a, D:] = acc[a, D:] * shrink[s][part] + mixed[s][part, D:]
        return tuple(ahead)

    start = ((jnp.int32(0), jnp.int32(0)),) * 2
    lax.fori_loop(0, jnp.maximum(batches(0), batches(1)), step, start)
    if last:

        @pl.loop(0, NR)
        def _(r):
            at = pl.ds(pl.multiple_of(r * ROWS, ROWS), ROWS)
            o = (acc[at, 0:D] / acc[at, D:]).astype(jnp.bfloat16)
            for g in range(GROUP):
                out_ref[pl.ds(pl.multiple_of(r * T, T), T), g * D : (g + 1) * D] = o[
                    g * T : (g + 1) * T
                ]


def passage_call(spot, counts_of, lists, q, acc, m, steps, pairs, last):
    n = SLOTS * ROWS
    counts = tuple(mine.shape[0] for mine, _ in pairs)
    total = sum(counts)
    state = (jax.ShapeDtypeStruct((n, 2 * D), jnp.float32), jax.ShapeDtypeStruct((n, D), jnp.float32))
    scratch = []
    if last:
        out_shape = (jax.ShapeDtypeStruct((NR * T, GROUP * D), jnp.bfloat16),)
        scratch = [pltpu.VMEM((n, 2 * D), jnp.float32), pltpu.VMEM((n, D), jnp.float32)]
        aliases = {}
    else:
        out_shape = state
        aliases = {4: 0, 5: 1}
    vmem = pl.BlockSpec(memory_space=pltpu.VMEM)
    smem = pl.BlockSpec(memory_space=pltpu.SMEM)
    return pl.pallas_call(
        functools.partial(passage_kernel, steps, counts, last),
        out_shape=out_shape,
        in_specs=[smem] * 3 + [vmem] * (3 + 2 * len(counts)),
        out_specs=(vmem,) * len(out_shape),
        scratch_shapes=scratch,
        input_output_aliases=aliases,
        compiler_params=pltpu.CompilerParams(vmem_limit_bytes=20 * 1024 * 1024),
        cost_estimate=pl.CostEstimate(
            flops=16 * total * 10 * ROWS * 512 * D,
            bytes_accessed=6 * 1024 * 1024,
            transcendentals=total * 10 * ROWS * 512,
        ),
        name="passages",
    )(spot, counts_of, lists, q, acc, m, *[a for pair in pairs for a in pair])


def per_device(
    queries,
    own_keys,
    own_values,
    prefix_keys,
    prefix_values,
    passage_keys,
    passage_values,
    retrieval,
    location,
):
    grp, dev = lax.axis_index("grp"), lax.axis_index("dev")
    x, c, y, z = grp >> 1, grp & 1, dev >> 3, dev & 7
    low = y & 1
    spot = jnp.stack([y, z])

    def two_heads(cache):
        return lax.dynamic_slice(cache[0], (c * 256, x * 2 * D), (256, 2 * D))

    k2, v2 = two_heads(passage_keys), two_heads(passage_values)
    even = jnp.concatenate([k2[:, :D], v2[:, :D]], axis=1)
    odd = jnp.concatenate([k2[:, D:], v2[:, D:]], axis=1)
    kept = jnp.where(low == 0, even, odd)
    given = jnp.where(low == 0, odd, even)
    column = jnp.stack(
        [kept, send(given, y_by(1)), send(given, y_by(-1)), send(kept, y_by(2))]
    )

    ids = jnp.pad(retrieval.astype(jnp.bfloat16), ((0, 0), (0, D - TOPK)))
    ids = jnp.broadcast_to(ids[:, None, :], (RESP, T, D)).reshape(64, D)
    parcel = parcel_call(after(low, given), queries, own_keys, own_values, prefix_keys, prefix_values, ids)
    got = lax.all_to_all(after(parcel, column), AXES, 0, 0, tiled=True, axis_index_groups=head_groups())
    theirs = send(got[:, :, 768:1024], other_core)
    chosen = got[:, :, 1024 : 1024 + TOPK].reshape(NR, T, TOPK)[:, 0].astype(jnp.int32)
    q, acc, m, counts_of, lists = first_call(chosen, location, got, theirs)

    def passages(chunks, acc, m, last=False):
        steps = tuple((offset, turn) for offset, turn, _ in chunks)
        pairs = [pair for _, _, pair in chunks]
        return passage_call(spot, counts_of, lists, q, acc, m, steps, pairs, last)

    def swap(block):
        return block, send(block, other_core)

    first = [swap(column[:2]), swap(column[2:])]
    up1, down1 = send(column, z_by(1)), send(column, z_by(-1))
    ups, downs = [swap(up1)], [swap(down1)]
    swapped = (first[0][1], first[1][1])
    ups.append(swap(send(after(up1, *swapped), z_by(1))))
    downs.append(swap(send(after(down1, *swapped), z_by(-1))))
    swapped = (ups[0][1], downs[0][1])
    ups.append(swap(send(after(ups[1][0], m, *swapped), z_by(1))))
    acc, m = passages([(0, early_turn, first[0]), (0, late_turn, first[1])], acc, m)
    downs.append(swap(send(after(downs[1][0], m, *swapped), z_by(-1))))
    for k in range(2):
        acc, m = passages([(-k - 1, any_turn, ups[k]), (k + 1, any_turn, downs[k])], acc, m)
    swapped = (ups[1][1], downs[1][1])
    last_up = swap(send(after(ups[2][0], m, *swapped)[:2], z_by(1)))
    last_down = swap(send(after(downs[2][0], m, *swapped)[2:], z_by(-1)))
    acc, m = passages([(-3, any_turn, ups[2]), (3, any_turn, downs[2])], acc, m)
    (out,) = passages([(4, early_turn, last_up), (4, late_turn, last_down)], acc, m, True)

    out = out.reshape(KV, 64, GROUP * D)
    home = lax.all_to_all(out, AXES, 0, 0, tiled=True, axis_index_groups=head_groups())
    return home.transpose(1, 0, 2).reshape(RESP, T, HEADS * D)


def solution(mesh):
    placed = (
        P(("grp", "dev"), None, None),
        P(("grp", "dev"), None, None),
        P(("grp", "dev"), None, None),
        P("grp", None),
        P("grp", None),
        P("dev", None, None),
        P("dev", None, None),
        P(("grp", "dev"), None),
        P(),
    )
    return jax.shard_map(
        per_device,
        mesh=mesh,
        in_specs=placed,
        out_specs=P(("grp", "dev"), None, None),
        check_vma=False,
    )
```

time: 137 us -> 110 us (0.80)
  Pallas kernels: 56.6 us -> 31.2 us
  local copies, waits for them, and re-layouts: 7.56 us -> 3.36 us
  waiting for transfers between devices: 21 us -> 23.1 us
    pallas_call x5 -> x6, Pallas kernels: 49.1 us -> 25.8 us  [the longest x5 23.9 us: passage_call(): pl.pallas_call(functools.partial(passage_kernel, steps, counts, last), ou...]
    unnamed x23 -> x18, local copies, waits for them, and re-layouts: 4.01 us -> 0.76 us
    pallas_call x1, Pallas kernels: 7.55 us -> 5.39 us  [first_call(): pl.pallas_call(first_kernel, out_shape=(jax.ShapeDtypeStruct((n, D), jnp....]
    ppermute x21 -> x22, waiting for transfers between devices: 21 us -> 23.1 us  [send(): return lax.ppermute(block, AXES, moves(to))]
    reduce_sum x4 -> x0, other arithmetic: 1.45 us -> none  [the longest x1 0.62 us: per_device(): jnp.sum(reads[:, None, :] & (jnp.arange(NR)[None, :] < jnp.arange(NR)[:,...]
    ppermute x21 -> x22, starting transfers between devices: 32.8 us -> 33.5 us  [send(): return lax.ppermute(block, AXES, moves(to))]
  transfers between devices with their start and end apart: 22 -> 23, of which waited for: 6 -> 8; matrix products, arithmetic and copies ran while one was open for 5% -> 0% of each run, Pallas kernels for 37% -> 26%
where the time goes in v2:
time: 110 us; the launch traced here: 109 us
  starting transfers between devices  38.2 us (35%)
  Pallas kernels  31.2 us (28%)
  waiting for transfers between devices  23.1 us (21%)
  blocking collectives  11.9 us (11%)
  local copies, waits for them, and re-layouts  3.36 us (3%)
  other arithmetic  1.1 us (1%)
    ppermute x22, starting transfers between devices, send(): return lax.ppermute(block, AXES, moves(to))  33.5 us
    pallas_call x5, Pallas kernels, passage_call(): pl.pallas_call(functools.partial(passage_kernel, steps, counts, last), ou...  23.9 us
    ppermute x22, waiting for transfers between devices, send(): return lax.ppermute(block, AXES, moves(to))  23.1 us
    all_to_all x1, blocking collectives, per_device(): lax.all_to_all(out, AXES, 0, 0, tiled=True, axis_index_groups=head_groups())  11.9 us
    pallas_call x1, Pallas kernels, first_call(): pl.pallas_call(first_kernel, out_shape=(jax.ShapeDtypeStruct((n, D), jnp....  5.39 us
    all_to_all x1, starting transfers between devices, per_device(): lax.all_to_all(after(parcel, column), AXES, 0, 0, tiled=True, axis_index_...  4.7 us
  transfers between devices with their start and end apart: 23, of which 8 were waited for; matrix products, arithmetic and copies ran while one was open for 0% of the time, Pallas kernels for 26%

profile of v2, /device:TPU:1, one launch (start us, length us, event | category | flops | bytes accessed | tf_op | source)
XLA Modules:
  0.0 109.2 jit_solution(12478876210780245680)
XLA Ops:
  0.0 1.1 dynamic-slice_bitcast_fusion
  1.3 2.2 %collective-permute-start = (bf16[256,256]{1,0:T(8,128)(2,1)S(1)}, bf16[256,256]{1,0:T(8,128)(2,1)S(1)}, u32[]{:S(2)}, u32[]{:S(2)}) collective-permute-start(bf16[256,256]{1,0:T(8,128)(2,1)S(1)} %get-tuple-element.48), channel_id=1, source_target_pairs={{0,8},{1,9},{2,10},{3,11},{4,12},{5,13},{6,14},{7,15},{8,16},{9,17... | collective-permute-start | bytes 393224 | tf_op jit(solution)/shard_map/ppermute | solution.py:40
  3.5 1.5 %collective-permute-start.1 = (bf16[256,256]{1,0:T(8,128)(2,1)S(1)}, bf16[256,256]{1,0:T(8,128)(2,1)S(1)}, u32[]{:S(2)}, u32[]{:S(2)}) collective-permute-start(bf16[256,256]{1,0:T(8,128)(2,1)S(1)} %get-tuple-element.48), channel_id=1, source_target_pairs={{0,24},{1,25},{2,26},{3,27},{4,28},{5,29},{6,30},{7,31},{8,0},{9,1... | collective-permute-start | bytes 393224 | tf_op jit(solution)/shard_map/ppermute | solution.py:40
  5.0 1.6 %collective-permute-start.2 = (bf16[256,256]{1,0:T(8,128)(2,1)S(1)}, bf16[256,256]{1,0:T(8,128)(2,1)S(1)}, u32[]{:S(2)}, u32[]{:S(2)}) collective-permute-start(bf16[256,256]{1,0:T(8,128)(2,1)S(1)} %get-tuple-element.47), channel_id=1, source_target_pairs={{0,16},{1,17},{2,18},{3,19},{4,20},{5,21},{6,22},{7,23},{8,24},{9,... | collective-permute-start | bytes 393224 | tf_op jit(solution)/shard_map/ppermute | solution.py:40
  6.7 1.9 %parcel.1 = bf16[8,64,1152]{2,1,0:T(8,128)(2,1)} custom-call(s32[1]{0:T(128)} %bitcast.4.low_ref, bf16[64,4096]{1,0:T(8,128)(2,1)S(1)} %bitcast.31, bf16[64,1024]{1,0:T(8,128)(2,1)S(1)} %bitcast.32, bf16[64,1024]{1,0:T(8,128)(2,1)S(1)} %bitcast.33, bf16[128,1024]{1,0:T(8,128)(2,1)S(1)} %copy-done.1, bf16[128,1024]{1,0:T(8,128)(2,1)S(1)} %copy-done.2, ...), custom_call_target="tpu_custom_call" | custom-call | bytes 6291456 | tf_op jit(solution)/shard_map/parcel/pallas_call | solution.py:106
  8.7 2.6 %collective-permute-done.2 = bf16[256,256]{1,0:T(8,128)(2,1)S(1)} collective-permute-done((bf16[256,256]{1,0:T(8,128)(2,1)S(1)}, bf16[256,256]{1,0:T(8,128)(2,1)S(1)}, u32[]{:S(2)}, u32[]{:S(2)}) %collective-permute-start.2) | collective-permute-done | bytes 131104 | tf_op jit(solution)/shard_map/ppermute | solution.py:40
  11.3 0.9 pad_maximum_fusion
  12.2 4.7 %all-to-all-start = ((bf16[8,64,1152]{2,1,0:T(8,128)(2,1)}), bf16[8,64,1152]{2,1,0:T(8,128)(2,1)S(1)}, u32[]{:S(2)}, u32[]{:S(2)}) async-start(bf16[8,64,1152]{2,1,0:T(8,128)(2,1)} %parcel.1), calls=%async_computation | async-start | bytes 2359296 | tf_op jit(solution)/shard_map/all_to_all | solution.py:371
  16.9 1.7 %collective-permute-start.6 = (bf16[4,256,256]{2,1,0:T(8,128)(2,1)}, bf16[4,256,256]{2,1,0:T(8,128)(2,1)S(1)}, u32[]{:S(2)}, u32[]{:S(2)}) collective-permute-start(bf16[4,256,256]{2,1,0:T(8,128)(2,1)} %pad_maximum_fusion), channel_id=1, source_target_pairs={{0,1},{1,2},{2,3},{3,4},{4,5},{5,6},{6,7},{7,0},{8,9},{9,10},{10,1... | collective-permute-start | bytes 1572872 | tf_op jit(solution)/shard_map/ppermute | solution.py:40
  18.6 4.0 %collective-permute-start.8 = (bf16[4,256,256]{2,1,0:T(8,128)(2,1)}, bf16[4,256,256]{2,1,0:T(8,128)(2,1)S(1)}, u32[]{:S(2)}, u32[]{:S(2)}) collective-permute-start(bf16[4,256,256]{2,1,0:T(8,128)(2,1)} %pad_maximum_fusion), channel_id=1, source_target_pairs={{0,7},{1,0},{2,1},{3,2},{4,3},{5,4},{6,5},{7,6},{8,15},{9,8},{10,9... | collective-permute-start | bytes 1572872 | tf_op jit(solution)/shard_map/ppermute | solution.py:40
  22.7 2.6 %collective-permute-start.4 = (bf16[2,256,256]{2,1,0:T(8,128)(2,1)S(1)}, bf16[2,256,256]{2,1,0:T(8,128)(2,1)S(1)}, u32[]{:S(2)}, u32[]{:S(2)}) collective-permute-start(bf16[2,256,256]{2,1,0:T(8,128)(2,1)S(1)} %pad_maximum_fusion.1.rest_0_), channel_id=1, source_target_pairs={{0,32},{1,33},{2,34},{3,35},{4,36},{5,37},{6,38},{7,39},{8,40},{9,... | collective-permute-start | bytes 786440 | tf_op jit(solution)/shard_map/ppermute | solution.py:40
  25.4 1.1 collective-permute-done.4.rest_1_
  27.6 5.2 %collective-permute-done.6.rest_0_ = bf16[4,256,256]{2,1,0:T(8,128)(2,1)S(1)} collective-permute-done((bf16[4,256,256]{2,1,0:T(8,128)(2,1)}, bf16[4,256,256]{2,1,0:T(8,128)(2,1)S(1)}, u32[]{:S(2)}, u32[]{:S(2)}) %collective-permute-start.6) | collective-permute-done | bytes 524320 | tf_op jit(solution)/shard_map/ppermute | solution.py:40
  32.8 2.9 %collective-permute-start.7 = (bf16[4,256,256]{2,1,0:T(8,128)(2,1)S(1)}, bf16[4,256,256]{2,1,0:T(8,128)(2,1)}, u32[]{:S(2)}, u32[]{:S(2)}) collective-permute-start(bf16[4,256,256]{2,1,0:T(8,128)(2,1)S(1)} %collective-permute-done.6.rest_0_), channel_id=1, source_target_pairs={{0,32},{1,33},{2,34},{3,35},{4,36},{5,37},{6,38},{7,39},{8,40},{9,... | collective-permute-start | bytes 1572872 | tf_op jit(solution)/shard_map/ppermute | solution.py:40
  36.4 4.4 %collective-permute-start.12 = (bf16[4,256,256]{2,1,0:T(8,128)(2,1)S(1)}, bf16[4,256,256]{2,1,0:T(8,128)(2,1)S(1)}, u32[]{:S(2)}, u32[]{:S(2)}) collective-permute-start(bf16[4,256,256]{2,1,0:T(8,128)(2,1)S(1)} %collective-permute-done.8.rest_2_), channel_id=1, source_target_pairs={{0,7},{1,0},{2,1},{3,2},{4,3},{5,4},{6,5},{7,6},{8,15},{9,8},{10,9... | collective-permute-start | bytes 1572872 | tf_op jit(solution)/shard_map/ppermute | solution.py:40
  40.9 5.4 %prefix_and_own.1 = (bf16[2112,128]{1,0:T(8,128)(2,1)S(1)}, f32[2112,256]{1,0:T(8,128)S(1)}, f32[2112,128]{1,0:T(8,128)S(1)}, s32[33]{0:T(128)S(1)}, s32[33,32]{1,0:T(8,128)S(1)}) custom-call(s32[32,8]{1,0:T(8,128)S(1)} %fusion.ids_ref, s32[32]{0:T(128)S(1)} %copy-done.7, bf16[8,64,1152]{2,1,0:T(8,128)(2,1)S(1)} %all-to-all-done.got_ref, ...), custom_call_target="tpu_custom_call" | custom-call | flops 2281701376 | bytes 6291456 | tf_op jit(solution)/shard_map/prefix_and_own/pallas_call | solution.py:201
  46.3 3.9 %passages.5 = (f32[2112,256]{1,0:T(8,128)S(1)}, f32[2112,128]{1,0:T(8,128)S(1)}) custom-call(s32[2]{0:T(128)S(1)} %pad_add_fusion.spot_ref, s32[33]{0:T(128)S(1)} %get-tuple-element.28.count_ref, s32[33,32]{1,0:T(8,128)S(1)} %get-tuple-element.29.list_ref, ...), custom_call_target="tpu_custom_call", output_to_operand_aliasing={{0}: (4, {}), {1}: (5, {})} | custom-call | flops 2684354560 | bytes 6291456 | tf_op jit(solution)/shard_map/passages/pallas_call | solution.py:323
  50.3 1.8 %collective-permute-done.12.rest_2_ = bf16[4,256,256]{2,1,0:T(8,128)(2,1)S(1)} collective-permute-done((bf16[4,256,256]{2,1,0:T(8,128)(2,1)S(1)}, bf16[4,256,256]{2,1,0:T(8,128)(2,1)S(1)}, u32[]{:S(2)}, u32[]{:S(2)}) %collective-permute-start.12) | collective-permute-done | bytes 524320 | tf_op jit(solution)/shard_map/ppermute | solution.py:40
  52.1 3.4 %collective-permute-start.16 = (bf16[4,256,256]{2,1,0:T(8,128)(2,1)S(1)}, bf16[4,256,256]{2,1,0:T(8,128)(2,1)S(1)}, u32[]{:S(2)}, u32[]{:S(2)}) collective-permute-start(bf16[4,256,256]{2,1,0:T(8,128)(2,1)S(1)} %collective-permute-done.12.rest_2_), channel_id=1, source_target_pairs={{0,7},{1,0},{2,1},{3,2},{4,3},{5,4},{6,5},{7,6},{8,15},{9,8},{10,9... | collective-permute-start | bytes 1572872 | tf_op jit(solution)/shard_map/ppermute | solution.py:40
  55.5 1.1 collective-permute-start.13
  56.6 5.2 %passages.6 = (f32[2112,256]{1,0:T(8,128)S(1)}, f32[2112,128]{1,0:T(8,128)S(1)}) custom-call(s32[2]{0:T(128)S(1)} %pad_add_fusion.spot_ref, s32[33]{0:T(128)S(1)} %get-tuple-element.28.count_ref, s32[33,32]{1,0:T(8,128)S(1)} %get-tuple-element.29.list_ref, ...), custom_call_target="tpu_custom_call", output_to_operand_aliasing={{0}: (4, {}), {1}: (5, {})} | custom-call | flops 5368709120 | bytes 6291456 | tf_op jit(solution)/shard_map/passages/pallas_call | solution.py:323
  61.8 4.2 %collective-permute-done.16.rest_2_ = bf16[4,256,256]{2,1,0:T(8,128)(2,1)S(1)} collective-permute-done((bf16[4,256,256]{2,1,0:T(8,128)(2,1)S(1)}, bf16[4,256,256]{2,1,0:T(8,128)(2,1)S(1)}, u32[]{:S(2)}, u32[]{:S(2)}) %collective-permute-start.16) | collective-permute-done | bytes 524320 | tf_op jit(solution)/shard_map/ppermute | solution.py:40
  66.0 1.7 %collective-permute-start.17 = (bf16[4,256,256]{2,1,0:T(8,128)(2,1)S(1)}, bf16[4,256,256]{2,1,0:T(8,128)(2,1)S(1)}, u32[]{:S(2)}, u32[]{:S(2)}) collective-permute-start(bf16[4,256,256]{2,1,0:T(8,128)(2,1)S(1)} %collective-permute-done.16.rest_2_), channel_id=1, source_target_pairs={{0,32},{1,33},{2,34},{3,35},{4,36},{5,37},{6,38},{7,39},{8,40},{9,... | collective-permute-start | bytes 1572872 | tf_op jit(solution)/shard_map/ppermute | solution.py:40
  67.7 1.4 %collective-permute-done.14.rest_0_ = bf16[4,256,256]{2,1,0:T(8,128)(2,1)S(1)} collective-permute-done((bf16[4,256,256]{2,1,0:T(8,128)(2,1)S(1)}, bf16[4,256,256]{2,1,0:T(8,128)(2,1)S(1)}, u32[]{:S(2)}, u32[]{:S(2)}) %collective-permute-start.14) | collective-permute-done | bytes 524320 | tf_op jit(solution)/shard_map/ppermute | solution.py:40
  69.1 2.0 %collective-permute-start.15 = (bf16[4,256,256]{2,1,0:T(8,128)(2,1)S(1)}, bf16[4,256,256]{2,1,0:T(8,128)(2,1)S(1)}, u32[]{:S(2)}, u32[]{:S(2)}) collective-permute-start(bf16[4,256,256]{2,1,0:T(8,128)(2,1)S(1)} %collective-permute-done.14.rest_0_), channel_id=1, source_target_pairs={{0,32},{1,33},{2,34},{3,35},{4,36},{5,37},{6,38},{7,39},{8,40},{9,... | collective-permute-start | bytes 1572872 | tf_op jit(solution)/shard_map/ppermute | solution.py:40
  71.1 5.7 %passages.7 = (f32[2112,256]{1,0:T(8,128)S(1)}, f32[2112,128]{1,0:T(8,128)S(1)}) custom-call(s32[2]{0:T(128)S(1)} %pad_add_fusion.spot_ref, s32[33]{0:T(128)S(1)} %get-tuple-element.28.count_ref, s32[33,32]{1,0:T(8,128)S(1)} %get-tuple-element.29.list_ref, ...), custom_call_target="tpu_custom_call", output_to_operand_aliasing={{0}: (4, {}), {1}: (5, {})} | custom-call | flops 5368709120 | bytes 6291456 | tf_op jit(solution)/shard_map/passages/pallas_call | solution.py:323
  77.0 2.7 %collective-permute-start.20 = (bf16[2,256,256]{2,1,0:T(8,128)(2,1)S(1)}, bf16[2,256,256]{2,1,0:T(8,128)(2,1)S(1)}, u32[]{:S(2)}, u32[]{:S(2)}) collective-permute-start(bf16[2,256,256]{2,1,0:T(8,128)(2,1)S(1)} %slice.39), channel_id=1, source_target_pairs={{0,7},{1,0},{2,1},{3,2},{4,3},{5,4},{6,5},{7,6},{8,15},{9,8},{10,9... | collective-permute-start | bytes 786440 | tf_op jit(solution)/shard_map/ppermute | solution.py:40
  79.7 6.4 %collective-permute-done.18.rest_0_ = bf16[2,256,256]{2,1,0:T(8,128)(2,1)S(1)} collective-permute-done((bf16[2,256,256]{2,1,0:T(8,128)(2,1)S(1)}, bf16[2,256,256]{2,1,0:T(8,128)(2,1)S(1)}, u32[]{:S(2)}, u32[]{:S(2)}) %collective-permute-start.18) | collective-permute-done | bytes 262176 | tf_op jit(solution)/shard_map/ppermute | solution.py:40
  86.9 5.7 %passages.8 = (f32[2112,256]{1,0:T(8,128)S(1)}, f32[2112,128]{1,0:T(8,128)S(1)}) custom-call(s32[2]{0:T(128)S(1)} %pad_add_fusion.spot_ref, s32[33]{0:T(128)S(1)} %get-tuple-element.28.count_ref, s32[33,32]{1,0:T(8,128)S(1)} %get-tuple-element.29.list_ref, ...), custom_call_target="tpu_custom_call", output_to_operand_aliasing={{0}: (4, {}), {1}: (5, {})} | custom-call | flops 5368709120 | bytes 6291456 | tf_op jit(solution)/shard_map/passages/pallas_call | solution.py:323
  92.6 3.3 %passages.9 = bf16[512,512]{1,0:T(8,128)(2,1)S(1)} custom-call(s32[2]{0:T(128)S(1)} %pad_add_fusion.spot_ref, s32[33]{0:T(128)S(1)} %get-tuple-element.28.count_ref, s32[33,32]{1,0:T(8,128)S(1)} %get-tuple-element.29.list_ref, bf16[2112,128]{1,0:T(8,128)(2,1)S(1)} %get-tuple-element.30.q_ref, f32[2112,256]{1,0:T(8,128)S(1)} %get-tuple-element.43.acc_in, ...), custom_call_target="tpu_custom_call" | custom-call | flops 2684354560 | bytes 6291456 | tf_op jit(solution)/shard_map/passages/pallas_call | solution.py:323
  95.9 11.9 %all_to_all.10 = bf16[8,64,512]{2,1,0:T(8,128)(2,1)S(1)} all-to-all(bf16[8,64,512]{2,1,0:T(8,128)(2,1)S(1)} %bitcast.30), channel_id=1, replica_groups={{0,8,64,72,128,136,192,200},{1,9,65,73,129,137,193,201},{2,10,66,74,130..., dimensions={0} | all-to-all | bytes 1048576 | tf_op jit(solution)/shard_map/all_to_all | solution.py:403
  108.2 1.0 reshape.91
  (60 shorter events, 3.5 us)
Async XLA Ops:
  0.0 6.6 %copy-start.8 = (s32[4,8]{1,0:T(4,128)S(1)}, s32[4,8]{1,0:T(4,128)}, u32[]{:S(2)}) copy-start(s32[4,8]{1,0:T(4,128)} %param.16) | copy-start | bytes 388
  0.0 6.6 %copy-start = (bf16[4,16,4096]{2,1,0:T(8,128)(2,1)S(1)}, bf16[4,16,4096]{2,1,0:T(8,128)(2,1)}, u32[]{:S(2)}) copy-start(bf16[4,16,4096]{2,1,0:T(8,128)(2,1)} %param.9) | copy-start | bytes 1572868
  0.0 6.6 %copy-start.3 = (bf16[4,16,1024]{2,1,0:T(8,128)(2,1)S(1)}, bf16[4,16,1024]{2,1,0:T(8,128)(2,1)}, u32[]{:S(2)}) copy-start(bf16[4,16,1024]{2,1,0:T(8,128)(2,1)} %param.10) | copy-start | bytes 393220
  0.0 6.6 %copy-start.4 = (bf16[4,16,1024]{2,1,0:T(8,128)(2,1)S(1)}, bf16[4,16,1024]{2,1,0:T(8,128)(2,1)}, u32[]{:S(2)}) copy-start(bf16[4,16,1024]{2,1,0:T(8,128)(2,1)} %param.11) | copy-start | bytes 393220
  0.0 6.6 %copy-start.1 = (bf16[128,1024]{1,0:T(8,128)(2,1)S(1)}, bf16[128,1024]{1,0:T(8,128)(2,1)}, u32[]{:S(2)}) copy-start(bf16[128,1024]{1,0:T(8,128)(2,1)} %pk_hbm.1) | copy-start | bytes 786436
  0.0 6.6 %copy-start.2 = (bf16[128,1024]{1,0:T(8,128)(2,1)S(1)}, bf16[128,1024]{1,0:T(8,128)(2,1)}, u32[]{:S(2)}) copy-start(bf16[128,1024]{1,0:T(8,128)(2,1)} %pv_hbm.1) | copy-start | bytes 786436
  1.3 7.4 %collective-permute-start = (bf16[256,256]{1,0:T(8,128)(2,1)S(1)}, bf16[256,256]{1,0:T(8,128)(2,1)S(1)}, u32[]{:S(2)}, u32[]{:S(2)}) collective-permute-start(bf16[256,256]{1,0:T(8,128)(2,1)S(1)} %get-tuple-element.48), channel_id=1, source_target_pairs={{0,8},{1,9},{2,10},{3,11},{4,12},{5,13},{6,14},{7,15},{8,16},{9,17... | collective-permute-start | bytes 393224 | tf_op jit(solution)/shard_map/ppermute | solution.py:40
  3.5 5.2 %collective-permute-start.1 = (bf16[256,256]{1,0:T(8,128)(2,1)S(1)}, bf16[256,256]{1,0:T(8,128)(2,1)S(1)}, u32[]{:S(2)}, u32[]{:S(2)}) collective-permute-start(bf16[256,256]{1,0:T(8,128)(2,1)S(1)} %get-tuple-element.48), channel_id=1, source_target_pairs={{0,24},{1,25},{2,26},{3,27},{4,28},{5,29},{6,30},{7,31},{8,0},{9,1... | collective-permute-start | bytes 393224 | tf_op jit(solution)/shard_map/ppermute | solution.py:40
  5.0 6.3 %collective-permute-start.2 = (bf16[256,256]{1,0:T(8,128)(2,1)S(1)}, bf16[256,256]{1,0:T(8,128)(2,1)S(1)}, u32[]{:S(2)}, u32[]{:S(2)}) collective-permute-start(bf16[256,256]{1,0:T(8,128)(2,1)S(1)} %get-tuple-element.47), channel_id=1, source_target_pairs={{0,16},{1,17},{2,18},{3,19},{4,20},{5,21},{6,22},{7,23},{8,24},{9,... | collective-permute-start | bytes 393224 | tf_op jit(solution)/shard_map/ppermute | solution.py:40
  12.2 23.5 %all-to-all-start = ((bf16[8,64,1152]{2,1,0:T(8,128)(2,1)}), bf16[8,64,1152]{2,1,0:T(8,128)(2,1)S(1)}, u32[]{:S(2)}, u32[]{:S(2)}) async-start(bf16[8,64,1152]{2,1,0:T(8,128)(2,1)} %parcel.1), calls=%async_computation | async-start | bytes 2359296 | tf_op jit(solution)/shard_map/all_to_all | solution.py:371
  16.9 24.0 %copy-start.7 = (s32[32]{0:T(128)S(1)}, s32[32]{0:T(128)}, u32[]{:S(2)}) copy-start(s32[32]{0:T(128)} %at_ref.1) | copy-start | bytes 388
  16.9 15.9 %collective-permute-start.6 = (bf16[4,256,256]{2,1,0:T(8,128)(2,1)}, bf16[4,256,256]{2,1,0:T(8,128)(2,1)S(1)}, u32[]{:S(2)}, u32[]{:S(2)}) collective-permute-start(bf16[4,256,256]{2,1,0:T(8,128)(2,1)} %pad_maximum_fusion), channel_id=1, source_target_pairs={{0,1},{1,2},{2,3},{3,4},{4,5},{5,6},{6,7},{7,0},{8,9},{9,10},{10,1... | collective-permute-start | bytes 1572872 | tf_op jit(solution)/shard_map/ppermute | solution.py:40
  18.6 17.0 %collective-permute-start.8 = (bf16[4,256,256]{2,1,0:T(8,128)(2,1)}, bf16[4,256,256]{2,1,0:T(8,128)(2,1)S(1)}, u32[]{:S(2)}, u32[]{:S(2)}) collective-permute-start(bf16[4,256,256]{2,1,0:T(8,128)(2,1)} %pad_maximum_fusion), channel_id=1, source_target_pairs={{0,7},{1,0},{2,1},{3,2},{4,3},{5,4},{6,5},{7,6},{8,15},{9,8},{10,9... | collective-permute-start | bytes 1572872 | tf_op jit(solution)/shard_map/ppermute | solution.py:40
  22.7 3.8 %collective-permute-start.4 = (bf16[2,256,256]{2,1,0:T(8,128)(2,1)S(1)}, bf16[2,256,256]{2,1,0:T(8,128)(2,1)S(1)}, u32[]{:S(2)}, u32[]{:S(2)}) collective-permute-start(bf16[2,256,256]{2,1,0:T(8,128)(2,1)S(1)} %pad_maximum_fusion.1.rest_0_), channel_id=1, source_target_pairs={{0,32},{1,33},{2,34},{3,35},{4,36},{5,37},{6,38},{7,39},{8,40},{9,... | collective-permute-start | bytes 786440 | tf_op jit(solution)/shard_map/ppermute | solution.py:40
  25.3 1.5 %collective-permute-start.5 = (bf16[2,256,256]{2,1,0:T(8,128)(2,1)S(1)}, bf16[2,256,256]{2,1,0:T(8,128)(2,1)S(1)}, u32[]{:S(2)}, u32[]{:S(2)}) collective-permute-start(bf16[2,256,256]{2,1,0:T(8,128)(2,1)S(1)} %pad_maximum_fusion.2.rest_2_), channel_id=1, source_target_pairs={{0,32},{1,33},{2,34},{3,35},{4,36},{5,37},{6,38},{7,39},{8,40},{9,... | collective-permute-start | bytes 786440 | tf_op jit(solution)/shard_map/ppermute | solution.py:40
  26.8 0.7 copy-start.5
  32.8 13.5 %collective-permute-start.10 = (bf16[4,256,256]{2,1,0:T(8,128)(2,1)S(1)}, bf16[4,256,256]{2,1,0:T(8,128)(2,1)S(1)}, u32[]{:S(2)}, u32[]{:S(2)}) collective-permute-start(bf16[4,256,256]{2,1,0:T(8,128)(2,1)S(1)} %collective-permute-done.6.rest_0_), channel_id=1, source_target_pairs={{0,1},{1,2},{2,3},{3,4},{4,5},{5,6},{6,7},{7,0},{8,9},{9,10},{10,1... | collective-permute-start | bytes 1572872 | tf_op jit(solution)/shard_map/ppermute | solution.py:40
  32.8 13.5 %collective-permute-start.7 = (bf16[4,256,256]{2,1,0:T(8,128)(2,1)S(1)}, bf16[4,256,256]{2,1,0:T(8,128)(2,1)}, u32[]{:S(2)}, u32[]{:S(2)}) collective-permute-start(bf16[4,256,256]{2,1,0:T(8,128)(2,1)S(1)} %collective-permute-done.6.rest_0_), channel_id=1, source_target_pairs={{0,32},{1,33},{2,34},{3,35},{4,36},{5,37},{6,38},{7,39},{8,40},{9,... | collective-permute-start | bytes 1572872 | tf_op jit(solution)/shard_map/ppermute | solution.py:40
  35.7 10.6 %collective-permute-start.9 = (bf16[4,256,256]{2,1,0:T(8,128)(2,1)S(1)}, bf16[4,256,256]{2,1,0:T(8,128)(2,1)}, u32[]{:S(2)}, u32[]{:S(2)}) collective-permute-start(bf16[4,256,256]{2,1,0:T(8,128)(2,1)S(1)} %collective-permute-done.8.rest_2_), channel_id=1, source_target_pairs={{0,32},{1,33},{2,34},{3,35},{4,36},{5,37},{6,38},{7,39},{8,40},{9,... | collective-permute-start | bytes 1572872 | tf_op jit(solution)/shard_map/ppermute | solution.py:40
  35.8 5.1 %collective-permute-start.3 = (bf16[8,64,256]{2,1,0:T(8,128)(2,1)S(1)}, bf16[8,64,256]{2,1,0:T(8,128)(2,1)S(1)}, u32[]{:S(2)}, u32[]{:S(2)}) collective-permute-start(bf16[8,64,256]{2,1,0:T(8,128)(2,1)S(1)} %slice.46), channel_id=1, source_target_pairs={{0,32},{1,33},{2,34},{3,35},{4,36},{5,37},{6,38},{7,39},{8,40},{9,... | collective-permute-start | bytes 786440 | tf_op jit(solution)/shard_map/ppermute | solution.py:40
  36.4 15.8 %collective-permute-start.12 = (bf16[4,256,256]{2,1,0:T(8,128)(2,1)S(1)}, bf16[4,256,256]{2,1,0:T(8,128)(2,1)S(1)}, u32[]{:S(2)}, u32[]{:S(2)}) collective-permute-start(bf16[4,256,256]{2,1,0:T(8,128)(2,1)S(1)} %collective-permute-done.8.rest_2_), channel_id=1, source_target_pairs={{0,7},{1,0},{2,1},{3,2},{4,3},{5,4},{6,5},{7,6},{8,15},{9,8},{10,9... | collective-permute-start | bytes 1572872 | tf_op jit(solution)/shard_map/ppermute | solution.py:40
  40.8 5.5 %copy-start.6 = (bf16[2,256,256]{2,1,0:T(8,128)(2,1)S(1)}, bf16[2,256,256]{2,1,0:T(8,128)(2,1)}, u32[]{:S(2)}) copy-start(bf16[2,256,256]{2,1,0:T(8,128)(2,1)} %copy-done.5) | copy-start | bytes 786436
  52.1 13.8 %collective-permute-start.16 = (bf16[4,256,256]{2,1,0:T(8,128)(2,1)S(1)}, bf16[4,256,256]{2,1,0:T(8,128)(2,1)S(1)}, u32[]{:S(2)}, u32[]{:S(2)}) collective-permute-start(bf16[4,256,256]{2,1,0:T(8,128)(2,1)S(1)} %collective-permute-done.12.rest_2_), channel_id=1, source_target_pairs={{0,7},{1,0},{2,1},{3,2},{4,3},{5,4},{6,5},{7,6},{8,15},{9,8},{10,9... | collective-permute-start | bytes 1572872 | tf_op jit(solution)/shard_map/ppermute | solution.py:40
  55.5 13.5 %collective-permute-start.14 = (bf16[4,256,256]{2,1,0:T(8,128)(2,1)S(1)}, bf16[4,256,256]{2,1,0:T(8,128)(2,1)S(1)}, u32[]{:S(2)}, u32[]{:S(2)}) collective-permute-start(bf16[4,256,256]{2,1,0:T(8,128)(2,1)S(1)} %collective-permute-done.10.rest_0_), channel_id=1, source_target_pairs={{0,1},{1,2},{2,3},{3,4},{4,5},{5,6},{6,7},{7,0},{8,9},{9,10},{10,1... | collective-permute-start | bytes 1572872 | tf_op jit(solution)/shard_map/ppermute | solution.py:40
  55.5 15.6 %collective-permute-start.13 = (bf16[4,256,256]{2,1,0:T(8,128)(2,1)S(1)}, bf16[4,256,256]{2,1,0:T(8,128)(2,1)S(1)}, u32[]{:S(2)}, u32[]{:S(2)}) collective-permute-start(bf16[4,256,256]{2,1,0:T(8,128)(2,1)S(1)} %collective-permute-done.12.rest_2_), channel_id=1, source_target_pairs={{0,32},{1,33},{2,34},{3,35},{4,36},{5,37},{6,38},{7,39},{8,40},{9,... | collective-permute-start | bytes 1572872 | tf_op jit(solution)/shard_map/ppermute | solution.py:40
  56.6 14.5 %collective-permute-start.11 = (bf16[4,256,256]{2,1,0:T(8,128)(2,1)S(1)}, bf16[4,256,256]{2,1,0:T(8,128)(2,1)S(1)}, u32[]{:S(2)}, u32[]{:S(2)}) collective-permute-start(bf16[4,256,256]{2,1,0:T(8,128)(2,1)S(1)} %collective-permute-done.10.rest_0_), channel_id=1, source_target_pairs={{0,32},{1,33},{2,34},{3,35},{4,36},{5,37},{6,38},{7,39},{8,40},{9,... | collective-permute-start | bytes 1572872 | tf_op jit(solution)/shard_map/ppermute | solution.py:40
  66.0 20.9 %collective-permute-start.17 = (bf16[4,256,256]{2,1,0:T(8,128)(2,1)S(1)}, bf16[4,256,256]{2,1,0:T(8,128)(2,1)S(1)}, u32[]{:S(2)}, u32[]{:S(2)}) collective-permute-start(bf16[4,256,256]{2,1,0:T(8,128)(2,1)S(1)} %collective-permute-done.16.rest_2_), channel_id=1, source_target_pairs={{0,32},{1,33},{2,34},{3,35},{4,36},{5,37},{6,38},{7,39},{8,40},{9,... | collective-permute-start | bytes 1572872 | tf_op jit(solution)/shard_map/ppermute | solution.py:40
  69.1 17.8 %collective-permute-start.15 = (bf16[4,256,256]{2,1,0:T(8,128)(2,1)S(1)}, bf16[4,256,256]{2,1,0:T(8,128)(2,1)S(1)}, u32[]{:S(2)}, u32[]{:S(2)}) collective-permute-start(bf16[4,256,256]{2,1,0:T(8,128)(2,1)S(1)} %collective-permute-done.14.rest_0_), channel_id=1, source_target_pairs={{0,32},{1,33},{2,34},{3,35},{4,36},{5,37},{6,38},{7,39},{8,40},{9,... | collective-permute-start | bytes 1572872 | tf_op jit(solution)/shard_map/ppermute | solution.py:40
  76.8 9.2 %collective-permute-start.18 = (bf16[2,256,256]{2,1,0:T(8,128)(2,1)S(1)}, bf16[2,256,256]{2,1,0:T(8,128)(2,1)S(1)}, u32[]{:S(2)}, u32[]{:S(2)}) collective-permute-start(bf16[2,256,256]{2,1,0:T(8,128)(2,1)S(1)} %slice.38), channel_id=1, source_target_pairs={{0,1},{1,2},{2,3},{3,4},{4,5},{5,6},{6,7},{7,0},{8,9},{9,10},{10,1... | collective-permute-start | bytes 786440 | tf_op jit(solution)/shard_map/ppermute | solution.py:40
  77.0 9.9 %collective-permute-start.20 = (bf16[2,256,256]{2,1,0:T(8,128)(2,1)S(1)}, bf16[2,256,256]{2,1,0:T(8,128)(2,1)S(1)}, u32[]{:S(2)}, u32[]{:S(2)}) collective-permute-start(bf16[2,256,256]{2,1,0:T(8,128)(2,1)S(1)} %slice.39), channel_id=1, source_target_pairs={{0,7},{1,0},{2,1},{3,2},{4,3},{5,4},{6,5},{7,6},{8,15},{9,8},{10,9... | collective-permute-start | bytes 786440 | tf_op jit(solution)/shard_map/ppermute | solution.py:40
  86.1 6.6 %collective-permute-start.19 = (bf16[2,256,256]{2,1,0:T(8,128)(2,1)S(1)}, bf16[2,256,256]{2,1,0:T(8,128)(2,1)S(1)}, u32[]{:S(2)}, u32[]{:S(2)}) collective-permute-start(bf16[2,256,256]{2,1,0:T(8,128)(2,1)S(1)} %collective-permute-done.18.rest_0_), channel_id=1, source_target_pairs={{0,32},{1,33},{2,34},{3,35},{4,36},{5,37},{6,38},{7,39},{8,40},{9,... | collective-permute-start | bytes 786440 | tf_op jit(solution)/shard_map/ppermute | solution.py:40
  86.8 5.8 %collective-permute-start.21 = (bf16[2,256,256]{2,1,0:T(8,128)(2,1)S(1)}, bf16[2,256,256]{2,1,0:T(8,128)(2,1)S(1)}, u32[]{:S(2)}, u32[]{:S(2)}) collective-permute-start(bf16[2,256,256]{2,1,0:T(8,128)(2,1)S(1)} %collective-permute-done.20.rest_2_), channel_id=1, source_target_pairs={{0,32},{1,33},{2,34},{3,35},{4,36},{5,37},{6,38},{7,39},{8,40},{9,... | collective-permute-start | bytes 786440 | tf_op jit(solution)/shard_map/ppermute | solution.py:40

commit v3 on v2

--- a/solution.py
+++ b/solution.py
@@ -1,5 +1,6 @@
 import functools
 import math
+import typing
 
 import jax
 import jax.numpy as jnp
@@ -65,16 +66,23 @@
     ]
 
 
+class Stream(typing.NamedTuple):
+    pair: int
+    base: int
+    count: int
+    offset: int
+
+
 def any_turn(i):
     return jnp.where(i < 2, -i, i - 1)
 
 
-def early_turn(i):
-    return -i
-
-
-def late_turn(i):
-    return i + 1
+def split(pair, offset):
+    return (Stream(pair, 0, 2, offset), Stream(pair, 2, 2, offset))
+
+
+def both(pair, offset):
+    return (Stream(pair, 0, 4, -offset), Stream(pair + 1, 0, 4, offset))
 
 
 def nt(a, b):
@@ -221,33 +229,48 @@
     )(ids, location, got, theirs)
 
 
-def passage_kernel(steps, counts, last, spot_ref, count_ref, list_ref, q_ref, acc_in, m_in, *rest):
-    blocks = rest[:4]
+def passage_kernel(rounds, n_pairs, last, spot_ref, count_ref, list_ref, q_ref, acc_in, m_in, *rest):
+    blocks = rest[: 2 * n_pairs]
     if last:
-        out_ref, acc, m = rest[4:]
+        out_ref, acc, m = rest[2 * n_pairs :]
     else:
-        acc, m = rest[4:]
+        acc, m = rest[2 * n_pairs :]
     acc[...] = acc_in[...]
     m[...] = m_in[...]
     ones = jnp.ones((256, D), jnp.bfloat16)
 
+    for streams in rounds:
+        run_streams(streams, blocks, ones, spot_ref, count_ref, list_ref, q_ref, acc, m)
+    if last:
+
+        @pl.loop(0, NR)
+        def _(r):
+            at = pl.ds(pl.multiple_of(r * ROWS, ROWS), ROWS)
+            o = (acc[at, 0:D] / acc[at, D:]).astype(jnp.bfloat16)
+            for g in range(GROUP):
+                out_ref[pl.ds(pl.multiple_of(r * T, T), T), g * D : (g + 1) * D] = o[
+                    g * T : (g + 1) * T
+                ]
+
+
+def run_streams(streams, blocks, ones, spot_ref, count_ref, list_ref, q_ref, acc, m):
     def place_of(s, i):
-        turn = steps[s][1](i)
-        return ((spot_ref[0] + turn) & (NY - 1)) * NZ + ((spot_ref[1] + steps[s][0]) & (NZ - 1))
+        turn = any_turn(streams[s].base + i)
+        up = spot_ref[1] + streams[s].offset
+        return ((spot_ref[0] + turn) & (NY - 1)) * NZ + (up & (NZ - 1))
 
     def batches(s):
         total = 0
-        for i in range(counts[s]):
-            count = count_ref[place_of(s, i)]
-            total = total + jnp.maximum((count + BATCH - 1) // BATCH, 1)
+        for i in range(streams[s].count):
+            total = total + jnp.maximum((count_ref[place_of(s, i)] + BATCH - 1) // BATCH, 1)
         return total
 
     def step(_, carry):
         at, sc, keep = [], [], []
         ahead = []
         for s, (i, b) in enumerate(carry):
-            i_here = jnp.minimum(i, counts[s] - 1)
-            place = jnp.where(i < counts[s], place_of(s, i_here), PLACES)
+            i_here = jnp.minimum(i, streams[s].count - 1)
+            place = jnp.where(i < streams[s].count, place_of(s, i_here), PLACES)
             count = count_ref[place]
             rows = [
                 jnp.where(b * BATCH + k < count, list_ref[place, b * BATCH + k], NR)
@@ -257,9 +280,10 @@
             full = (b + 1) * BATCH >= count
             ahead.append((i + full.astype(jnp.int32), jnp.where(full, 0, b + 1)))
             q = jnp.concatenate([q_ref[a, :] for a in at[s]], axis=0)
-            here = [blocks[2 * s], blocks[2 * s + 1]]
-            sc.append([nt(q, h[i_here, :, 0:D]) for h in here])
-            keep.append([jnp.concatenate([h[i_here, :, D:], ones], axis=1) for h in here])
+            pair = streams[s].pair
+            here = [h.at[streams[s].base + i_here] for h in blocks[2 * pair : 2 * pair + 2]]
+            sc.append([nt(q, h[:, 0:D]) for h in here])
+            keep.append([jnp.concatenate([h[:, D:], ones], axis=1) for h in here])
         new, shrink = [], []
         for s in range(2):
             top = jnp.maximum(
@@ -293,22 +317,11 @@
 
     start = ((jnp.int32(0), jnp.int32(0)),) * 2
     lax.fori_loop(0, jnp.maximum(batches(0), batches(1)), step, start)
-    if last:
-
-        @pl.loop(0, NR)
-        def _(r):
-            at = pl.ds(pl.multiple_of(r * ROWS, ROWS), ROWS)
-            o = (acc[at, 0:D] / acc[at, D:]).astype(jnp.bfloat16)
-            for g in range(GROUP):
-                out_ref[pl.ds(pl.multiple_of(r * T, T), T), g * D : (g + 1) * D] = o[
-                    g * T : (g + 1) * T
-                ]
-
-
-def passage_call(spot, counts_of, lists, q, acc, m, steps, pairs, last):
+
+
+def passage_call(spot, counts_of, lists, q, acc, m, rounds, pairs, last=False):
     n = SLOTS * ROWS
-    counts = tuple(mine.shape[0] for mine, _ in pairs)
-    total = sum(counts)
+    total = sum(stream.count for streams in rounds for stream in streams)
     state = (jax.ShapeDtypeStruct((n, 2 * D), jnp.float32), jax.ShapeDtypeStruct((n, D), jnp.float32))
     scratch = []
     if last:
@@ -321,9 +334,9 @@
     vmem = pl.BlockSpec(memory_space=pltpu.VMEM)
     smem = pl.BlockSpec(memory_space=pltpu.SMEM)
     return pl.pallas_call(
-        functools.partial(passage_kernel, steps, counts, last),
+        functools.partial(passage_kernel, rounds, len(pairs), last),
         out_shape=out_shape,
-        in_specs=[smem] * 3 + [vmem] * (3 + 2 * len(counts)),
+        in_specs=[smem] * 3 + [vmem] * (3 + 2 * len(pairs)),
         out_specs=(vmem,) * len(out_shape),
         scratch_shapes=scratch,
         input_output_aliases=aliases,
@@ -361,43 +374,37 @@
     odd = jnp.concatenate([k2[:, D:], v2[:, D:]], axis=1)
     kept = jnp.where(low == 0, even, odd)
     given = jnp.where(low == 0, odd, even)
-    column = jnp.stack(
-        [kept, send(given, y_by(1)), send(given, y_by(-1)), send(kept, y_by(2))]
-    )
-
     ids = jnp.pad(retrieval.astype(jnp.bfloat16), ((0, 0), (0, D - TOPK)))
     ids = jnp.broadcast_to(ids[:, None, :], (RESP, T, D)).reshape(64, D)
     parcel = parcel_call(after(low, given), queries, own_keys, own_values, prefix_keys, prefix_values, ids)
+    pieces = [kept, send(given, y_by(1)), send(given, y_by(-1)), send(kept, y_by(2))]
+    pieces[3] = after(pieces[3], parcel)
+    column = jnp.stack(pieces)
+    def swap(block):
+        return block, send(block, other_core)
+
     got = lax.all_to_all(after(parcel, column), AXES, 0, 0, tiled=True, axis_index_groups=head_groups())
+    up1, down1 = send(column, z_by(1)), send(column, z_by(-1))
+    up2, down2 = send(up1, z_by(1)), send(down1, z_by(-1))
+    one = [swap(up1), swap(down1)]
+    got = after(got, one[0][1], one[1][1])
+    here = swap(after(column, got))
     theirs = send(got[:, :, 768:1024], other_core)
     chosen = got[:, :, 1024 : 1024 + TOPK].reshape(NR, T, TOPK)[:, 0].astype(jnp.int32)
     q, acc, m, counts_of, lists = first_call(chosen, location, got, theirs)
 
-    def passages(chunks, acc, m, last=False):
-        steps = tuple((offset, turn) for offset, turn, _ in chunks)
-        pairs = [pair for _, _, pair in chunks]
-        return passage_call(spot, counts_of, lists, q, acc, m, steps, pairs, last)
-
-    def swap(block):
-        return block, send(block, other_core)
-
-    first = [swap(column[:2]), swap(column[2:])]
-    up1, down1 = send(column, z_by(1)), send(column, z_by(-1))
-    ups, downs = [swap(up1)], [swap(down1)]
-    swapped = (first[0][1], first[1][1])
-    ups.append(swap(send(after(up1, *swapped), z_by(1))))
-    downs.append(swap(send(after(down1, *swapped), z_by(-1))))
-    swapped = (ups[0][1], downs[0][1])
-    ups.append(swap(send(after(ups[1][0], m, *swapped), z_by(1))))
-    acc, m = passages([(0, early_turn, first[0]), (0, late_turn, first[1])], acc, m)
-    downs.append(swap(send(after(downs[1][0], m, *swapped), z_by(-1))))
-    for k in range(2):
-        acc, m = passages([(-k - 1, any_turn, ups[k]), (k + 1, any_turn, downs[k])], acc, m)
-    swapped = (ups[1][1], downs[1][1])
-    last_up = swap(send(after(ups[2][0], m, *swapped)[:2], z_by(1)))
-    last_down = swap(send(after(downs[2][0], m, *swapped)[2:], z_by(-1)))
-    acc, m = passages([(-3, any_turn, ups[2]), (3, any_turn, downs[2])], acc, m)
-    (out,) = passages([(4, early_turn, last_up), (4, late_turn, last_down)], acc, m, True)
+    state = (spot, counts_of, lists, q)
+    seen = (m, one[0][1], one[1][1])
+    up3, down3 = send(after(up2, *seen), z_by(1)), send(after(down2, *seen), z_by(-1))
+    two = [swap(after(up2, m)), swap(after(down2, m))]
+    acc, m = passage_call(*state, acc, m, (split(0, 0), both(1, 1)), [here] + one)
+    up3, down3 = after(up3, m), after(down3, m)
+    four = send(jnp.where(c == 0, up3, down3), lambda x, c, y, z: (x, c, y, z + 1 - 2 * c))
+    three = [swap(up3), swap(down3)]
+    acc, m = passage_call(*state, acc, m, (both(0, 2),), two)
+    four = after(four, m)
+    acc, m = passage_call(*state, acc, m, (both(0, 3),), three)
+    (out,) = passage_call(*state, acc, m, (split(0, 4),), [swap(four)], True)
 
     out = out.reshape(KV, 64, GROUP * D)
     home = lax.all_to_all(out, AXES, 0, 0, tiled=True, axis_index_groups=head_groups())

time: 110 us -> 99.3 us (0.903)
  starting transfers between devices: 38.2 us -> 33.5 us
  waiting for transfers between devices: 23.1 us -> 18.5 us
  blocking collectives: 11.9 us -> 13.8 us
  Pallas kernels: 31.2 us -> 29.4 us
    ppermute x22 -> x19, waiting for transfers between devices: 23.1 us -> 13.1 us  [send(): return lax.ppermute(block, AXES, moves(to))]
    ppermute x22 -> x19, starting transfers between devices: 33.5 us -> 27.8 us  [send(): return lax.ppermute(block, AXES, moves(to))]
    all_to_all x1, waiting for transfers between devices: 0.01 us -> 5.37 us  [per_device(): lax.all_to_all(after(parcel, column), AXES, 0, 0, tiled=True, axis_index_...]
    all_to_all x1, blocking collectives: 11.9 us -> 13.8 us  [per_device(): lax.all_to_all(out, AXES, 0, 0, tiled=True, axis_index_groups=head_groups())]
    pallas_call x5 -> x4, Pallas kernels: 23.9 us -> 22.1 us  [passage_call(): pl.pallas_call(functools.partial(passage_kernel, rounds, len(pairs), last...]
  transfers between devices with their start and end apart: 23 -> 20, of which waited for: 8 -> 7; matrix products, arithmetic and copies ran while one was open for 0% -> 1% of each run, Pallas kernels for 26% -> 26%
where the time goes in v3:
time: 99.3 us; the launch traced here: 99.1 us
  starting transfers between devices  33.5 us (34%)
  Pallas kernels  29.4 us (30%)
  waiting for transfers between devices  18.5 us (19%)
  blocking collectives  13.8 us (14%)
  local copies, waits for them, and re-layouts  3.3 us (3%)
    ppermute x19, starting transfers between devices, send(): return lax.ppermute(block, AXES, moves(to))  27.8 us
    pallas_call x4, Pallas kernels, passage_call(): pl.pallas_call(functools.partial(passage_kernel, rounds, len(pairs), last...  22.1 us
    all_to_all x1, blocking collectives, per_device(): lax.all_to_all(out, AXES, 0, 0, tiled=True, axis_index_groups=head_groups())  13.8 us
    ppermute x19, waiting for transfers between devices, send(): return lax.ppermute(block, AXES, moves(to))  13.1 us
    all_to_all x1, starting transfers between devices, per_device(): lax.all_to_all(after(parcel, column), AXES, 0, 0, tiled=True, axis_index_...  5.71 us
    pallas_call x1, Pallas kernels, first_call(): pl.pallas_call(first_kernel, out_shape=(jax.ShapeDtypeStruct((n, D), jnp....  5.38 us
    all_to_all x1, waiting for transfers between devices, per_device(): lax.all_to_all(after(parcel, column), AXES, 0, 0, tiled=True, axis_index_...  5.37 us
  transfers between devices with their start and end apart: 20, of which 7 were waited for; matrix products, arithmetic and copies ran while one was open for 1% of the time, Pallas kernels for 26%

profile of v3, /device:TPU:1, one launch (start us, length us, event | category | flops | bytes accessed | tf_op | source)
XLA Modules:
  0.0 99.1 jit_solution(7973878378119345219)
XLA Ops:
  0.1 1.1 %dynamic-slice_bitcast_fusion = (bf16[256,256]{1,0:T(8,128)(2,1)S(1)}, bf16[256,256]{1,0:T(8,128)(2,1)S(1)}) fusion(bf16[1,512,1024]{2,1,0:T(8,128)(2,1)} %param.15, s32[]{:T(128)S(6)} %select_n.40, s32[]{:T(128)S(6)} %select_n.41, bf16[1,512,1024]{2,1,0:T(8,128)(2,1)} %param.14), kind=kLoop, calls=%fused_computation.5 | loop fusion | bytes 524296 | tf_op jit(solution)/shard_map/dynamic_slice | solution.py:370
  1.3 3.8 %collective-permute-start.2 = (bf16[256,256]{1,0:T(8,128)(2,1)S(1)}, bf16[256,256]{1,0:T(8,128)(2,1)S(1)}, u32[]{:S(2)}, u32[]{:S(2)}) collective-permute-start(bf16[256,256]{1,0:T(8,128)(2,1)S(1)} %get-tuple-element.51), channel_id=1, source_target_pairs={{0,16},{1,17},{2,18},{3,19},{4,20},{5,21},{6,22},{7,23},{8,24},{9,... | collective-permute-start | bytes 393224 | tf_op jit(solution)/shard_map/ppermute | solution.py:41
  5.1 0.8 collective-permute-start.1
  5.9 0.7 collective-permute-start
  6.7 1.9 %parcel.1 = bf16[8,64,1152]{2,1,0:T(8,128)(2,1)} custom-call(s32[1]{0:T(128)} %bitcast.4.low_ref, bf16[64,4096]{1,0:T(8,128)(2,1)S(1)} %bitcast.31, bf16[64,1024]{1,0:T(8,128)(2,1)S(1)} %bitcast.32, bf16[64,1024]{1,0:T(8,128)(2,1)S(1)} %bitcast.33, bf16[128,1024]{1,0:T(8,128)(2,1)S(1)} %copy-done.1, bf16[128,1024]{1,0:T(8,128)(2,1)S(1)} %copy-done.2, ...), custom_call_target="tpu_custom_call" | custom-call | bytes 6291456 | tf_op jit(solution)/shard_map/parcel/pallas_call | solution.py:114
  8.7 2.6 %collective-permute-done.1 = bf16[256,256]{1,0:T(8,128)(2,1)S(1)} collective-permute-done((bf16[256,256]{1,0:T(8,128)(2,1)S(1)}, bf16[256,256]{1,0:T(8,128)(2,1)S(1)}, u32[]{:S(2)}, u32[]{:S(2)}) %collective-permute-start.1) | collective-permute-done | bytes 131104 | tf_op jit(solution)/shard_map/ppermute | solution.py:41
  11.2 1.9 %collective-permute-done = bf16[256,256]{1,0:T(8,128)(2,1)S(1)} collective-permute-done((bf16[256,256]{1,0:T(8,128)(2,1)S(1)}, bf16[256,256]{1,0:T(8,128)(2,1)S(1)}, u32[]{:S(2)}, u32[]{:S(2)}) %collective-permute-start) | collective-permute-done | bytes 131104 | tf_op jit(solution)/shard_map/ppermute | solution.py:41
  13.2 3.8 %collective-permute-start.5 = (bf16[4,256,256]{2,1,0:T(8,128)(2,1)S(1)}, bf16[4,256,256]{2,1,0:T(8,128)(2,1)S(1)}, u32[]{:S(2)}, u32[]{:S(2)}) collective-permute-start(bf16[4,256,256]{2,1,0:T(8,128)(2,1)S(1)} %pad_maximum_fusion.rest_0_), channel_id=1, source_target_pairs={{0,7},{1,0},{2,1},{3,2},{4,3},{5,4},{6,5},{7,6},{8,15},{9,8},{10,9... | collective-permute-start | bytes 1572872 | tf_op jit(solution)/shard_map/ppermute | solution.py:41
  17.0 5.7 %all-to-all-start = ((bf16[8,64,1152]{2,1,0:T(8,128)(2,1)}), bf16[8,64,1152]{2,1,0:T(8,128)(2,1)S(1)}, u32[]{:S(2)}, u32[]{:S(2)}) async-start(bf16[8,64,1152]{2,1,0:T(8,128)(2,1)} %parcel.1), calls=%async_computation | async-start | bytes 2359296 | tf_op jit(solution)/shard_map/all_to_all | solution.py:386
  22.7 3.4 %collective-permute-done.5.rest_4_ = bf16[4,256,256]{2,1,0:T(8,128)(2,1)S(1)} collective-permute-done((bf16[4,256,256]{2,1,0:T(8,128)(2,1)S(1)}, bf16[4,256,256]{2,1,0:T(8,128)(2,1)S(1)}, u32[]{:S(2)}, u32[]{:S(2)}) %collective-permute-start.5) | collective-permute-done | bytes 524320 | tf_op jit(solution)/shard_map/ppermute | solution.py:41
  26.1 3.0 %collective-permute-start.6 = (bf16[4,256,256]{2,1,0:T(8,128)(2,1)S(1)}, bf16[4,256,256]{2,1,0:T(8,128)(2,1)}, u32[]{:S(2)}, u32[]{:S(2)}) collective-permute-start(bf16[4,256,256]{2,1,0:T(8,128)(2,1)S(1)} %collective-permute-done.5.rest_4_), channel_id=1, source_target_pairs={{0,32},{1,33},{2,34},{3,35},{4,36},{5,37},{6,38},{7,39},{8,40},{9,... | collective-permute-start | bytes 1572872 | tf_op jit(solution)/shard_map/ppermute | solution.py:41
  29.1 0.2 collective-permute-done.3.rest_2_
  29.4 3.3 %collective-permute-start.4 = (bf16[4,256,256]{2,1,0:T(8,128)(2,1)}, bf16[4,256,256]{2,1,0:T(8,128)(2,1)}, u32[]{:S(2)}, u32[]{:S(2)}) collective-permute-start(bf16[4,256,256]{2,1,0:T(8,128)(2,1)} %collective-permute-done.3.rest_2_), channel_id=1, source_target_pairs={{0,32},{1,33},{2,34},{3,35},{4,36},{5,37},{6,38},{7,39},{8,40},{9,... | collective-permute-start | bytes 1572872 | tf_op jit(solution)/shard_map/ppermute | solution.py:41
  32.6 1.5 %collective-permute-start.9 = (bf16[4,256,256]{2,1,0:T(8,128)(2,1)}, bf16[4,256,256]{2,1,0:T(8,128)(2,1)S(1)}, u32[]{:S(2)}, u32[]{:S(2)}) collective-permute-start(bf16[4,256,256]{2,1,0:T(8,128)(2,1)} %collective-permute-done.3.rest_2_), channel_id=1, source_target_pairs={{0,1},{1,2},{2,3},{3,4},{4,5},{5,6},{6,7},{7,0},{8,9},{9,10},{10,1... | collective-permute-start | bytes 1572872 | tf_op jit(solution)/shard_map/ppermute | solution.py:41
  34.1 5.4 %all-to-all-done.got_ref = bf16[8,64,1152]{2,1,0:T(8,128)(2,1)S(1)} async-done(((bf16[8,64,1152]{2,1,0:T(8,128)(2,1)}), bf16[8,64,1152]{2,1,0:T(8,128)(2,1)S(1)}, u32[]{:S(2)}, u32[]{:S(2)}) %all-to-all-start) | async-done | bytes 1179680 | tf_op jit(solution)/shard_map/all_to_all | solution.py:386
  39.5 0.7 slice.27
  40.2 1.7 %collective-permute-start.7 = (bf16[8,64,256]{2,1,0:T(8,128)(2,1)}, bf16[8,64,256]{2,1,0:T(8,128)(2,1)S(1)}, u32[]{:S(2)}, u32[]{:S(2)}) collective-permute-start(bf16[8,64,256]{2,1,0:T(8,128)(2,1)} %slice.27), channel_id=1, source_target_pairs={{0,32},{1,33},{2,34},{3,35},{4,36},{5,37},{6,38},{7,39},{8,40},{9,... | collective-permute-start | bytes 786440 | tf_op jit(solution)/shard_map/ppermute | solution.py:41
  42.1 1.6 %collective-permute-done.7.theirs_ref = bf16[8,64,256]{2,1,0:T(8,128)(2,1)S(1)} collective-permute-done((bf16[8,64,256]{2,1,0:T(8,128)(2,1)}, bf16[8,64,256]{2,1,0:T(8,128)(2,1)S(1)}, u32[]{:S(2)}, u32[]{:S(2)}) %collective-permute-start.7) | collective-permute-done | bytes 262176 | tf_op jit(solution)/shard_map/ppermute | solution.py:41
  43.7 5.4 %prefix_and_own.1 = (bf16[2112,128]{1,0:T(8,128)(2,1)S(1)}, f32[2112,256]{1,0:T(8,128)S(1)}, f32[2112,128]{1,0:T(8,128)S(1)}, s32[33]{0:T(128)S(1)}, s32[33,32]{1,0:T(8,128)S(1)}) custom-call(s32[32,8]{1,0:T(8,128)S(1)} %fusion.ids_ref, s32[32]{0:T(128)S(1)} %copy-done.5, bf16[8,64,1152]{2,1,0:T(8,128)(2,1)S(1)} %all-to-all-done.got_ref, ...), custom_call_target="tpu_custom_call" | custom-call | flops 2281701376 | bytes 6291456 | tf_op jit(solution)/shard_map/prefix_and_own/pallas_call | solution.py:209
  49.1 0.5 collective-permute-start.10
  49.7 2.7 %collective-permute-start.15 = (bf16[4,256,256]{2,1,0:T(8,128)(2,1)S(1)}, bf16[4,256,256]{2,1,0:T(8,128)(2,1)S(1)}, u32[]{:S(2)}, u32[]{:S(2)}) collective-permute-start(bf16[4,256,256]{2,1,0:T(8,128)(2,1)S(1)} %collective-permute-done.11.rest_2_), channel_id=1, source_target_pairs={{0,7},{1,0},{2,1},{3,2},{4,3},{5,4},{6,5},{7,6},{8,15},{9,8},{10,9... | collective-permute-start | bytes 1572872 | tf_op jit(solution)/shard_map/ppermute | solution.py:41
  52.4 8.2 %passages.4 = (f32[2112,256]{1,0:T(8,128)S(1)}, f32[2112,128]{1,0:T(8,128)S(1)}) custom-call(s32[2]{0:T(128)S(1)} %pad_add_fusion.spot_ref, s32[33]{0:T(128)S(1)} %get-tuple-element.32.count_ref, s32[33,32]{1,0:T(8,128)S(1)} %get-tuple-element.33.list_ref, ...), custom_call_target="tpu_custom_call", output_to_operand_aliasing={{0}: (4, {}), {1}: (5, {})} | custom-call | flops 8053063680 | bytes 6291456 | tf_op jit(solution)/shard_map/passages/pallas_call | solution.py:336
  60.6 3.4 %collective-permute-done.13.rest_0_ = bf16[4,256,256]{2,1,0:T(8,128)(2,1)S(1)} collective-permute-done((bf16[4,256,256]{2,1,0:T(8,128)(2,1)S(1)}, bf16[4,256,256]{2,1,0:T(8,128)(2,1)S(1)}, u32[]{:S(2)}, u32[]{:S(2)}) %collective-permute-start.13) | collective-permute-done | bytes 524320 | tf_op jit(solution)/shard_map/ppermute | solution.py:41
  64.1 2.4 %collective-permute-start.17 = (bf16[4,256,256]{2,1,0:T(8,128)(2,1)S(1)}, bf16[4,256,256]{2,1,0:T(8,128)(2,1)S(1)}, u32[]{:S(2)}, u32[]{:S(2)}) collective-permute-start(bf16[4,256,256]{2,1,0:T(8,128)(2,1)S(1)} %broadcast_select_fusion), channel_id=1, source_target_pairs={{0,1},{1,2},{2,3},{3,4},{4,5},{5,6},{6,7},{7,0},{8,9},{9,10},{10,1... | collective-permute-start | bytes 1572872 | tf_op jit(solution)/shard_map/ppermute | solution.py:41
  66.5 0.5 collective-permute-start.16
  67.0 5.7 %passages.5 = (f32[2112,256]{1,0:T(8,128)S(1)}, f32[2112,128]{1,0:T(8,128)S(1)}) custom-call(s32[2]{0:T(128)S(1)} %pad_add_fusion.spot_ref, s32[33]{0:T(128)S(1)} %get-tuple-element.32.count_ref, s32[33,32]{1,0:T(8,128)S(1)} %get-tuple-element.33.list_ref, ...), custom_call_target="tpu_custom_call", output_to_operand_aliasing={{0}: (4, {}), {1}: (5, {})} | custom-call | flops 5368709120 | bytes 6291456 | tf_op jit(solution)/shard_map/passages/pallas_call | solution.py:336
  72.8 3.0 %collective-permute-start.18 = (bf16[4,256,256]{2,1,0:T(8,128)(2,1)S(1)}, bf16[4,256,256]{2,1,0:T(8,128)(2,1)S(1)}, u32[]{:S(2)}, u32[]{:S(2)}) collective-permute-start(bf16[4,256,256]{2,1,0:T(8,128)(2,1)S(1)} %collective-permute-done.17.rest_0_), channel_id=1, source_target_pairs={{0,32},{1,33},{2,34},{3,35},{4,36},{5,37},{6,38},{7,39},{8,40},{9,... | collective-permute-start | bytes 1572872 | tf_op jit(solution)/shard_map/ppermute | solution.py:41
  75.8 4.9 %passages.6 = (f32[2112,256]{1,0:T(8,128)S(1)}, f32[2112,128]{1,0:T(8,128)S(1)}) custom-call(s32[2]{0:T(128)S(1)} %pad_add_fusion.spot_ref, s32[33]{0:T(128)S(1)} %get-tuple-element.32.count_ref, s32[33,32]{1,0:T(8,128)S(1)} %get-tuple-element.33.list_ref, ...), custom_call_target="tpu_custom_call", output_to_operand_aliasing={{0}: (4, {}), {1}: (5, {})} | custom-call | flops 5368709120 | bytes 6291456 | tf_op jit(solution)/shard_map/passages/pallas_call | solution.py:336
  80.7 3.3 %passages.7 = bf16[512,512]{1,0:T(8,128)(2,1)S(1)} custom-call(s32[2]{0:T(128)S(1)} %pad_add_fusion.spot_ref, s32[33]{0:T(128)S(1)} %get-tuple-element.32.count_ref, s32[33,32]{1,0:T(8,128)S(1)} %get-tuple-element.33.list_ref, bf16[2112,128]{1,0:T(8,128)(2,1)S(1)} %get-tuple-element.34.q_ref, f32[2112,256]{1,0:T(8,128)S(1)} %get-tuple-element.48.acc_in, ...), custom_call_target="tpu_custom_call" | custom-call | flops 2684354560 | bytes 6291456 | tf_op jit(solution)/shard_map/passages/pallas_call | solution.py:336
  84.0 13.8 %all_to_all.10 = bf16[8,64,512]{2,1,0:T(8,128)(2,1)S(1)} all-to-all(bf16[8,64,512]{2,1,0:T(8,128)(2,1)S(1)} %bitcast.30), channel_id=1, replica_groups={{0,8,64,72,128,136,192,200},{1,9,65,73,129,137,193,201},{2,10,66,74,130..., dimensions={0} | all-to-all | bytes 1048576 | tf_op jit(solution)/shard_map/all_to_all | solution.py:410
  97.7 0.3 copy.17
  98.0 1.0 %reshape.91 = bf16[4,16,4096]{2,1,0:T(8,128)(2,1)} reshape(bf16[64,8,512]{2,1,0:T(8,128)(2,1)S(1)} %copy.17) | data formatting | bytes 1048576 | tf_op jit(solution)/shard_map/reshape | solution.py:411
  (46 shorter events, 0.6 us)
Async XLA Ops:
  0.0 6.6 %copy-start.6 = (s32[4,8]{1,0:T(4,128)S(1)}, s32[4,8]{1,0:T(4,128)}, u32[]{:S(2)}) copy-start(s32[4,8]{1,0:T(4,128)} %param.16) | copy-start | bytes 388
  0.0 6.6 %copy-start.2 = (bf16[128,1024]{1,0:T(8,128)(2,1)S(1)}, bf16[128,1024]{1,0:T(8,128)(2,1)}, u32[]{:S(2)}) copy-start(bf16[128,1024]{1,0:T(8,128)(2,1)} %pv_hbm.1) | copy-start | bytes 786436
  0.0 6.6 %copy-start.1 = (bf16[128,1024]{1,0:T(8,128)(2,1)S(1)}, bf16[128,1024]{1,0:T(8,128)(2,1)}, u32[]{:S(2)}) copy-start(bf16[128,1024]{1,0:T(8,128)(2,1)} %pk_hbm.1) | copy-start | bytes 786436
  0.0 6.6 %copy-start.4 = (bf16[4,16,1024]{2,1,0:T(8,128)(2,1)S(1)}, bf16[4,16,1024]{2,1,0:T(8,128)(2,1)}, u32[]{:S(2)}) copy-start(bf16[4,16,1024]{2,1,0:T(8,128)(2,1)} %param.11) | copy-start | bytes 393220
  0.0 6.6 %copy-start.3 = (bf16[4,16,1024]{2,1,0:T(8,128)(2,1)S(1)}, bf16[4,16,1024]{2,1,0:T(8,128)(2,1)}, u32[]{:S(2)}) copy-start(bf16[4,16,1024]{2,1,0:T(8,128)(2,1)} %param.10) | copy-start | bytes 393220
  0.0 6.6 %copy-start = (bf16[4,16,4096]{2,1,0:T(8,128)(2,1)S(1)}, bf16[4,16,4096]{2,1,0:T(8,128)(2,1)}, u32[]{:S(2)}) copy-start(bf16[4,16,4096]{2,1,0:T(8,128)(2,1)} %param.9) | copy-start | bytes 1572868
  1.3 7.4 %collective-permute-start.2 = (bf16[256,256]{1,0:T(8,128)(2,1)S(1)}, bf16[256,256]{1,0:T(8,128)(2,1)S(1)}, u32[]{:S(2)}, u32[]{:S(2)}) collective-permute-start(bf16[256,256]{1,0:T(8,128)(2,1)S(1)} %get-tuple-element.51), channel_id=1, source_target_pairs={{0,16},{1,17},{2,18},{3,19},{4,20},{5,21},{6,22},{7,23},{8,24},{9,... | collective-permute-start | bytes 393224 | tf_op jit(solution)/shard_map/ppermute | solution.py:41
  5.1 6.1 %collective-permute-start.1 = (bf16[256,256]{1,0:T(8,128)(2,1)S(1)}, bf16[256,256]{1,0:T(8,128)(2,1)S(1)}, u32[]{:S(2)}, u32[]{:S(2)}) collective-permute-start(bf16[256,256]{1,0:T(8,128)(2,1)S(1)} %get-tuple-element.52), channel_id=1, source_target_pairs={{0,24},{1,25},{2,26},{3,27},{4,28},{5,29},{6,30},{7,31},{8,0},{9,1... | collective-permute-start | bytes 393224 | tf_op jit(solution)/shard_map/ppermute | solution.py:41
  5.9 7.2 %collective-permute-start = (bf16[256,256]{1,0:T(8,128)(2,1)S(1)}, bf16[256,256]{1,0:T(8,128)(2,1)S(1)}, u32[]{:S(2)}, u32[]{:S(2)}) collective-permute-start(bf16[256,256]{1,0:T(8,128)(2,1)S(1)} %get-tuple-element.52), channel_id=1, source_target_pairs={{0,8},{1,9},{2,10},{3,11},{4,12},{5,13},{6,14},{7,15},{8,16},{9,17... | collective-permute-start | bytes 393224 | tf_op jit(solution)/shard_map/ppermute | solution.py:41
  13.2 30.5 %copy-start.5 = (s32[32]{0:T(128)S(1)}, s32[32]{0:T(128)}, u32[]{:S(2)}) copy-start(s32[32]{0:T(128)} %at_ref.1) | copy-start | bytes 388
  13.2 12.9 %collective-permute-start.5 = (bf16[4,256,256]{2,1,0:T(8,128)(2,1)S(1)}, bf16[4,256,256]{2,1,0:T(8,128)(2,1)S(1)}, u32[]{:S(2)}, u32[]{:S(2)}) collective-permute-start(bf16[4,256,256]{2,1,0:T(8,128)(2,1)S(1)} %pad_maximum_fusion.rest_0_), channel_id=1, source_target_pairs={{0,7},{1,0},{2,1},{3,2},{4,3},{5,4},{6,5},{7,6},{8,15},{9,8},{10,9... | collective-permute-start | bytes 1572872 | tf_op jit(solution)/shard_map/ppermute | solution.py:41
  17.0 12.4 %collective-permute-start.3 = (bf16[4,256,256]{2,1,0:T(8,128)(2,1)S(1)}, bf16[4,256,256]{2,1,0:T(8,128)(2,1)}, u32[]{:S(2)}, u32[]{:S(2)}) collective-permute-start(bf16[4,256,256]{2,1,0:T(8,128)(2,1)S(1)} %pad_maximum_fusion.rest_0_), channel_id=1, source_target_pairs={{0,1},{1,2},{2,3},{3,4},{4,5},{5,6},{6,7},{7,0},{8,9},{9,10},{10,1... | collective-permute-start | bytes 1572872 | tf_op jit(solution)/shard_map/ppermute | solution.py:41
  17.0 22.5 %all-to-all-start = ((bf16[8,64,1152]{2,1,0:T(8,128)(2,1)}), bf16[8,64,1152]{2,1,0:T(8,128)(2,1)S(1)}, u32[]{:S(2)}, u32[]{:S(2)}) async-start(bf16[8,64,1152]{2,1,0:T(8,128)(2,1)} %parcel.1), calls=%async_computation | async-start | bytes 2359296 | tf_op jit(solution)/shard_map/all_to_all | solution.py:386
  26.1 13.4 %collective-permute-start.6 = (bf16[4,256,256]{2,1,0:T(8,128)(2,1)S(1)}, bf16[4,256,256]{2,1,0:T(8,128)(2,1)}, u32[]{:S(2)}, u32[]{:S(2)}) collective-permute-start(bf16[4,256,256]{2,1,0:T(8,128)(2,1)S(1)} %collective-permute-done.5.rest_4_), channel_id=1, source_target_pairs={{0,32},{1,33},{2,34},{3,35},{4,36},{5,37},{6,38},{7,39},{8,40},{9,... | collective-permute-start | bytes 1572872 | tf_op jit(solution)/shard_map/ppermute | solution.py:41
  29.4 10.1 %collective-permute-start.4 = (bf16[4,256,256]{2,1,0:T(8,128)(2,1)}, bf16[4,256,256]{2,1,0:T(8,128)(2,1)}, u32[]{:S(2)}, u32[]{:S(2)}) collective-permute-start(bf16[4,256,256]{2,1,0:T(8,128)(2,1)} %collective-permute-done.3.rest_2_), channel_id=1, source_target_pairs={{0,32},{1,33},{2,34},{3,35},{4,36},{5,37},{6,38},{7,39},{8,40},{9,... | collective-permute-start | bytes 1572872 | tf_op jit(solution)/shard_map/ppermute | solution.py:41
  32.6 16.4 %collective-permute-start.11 = (bf16[4,256,256]{2,1,0:T(8,128)(2,1)S(1)}, bf16[4,256,256]{2,1,0:T(8,128)(2,1)S(1)}, u32[]{:S(2)}, u32[]{:S(2)}) collective-permute-start(bf16[4,256,256]{2,1,0:T(8,128)(2,1)S(1)} %collective-permute-done.5.rest_4_), channel_id=1, source_target_pairs={{0,7},{1,0},{2,1},{3,2},{4,3},{5,4},{6,5},{7,6},{8,15},{9,8},{10,9... | collective-permute-start | bytes 1572872 | tf_op jit(solution)/shard_map/ppermute | solution.py:41
  32.6 16.4 %collective-permute-start.9 = (bf16[4,256,256]{2,1,0:T(8,128)(2,1)}, bf16[4,256,256]{2,1,0:T(8,128)(2,1)S(1)}, u32[]{:S(2)}, u32[]{:S(2)}) collective-permute-start(bf16[4,256,256]{2,1,0:T(8,128)(2,1)} %collective-permute-done.3.rest_2_), channel_id=1, source_target_pairs={{0,1},{1,2},{2,3},{3,4},{4,5},{5,6},{6,7},{7,0},{8,9},{9,10},{10,1... | collective-permute-start | bytes 1572872 | tf_op jit(solution)/shard_map/ppermute | solution.py:41
  40.2 3.5 %collective-permute-start.7 = (bf16[8,64,256]{2,1,0:T(8,128)(2,1)}, bf16[8,64,256]{2,1,0:T(8,128)(2,1)S(1)}, u32[]{:S(2)}, u32[]{:S(2)}) collective-permute-start(bf16[8,64,256]{2,1,0:T(8,128)(2,1)} %slice.27), channel_id=1, source_target_pairs={{0,32},{1,33},{2,34},{3,35},{4,36},{5,37},{6,38},{7,39},{8,40},{9,... | collective-permute-start | bytes 786440 | tf_op jit(solution)/shard_map/ppermute | solution.py:41
  42.0 10.4 %collective-permute-start.8 = (bf16[4,256,256]{2,1,0:T(8,128)(2,1)S(1)}, bf16[4,256,256]{2,1,0:T(8,128)(2,1)}, u32[]{:S(2)}, u32[]{:S(2)}) collective-permute-start(bf16[4,256,256]{2,1,0:T(8,128)(2,1)S(1)} %pad_maximum_fusion.rest_0_), channel_id=1, source_target_pairs={{0,32},{1,33},{2,34},{3,35},{4,36},{5,37},{6,38},{7,39},{8,40},{9,... | collective-permute-start | bytes 1572872 | tf_op jit(solution)/shard_map/ppermute | solution.py:41
  49.1 17.9 %collective-permute-start.10 = (bf16[4,256,256]{2,1,0:T(8,128)(2,1)S(1)}, bf16[4,256,256]{2,1,0:T(8,128)(2,1)S(1)}, u32[]{:S(2)}, u32[]{:S(2)}) collective-permute-start(bf16[4,256,256]{2,1,0:T(8,128)(2,1)S(1)} %collective-permute-done.9.rest_0_), channel_id=1, source_target_pairs={{0,32},{1,33},{2,34},{3,35},{4,36},{5,37},{6,38},{7,39},{8,40},{9,... | collective-permute-start | bytes 1572872 | tf_op jit(solution)/shard_map/ppermute | solution.py:41
  49.5 17.5 %collective-permute-start.12 = (bf16[4,256,256]{2,1,0:T(8,128)(2,1)S(1)}, bf16[4,256,256]{2,1,0:T(8,128)(2,1)S(1)}, u32[]{:S(2)}, u32[]{:S(2)}) collective-permute-start(bf16[4,256,256]{2,1,0:T(8,128)(2,1)S(1)} %collective-permute-done.11.rest_2_), channel_id=1, source_target_pairs={{0,32},{1,33},{2,34},{3,35},{4,36},{5,37},{6,38},{7,39},{8,40},{9,... | collective-permute-start | bytes 1572872 | tf_op jit(solution)/shard_map/ppermute | solution.py:41
  49.7 14.3 %collective-permute-start.13 = (bf16[4,256,256]{2,1,0:T(8,128)(2,1)S(1)}, bf16[4,256,256]{2,1,0:T(8,128)(2,1)S(1)}, u32[]{:S(2)}, u32[]{:S(2)}) collective-permute-start(bf16[4,256,256]{2,1,0:T(8,128)(2,1)S(1)} %collective-permute-done.9.rest_0_), channel_id=1, source_target_pairs={{0,1},{1,2},{2,3},{3,4},{4,5},{5,6},{6,7},{7,0},{8,9},{9,10},{10,1... | collective-permute-start | bytes 1572872 | tf_op jit(solution)/shard_map/ppermute | solution.py:41
  49.7 14.3 %collective-permute-start.15 = (bf16[4,256,256]{2,1,0:T(8,128)(2,1)S(1)}, bf16[4,256,256]{2,1,0:T(8,128)(2,1)S(1)}, u32[]{:S(2)}, u32[]{:S(2)}) collective-permute-start(bf16[4,256,256]{2,1,0:T(8,128)(2,1)S(1)} %collective-permute-done.11.rest_2_), channel_id=1, source_target_pairs={{0,7},{1,0},{2,1},{3,2},{4,3},{5,4},{6,5},{7,6},{8,15},{9,8},{10,9... | collective-permute-start | bytes 1572872 | tf_op jit(solution)/shard_map/ppermute | solution.py:41
  64.1 8.7 %collective-permute-start.17 = (bf16[4,256,256]{2,1,0:T(8,128)(2,1)S(1)}, bf16[4,256,256]{2,1,0:T(8,128)(2,1)S(1)}, u32[]{:S(2)}, u32[]{:S(2)}) collective-permute-start(bf16[4,256,256]{2,1,0:T(8,128)(2,1)S(1)} %broadcast_select_fusion), channel_id=1, source_target_pairs={{0,1},{1,2},{2,3},{3,4},{4,5},{5,6},{6,7},{7,0},{8,9},{9,10},{10,1... | collective-permute-start | bytes 1572872 | tf_op jit(solution)/shard_map/ppermute | solution.py:41
  66.5 9.3 %collective-permute-start.14 = (bf16[4,256,256]{2,1,0:T(8,128)(2,1)S(1)}, bf16[4,256,256]{2,1,0:T(8,128)(2,1)S(1)}, u32[]{:S(2)}, u32[]{:S(2)}) collective-permute-start(bf16[4,256,256]{2,1,0:T(8,128)(2,1)S(1)} %collective-permute-done.13.rest_0_), channel_id=1, source_target_pairs={{0,32},{1,33},{2,34},{3,35},{4,36},{5,37},{6,38},{7,39},{8,40},{9,... | collective-permute-start | bytes 1572872 | tf_op jit(solution)/shard_map/ppermute | solution.py:41
  66.5 9.3 %collective-permute-start.16 = (bf16[4,256,256]{2,1,0:T(8,128)(2,1)S(1)}, bf16[4,256,256]{2,1,0:T(8,128)(2,1)S(1)}, u32[]{:S(2)}, u32[]{:S(2)}) collective-permute-start(bf16[4,256,256]{2,1,0:T(8,128)(2,1)S(1)} %collective-permute-done.15.rest_2_), channel_id=1, source_target_pairs={{0,32},{1,33},{2,34},{3,35},{4,36},{5,37},{6,38},{7,39},{8,40},{9,... | collective-permute-start | bytes 1572872 | tf_op jit(solution)/shard_map/ppermute | solution.py:41
  72.8 7.9 %collective-permute-start.18 = (bf16[4,256,256]{2,1,0:T(8,128)(2,1)S(1)}, bf16[4,256,256]{2,1,0:T(8,128)(2,1)S(1)}, u32[]{:S(2)}, u32[]{:S(2)}) collective-permute-start(bf16[4,256,256]{2,1,0:T(8,128)(2,1)S(1)} %collective-permute-done.17.rest_0_), channel_id=1, source_target_pairs={{0,32},{1,33},{2,34},{3,35},{4,36},{5,37},{6,38},{7,39},{8,40},{9,... | collective-permute-start | bytes 1572872 | tf_op jit(solution)/shard_map/ppermute | solution.py:41

commit v4 on v3

--- a/solution.py
+++ b/solution.py
@@ -134,16 +134,13 @@
 
 
 def first_kernel(
-    ids_ref, at_ref, got_ref, theirs_ref, q_ref, acc_ref, m_ref, count_ref, list_ref, keys, values
+    ids_ref, at_ref, got_ref, q_ref, acc_ref, m_ref, count_ref, list_ref, keys, values
 ):
     for s in range(8):
         at = pl.ds(s * 64, 64)
         keys[at, :] = got_ref[s, :, 768:896]
         values[at, 0:D] = got_ref[s, :, 896:1024]
-        at = pl.ds(512 + s * 64, 64)
-        keys[at, :] = theirs_ref[s, :, 0:D]
-        values[at, 0:D] = theirs_ref[s, :, D : 2 * D]
-    values[:, D:] = jnp.ones((1024, D), jnp.bfloat16)
+    values[:, D:] = jnp.ones((512, D), jnp.bfloat16)
     q_ref[NR * ROWS :, :] = jnp.zeros((ROWS, D), jnp.bfloat16)
     m_ref[NR * ROWS :, :] = jnp.zeros((ROWS, D), jnp.float32)
     acc_ref[NR * ROWS :, :] = jnp.zeros((ROWS, 2 * D), jnp.float32)
@@ -188,7 +185,7 @@
             p = jnp.concatenate(
                 [
                     jnp.exp2(far[i][:, j * D : (j + 1) * D] * COEF - m[i]).astype(jnp.bfloat16)
-                    for j in range(8)
+                    for j in range(4)
                 ],
                 axis=1,
             )
@@ -202,7 +199,7 @@
             acc_ref[at, :] = acc + jnp.dot(po, vo, preferred_element_type=jnp.float32)
 
 
-def first_call(ids, location, got, theirs):
+def first_call(ids, location, got):
     n = SLOTS * ROWS
     vmem = pl.BlockSpec(memory_space=pltpu.VMEM)
     smem = pl.BlockSpec(memory_space=pltpu.SMEM)
@@ -215,35 +212,32 @@
             jax.ShapeDtypeStruct((PLACES + 1,), jnp.int32),
             jax.ShapeDtypeStruct((PLACES + 1, NR), jnp.int32),
         ),
-        in_specs=[smem] * 2 + [vmem] * 2,
+        in_specs=[smem] * 2 + [vmem],
         out_specs=(vmem,) * 3 + (smem,) * 2,
         scratch_shapes=[
-            pltpu.VMEM((1024, D), jnp.bfloat16),
-            pltpu.VMEM((1024, 2 * D), jnp.bfloat16),
+            pltpu.VMEM((512, D), jnp.bfloat16),
+            pltpu.VMEM((512, 2 * D), jnp.bfloat16),
         ],
         compiler_params=pltpu.CompilerParams(vmem_limit_bytes=16 * 1024 * 1024),
         cost_estimate=pl.CostEstimate(
-            flops=8 * 2048 * 1088 * D, bytes_accessed=6 * 1024 * 1024, transcendentals=2048 * 1088
+            flops=8 * 2048 * 576 * D, bytes_accessed=6 * 1024 * 1024, transcendentals=2048 * 576
         ),
         name="prefix_and_own",
-    )(ids, location, got, theirs)
-
-
-def passage_kernel(rounds, n_pairs, last, spot_ref, count_ref, list_ref, q_ref, acc_in, m_in, *rest):
-    blocks = rest[: 2 * n_pairs]
-    if last:
-        out_ref, acc, m = rest[2 * n_pairs :]
-    else:
-        acc, m = rest[2 * n_pairs :]
-    acc[...] = acc_in[...]
-    m[...] = m_in[...]
+    )(ids, location, got)
+
+
+def passage_kernel(rounds, n_blocks, prefix, last, spot_ref, count_ref, list_ref, q_ref, *rest):
+    blocks = rest[2 : 2 + n_blocks]
+    acc, m = rest[2 + n_blocks : 4 + n_blocks]
     ones = jnp.ones((256, D), jnp.bfloat16)
-
+    if prefix:
+        run_prefix(blocks[-1], ones, q_ref, acc, m)
     for streams in rounds:
         run_streams(streams, blocks, ones, spot_ref, count_ref, list_ref, q_ref, acc, m)
     if last:
-
-        @pl.loop(0, NR)
+        out_ref = rest[4 + n_blocks]
+
+        @pl.loop(0, NR, unroll=4)
         def _(r):
             at = pl.ds(pl.multiple_of(r * ROWS, ROWS), ROWS)
             o = (acc[at, 0:D] / acc[at, D:]).astype(jnp.bfloat16)
@@ -253,6 +247,49 @@
                 ]
 
 
+def attend(rows, halves, ones, q_ref, acc, m):
+    at = [[pl.ds(pl.multiple_of(r * ROWS, ROWS), ROWS) for r in rows[s]] for s in range(2)]
+    sc, keep = [], []
+    for s in range(2):
+        q = jnp.concatenate([q_ref[a, :] for a in at[s]], axis=0)
+        sc.append([nt(q, h[:, 0:D]) for h in halves[s]])
+        keep.append([jnp.concatenate([h[:, D:], ones], axis=1) for h in halves[s]])
+    new, shrink = [], []
+    for s in range(2):
+        top = jnp.maximum(
+            jnp.max(sc[s][0], axis=1, keepdims=True), jnp.max(sc[s][1], axis=1, keepdims=True)
+        )
+        old = jnp.concatenate([m[a, :] for a in at[s]], axis=0)
+        new.append(jnp.maximum(old, top * COEF))
+        shrink.append(jnp.exp2(old - new[s]))
+        for k, a in enumerate(at[s]):
+            m[a, :] = new[s][k * ROWS : (k + 1) * ROWS]
+    mixed = []
+    for s in range(2):
+        mixed.append(0)
+        for h in range(2):
+            p = jnp.concatenate(
+                [
+                    jnp.exp2(sc[s][h][:, j * D : (j + 1) * D] * COEF - new[s]).astype(jnp.bfloat16)
+                    for j in range(2)
+                ],
+                axis=1,
+            )
+            mixed[s] = mixed[s] + jnp.dot(p, keep[s][h], preferred_element_type=jnp.float32)
+    for s in range(2):
+        for k, a in enumerate(at[s]):
+            part = slice(k * ROWS, (k + 1) * ROWS)
+            acc[a, 0:D] = acc[a, 0:D] * shrink[s][part] + mixed[s][part, 0:D]
+            acc[a, D:] = acc[a, D:] * shrink[s][part] + mixed[s][part, D:]
+
+
+def run_prefix(rows_ref, ones, q_ref, acc, m):
+    @pl.loop(0, NR // (2 * BATCH))
+    def _(b):
+        rows = [[(2 * b + s) * BATCH + k for k in range(BATCH)] for s in range(2)]
+        attend(rows, [[rows_ref.at[0], rows_ref.at[1]]] * 2, ones, q_ref, acc, m)
+
+
 def run_streams(streams, blocks, ones, spot_ref, count_ref, list_ref, q_ref, acc, m):
     def place_of(s, i):
         turn = any_turn(streams[s].base + i)
@@ -266,80 +303,46 @@
         return total
 
     def step(_, carry):
-        at, sc, keep = [], [], []
-        ahead = []
+        rows, halves, ahead = [], [], []
         for s, (i, b) in enumerate(carry):
             i_here = jnp.minimum(i, streams[s].count - 1)
             place = jnp.where(i < streams[s].count, place_of(s, i_here), PLACES)
             count = count_ref[place]
-            rows = [
-                jnp.where(b * BATCH + k < count, list_ref[place, b * BATCH + k], NR)
-                for k in range(BATCH)
-            ]
-            at.append([pl.ds(pl.multiple_of(r * ROWS, ROWS), ROWS) for r in rows])
+            rows.append(
+                [
+                    jnp.where(b * BATCH + k < count, list_ref[place, b * BATCH + k], NR)
+                    for k in range(BATCH)
+                ]
+            )
             full = (b + 1) * BATCH >= count
             ahead.append((i + full.astype(jnp.int32), jnp.where(full, 0, b + 1)))
-            q = jnp.concatenate([q_ref[a, :] for a in at[s]], axis=0)
             pair = streams[s].pair
-            here = [h.at[streams[s].base + i_here] for h in blocks[2 * pair : 2 * pair + 2]]
-            sc.append([nt(q, h[:, 0:D]) for h in here])
-            keep.append([jnp.concatenate([h[:, D:], ones], axis=1) for h in here])
-        new, shrink = [], []
-        for s in range(2):
-            top = jnp.maximum(
-                jnp.max(sc[s][0], axis=1, keepdims=True), jnp.max(sc[s][1], axis=1, keepdims=True)
-            )
-            old = jnp.concatenate([m[a, :] for a in at[s]], axis=0)
-            new.append(jnp.maximum(old, top * COEF))
-            shrink.append(jnp.exp2(old - new[s]))
-            for k, a in enumerate(at[s]):
-                m[a, :] = new[s][k * ROWS : (k + 1) * ROWS]
-        mixed = []
-        for s in range(2):
-            mixed.append(0)
-            for h in range(2):
-                p = jnp.concatenate(
-                    [
-                        jnp.exp2(sc[s][h][:, j * D : (j + 1) * D] * COEF - new[s]).astype(
-                            jnp.bfloat16
-                        )
-                        for j in range(2)
-                    ],
-                    axis=1,
-                )
-                mixed[s] = mixed[s] + jnp.dot(p, keep[s][h], preferred_element_type=jnp.float32)
-        for s in range(2):
-            for k, a in enumerate(at[s]):
-                part = slice(k * ROWS, (k + 1) * ROWS)
-                acc[a, 0:D] = acc[a, 0:D] * shrink[s][part] + mixed[s][part, 0:D]
-                acc[a, D:] = acc[a, D:] * shrink[s][part] + mixed[s][part, D:]
+            halves.append([h.at[streams[s].base + i_here] for h in blocks[2 * pair : 2 * pair + 2]])
+        attend(rows, halves, ones, q_ref, acc, m)
         return tuple(ahead)
 
     start = ((jnp.int32(0), jnp.int32(0)),) * 2
     lax.fori_loop(0, jnp.maximum(batches(0), batches(1)), step, start)
 
 
-def passage_call(spot, counts_of, lists, q, acc, m, rounds, pairs, last=False):
+def passage_call(spot, counts_of, lists, q, acc, m, rounds, pairs, prefix=None, last=False):
     n = SLOTS * ROWS
     total = sum(stream.count for streams in rounds for stream in streams)
-    state = (jax.ShapeDtypeStruct((n, 2 * D), jnp.float32), jax.ShapeDtypeStruct((n, D), jnp.float32))
-    scratch = []
+    blocks = [a for pair in pairs for a in pair] + ([] if prefix is None else [prefix])
+    out_shape = [
+        jax.ShapeDtypeStruct((n, 2 * D), jnp.float32),
+        jax.ShapeDtypeStruct((n, D), jnp.float32),
+    ]
     if last:
-        out_shape = (jax.ShapeDtypeStruct((NR * T, GROUP * D), jnp.bfloat16),)
-        scratch = [pltpu.VMEM((n, 2 * D), jnp.float32), pltpu.VMEM((n, D), jnp.float32)]
-        aliases = {}
-    else:
-        out_shape = state
-        aliases = {4: 0, 5: 1}
+        out_shape.append(jax.ShapeDtypeStruct((NR * T, GROUP * D), jnp.bfloat16))
     vmem = pl.BlockSpec(memory_space=pltpu.VMEM)
     smem = pl.BlockSpec(memory_space=pltpu.SMEM)
     return pl.pallas_call(
-        functools.partial(passage_kernel, rounds, len(pairs), last),
-        out_shape=out_shape,
-        in_specs=[smem] * 3 + [vmem] * (3 + 2 * len(pairs)),
+        functools.partial(passage_kernel, rounds, len(blocks), prefix is not None, last),
+        out_shape=tuple(out_shape),
+        in_specs=[smem] * 3 + [vmem] * (3 + len(blocks)),
         out_specs=(vmem,) * len(out_shape),
-        scratch_shapes=scratch,
-        input_output_aliases=aliases,
+        input_output_aliases={4: 0, 5: 1},
         compiler_params=pltpu.CompilerParams(vmem_limit_bytes=20 * 1024 * 1024),
         cost_estimate=pl.CostEstimate(
             flops=16 * total * 10 * ROWS * 512 * D,
@@ -347,7 +350,7 @@
             transcendentals=total * 10 * ROWS * 512,
         ),
         name="passages",
-    )(spot, counts_of, lists, q, acc, m, *[a for pair in pairs for a in pair])
+    )(spot, counts_of, lists, q, acc, m, *blocks)
 
 
 def per_device(
@@ -389,22 +392,22 @@
     one = [swap(up1), swap(down1)]
     got = after(got, one[0][1], one[1][1])
     here = swap(after(column, got))
-    theirs = send(got[:, :, 768:1024], other_core)
+    theirs = send(got[:, :, 768:1024].reshape(2, 256, 2 * D), other_core)
     chosen = got[:, :, 1024 : 1024 + TOPK].reshape(NR, T, TOPK)[:, 0].astype(jnp.int32)
-    q, acc, m, counts_of, lists = first_call(chosen, location, got, theirs)
+    q, acc, m, counts_of, lists = first_call(chosen, location, got)
 
     state = (spot, counts_of, lists, q)
     seen = (m, one[0][1], one[1][1])
     up3, down3 = send(after(up2, *seen), z_by(1)), send(after(down2, *seen), z_by(-1))
     two = [swap(after(up2, m)), swap(after(down2, m))]
-    acc, m = passage_call(*state, acc, m, (split(0, 0), both(1, 1)), [here] + one)
+    acc, m = passage_call(*state, acc, m, (split(0, 0), both(1, 1)), [here] + one, theirs)
     up3, down3 = after(up3, m), after(down3, m)
     four = send(jnp.where(c == 0, up3, down3), lambda x, c, y, z: (x, c, y, z + 1 - 2 * c))
     three = [swap(up3), swap(down3)]
     acc, m = passage_call(*state, acc, m, (both(0, 2),), two)
+    acc, m = passage_call(*state, acc, m, (both(0, 3),), three)
     four = after(four, m)
-    acc, m = passage_call(*state, acc, m, (both(0, 3),), three)
-    (out,) = passage_call(*state, acc, m, (split(0, 4),), [swap(four)], True)
+    _, _, out = passage_call(*state, acc, m, (split(0, 4),), [swap(four)], last=True)
 
     out = out.reshape(KV, 64, GROUP * D)
     home = lax.all_to_all(out, AXES, 0, 0, tiled=True, axis_index_groups=head_groups())

time: 99.3 us -> 98.7 us (level)
  waiting for transfers between devices: 18.5 us -> 17.2 us
  Pallas kernels: 29.4 us -> 30.6 us
    pallas_call x4, Pallas kernels: 22.1 us -> 24.2 us  [passage_call(): pl.pallas_call(functools.partial(passage_kernel, rounds, len(blocks), pre...]
    ppermute x19, waiting for transfers between devices: 13.1 us -> 11.9 us  [send(): return lax.ppermute(block, AXES, moves(to))]
  transfers between devices with their start and end apart: 20 -> 20, of which waited for: 7 -> 9; matrix products, arithmetic and copies ran while one was open for 1% -> 0% of each run, Pallas kernels for 26% -> 28%
where the time goes in v4:
time: 98.7 us; the launch traced here: 98.5 us
  starting transfers between devices  32.8 us (33%)
  Pallas kernels  30.6 us (31%)
  waiting for transfers between devices  17.2 us (17%)
  blocking collectives  14.7 us (15%)
  local copies, waits for them, and re-layouts  2.59 us (3%)
    ppermute x19, starting transfers between devices, send(): return lax.ppermute(block, AXES, moves(to))  27.1 us
    pallas_call x4, Pallas kernels, passage_call(): pl.pallas_call(functools.partial(passage_kernel, rounds, len(blocks), pre...  24.2 us
    all_to_all x1, blocking collectives, per_device(): lax.all_to_all(out, AXES, 0, 0, tiled=True, axis_index_groups=head_groups())  14.7 us
    ppermute x19, waiting for transfers between devices, send(): return lax.ppermute(block, AXES, moves(to))  11.9 us
    all_to_all x1, starting transfers between devices, per_device(): lax.all_to_all(after(parcel, column), AXES, 0, 0, tiled=True, axis_index_...  5.71 us
    all_to_all x1, waiting for transfers between devices, per_device(): lax.all_to_all(after(parcel, column), AXES, 0, 0, tiled=True, axis_index_...  5.37 us
    pallas_call x1, Pallas kernels, first_call(): pl.pallas_call(first_kernel, out_shape=(jax.ShapeDtypeStruct((n, D), jnp....  4.44 us
  transfers between devices with their start and end apart: 20, of which 9 were waited for; matrix products, arithmetic and copies ran while one was open for 0% of the time, Pallas kernels for 28%

profile of v4, /device:TPU:1, one launch (start us, length us, event | category | flops | bytes accessed | tf_op | source)
XLA Modules:
  0.0 98.5 jit_solution(17768936780739132512)
XLA Ops:
  0.1 1.1 %dynamic-slice_bitcast_fusion = (bf16[256,256]{1,0:T(8,128)(2,1)S(1)}, bf16[256,256]{1,0:T(8,128)(2,1)S(1)}) fusion(bf16[1,512,1024]{2,1,0:T(8,128)(2,1)} %param.15, s32[]{:T(128)S(6)} %select_n.40, s32[]{:T(128)S(6)} %select_n.41, bf16[1,512,1024]{2,1,0:T(8,128)(2,1)} %param.14), kind=kLoop, calls=%fused_computation.5 | loop fusion | bytes 524296 | tf_op jit(solution)/shard_map/dynamic_slice | solution.py:373
  1.3 3.8 %collective-permute-start.2 = (bf16[256,256]{1,0:T(8,128)(2,1)S(1)}, bf16[256,256]{1,0:T(8,128)(2,1)S(1)}, u32[]{:S(2)}, u32[]{:S(2)}) collective-permute-start(bf16[256,256]{1,0:T(8,128)(2,1)S(1)} %get-tuple-element.53), channel_id=1, source_target_pairs={{0,16},{1,17},{2,18},{3,19},{4,20},{5,21},{6,22},{7,23},{8,24},{9,... | collective-permute-start | bytes 393224 | tf_op jit(solution)/shard_map/ppermute | solution.py:41
  5.1 0.8 collective-permute-start.1
  5.9 0.7 collective-permute-start
  6.7 1.9 %parcel.1 = bf16[8,64,1152]{2,1,0:T(8,128)(2,1)} custom-call(s32[1]{0:T(128)} %bitcast.4.low_ref, bf16[64,4096]{1,0:T(8,128)(2,1)S(1)} %bitcast.32, bf16[64,1024]{1,0:T(8,128)(2,1)S(1)} %bitcast.33, bf16[64,1024]{1,0:T(8,128)(2,1)S(1)} %bitcast.34, bf16[128,1024]{1,0:T(8,128)(2,1)S(1)} %copy-done.1, bf16[128,1024]{1,0:T(8,128)(2,1)S(1)} %copy-done.2, ...), custom_call_target="tpu_custom_call" | custom-call | bytes 6291456 | tf_op jit(solution)/shard_map/parcel/pallas_call | solution.py:114
  8.7 2.6 %collective-permute-done.1 = bf16[256,256]{1,0:T(8,128)(2,1)S(1)} collective-permute-done((bf16[256,256]{1,0:T(8,128)(2,1)S(1)}, bf16[256,256]{1,0:T(8,128)(2,1)S(1)}, u32[]{:S(2)}, u32[]{:S(2)}) %collective-permute-start.1) | collective-permute-done | bytes 131104 | tf_op jit(solution)/shard_map/ppermute | solution.py:41
  11.2 1.9 %collective-permute-done = bf16[256,256]{1,0:T(8,128)(2,1)S(1)} collective-permute-done((bf16[256,256]{1,0:T(8,128)(2,1)S(1)}, bf16[256,256]{1,0:T(8,128)(2,1)S(1)}, u32[]{:S(2)}, u32[]{:S(2)}) %collective-permute-start) | collective-permute-done | bytes 131104 | tf_op jit(solution)/shard_map/ppermute | solution.py:41
  13.2 3.8 %collective-permute-start.5 = (bf16[4,256,256]{2,1,0:T(8,128)(2,1)S(1)}, bf16[4,256,256]{2,1,0:T(8,128)(2,1)S(1)}, u32[]{:S(2)}, u32[]{:S(2)}) collective-permute-start(bf16[4,256,256]{2,1,0:T(8,128)(2,1)S(1)} %pad_maximum_fusion.rest_2_), channel_id=1, source_target_pairs={{0,7},{1,0},{2,1},{3,2},{4,3},{5,4},{6,5},{7,6},{8,15},{9,8},{10,9... | collective-permute-start | bytes 1572872 | tf_op jit(solution)/shard_map/ppermute | solution.py:41
  17.0 5.7 %all-to-all-start = ((bf16[8,64,1152]{2,1,0:T(8,128)(2,1)}), bf16[8,64,1152]{2,1,0:T(8,128)(2,1)S(1)}, u32[]{:S(2)}, u32[]{:S(2)}) async-start(bf16[8,64,1152]{2,1,0:T(8,128)(2,1)} %parcel.1), calls=%async_computation | async-start | bytes 2359296 | tf_op jit(solution)/shard_map/all_to_all | solution.py:389
  22.7 3.4 %collective-permute-done.5.rest_6_ = bf16[4,256,256]{2,1,0:T(8,128)(2,1)S(1)} collective-permute-done((bf16[4,256,256]{2,1,0:T(8,128)(2,1)S(1)}, bf16[4,256,256]{2,1,0:T(8,128)(2,1)S(1)}, u32[]{:S(2)}, u32[]{:S(2)}) %collective-permute-start.5) | collective-permute-done | bytes 524320 | tf_op jit(solution)/shard_map/ppermute | solution.py:41
  26.1 3.0 %collective-permute-start.6 = (bf16[4,256,256]{2,1,0:T(8,128)(2,1)S(1)}, bf16[4,256,256]{2,1,0:T(8,128)(2,1)}, u32[]{:S(2)}, u32[]{:S(2)}) collective-permute-start(bf16[4,256,256]{2,1,0:T(8,128)(2,1)S(1)} %collective-permute-done.5.rest_6_), channel_id=1, source_target_pairs={{0,32},{1,33},{2,34},{3,35},{4,36},{5,37},{6,38},{7,39},{8,40},{9,... | collective-permute-start | bytes 1572872 | tf_op jit(solution)/shard_map/ppermute | solution.py:41
  29.4 3.3 %collective-permute-start.4 = (bf16[4,256,256]{2,1,0:T(8,128)(2,1)}, bf16[4,256,256]{2,1,0:T(8,128)(2,1)}, u32[]{:S(2)}, u32[]{:S(2)}) collective-permute-start(bf16[4,256,256]{2,1,0:T(8,128)(2,1)} %collective-permute-done.3.rest_4_), channel_id=1, source_target_pairs={{0,32},{1,33},{2,34},{3,35},{4,36},{5,37},{6,38},{7,39},{8,40},{9,... | collective-permute-start | bytes 1572872 | tf_op jit(solution)/shard_map/ppermute | solution.py:41
  32.6 1.5 %collective-permute-start.9 = (bf16[4,256,256]{2,1,0:T(8,128)(2,1)}, bf16[4,256,256]{2,1,0:T(8,128)(2,1)S(1)}, u32[]{:S(2)}, u32[]{:S(2)}) collective-permute-start(bf16[4,256,256]{2,1,0:T(8,128)(2,1)} %collective-permute-done.3.rest_4_), channel_id=1, source_target_pairs={{0,1},{1,2},{2,3},{3,4},{4,5},{5,6},{6,7},{7,0},{8,9},{9,10},{10,1... | collective-permute-start | bytes 1572872 | tf_op jit(solution)/shard_map/ppermute | solution.py:41
  34.1 5.4 %all-to-all-done.got_ref = bf16[8,64,1152]{2,1,0:T(8,128)(2,1)S(1)} async-done(((bf16[8,64,1152]{2,1,0:T(8,128)(2,1)}), bf16[8,64,1152]{2,1,0:T(8,128)(2,1)S(1)}, u32[]{:S(2)}, u32[]{:S(2)}) %all-to-all-start) | async-done | bytes 1179680 | tf_op jit(solution)/shard_map/all_to_all | solution.py:389
  39.5 1.8 %collective-permute-start.7 = (bf16[4,256,256]{2,1,0:T(8,128)(2,1)S(1)}, bf16[4,256,256]{2,1,0:T(8,128)(2,1)}, u32[]{:S(2)}, u32[]{:S(2)}) collective-permute-start(bf16[4,256,256]{2,1,0:T(8,128)(2,1)S(1)} %pad_maximum_fusion.rest_2_), channel_id=1, source_target_pairs={{0,32},{1,33},{2,34},{3,35},{4,36},{5,37},{6,38},{7,39},{8,40},{9,... | collective-permute-start | bytes 1572872 | tf_op jit(solution)/shard_map/ppermute | solution.py:41
  41.5 4.4 %prefix_and_own.1 = (bf16[2112,128]{1,0:T(8,128)(2,1)S(1)}, f32[2112,256]{1,0:T(8,128)S(1)}, f32[2112,128]{1,0:T(8,128)S(1)}, s32[33]{0:T(128)S(1)}, s32[33,32]{1,0:T(8,128)S(1)}) custom-call(s32[32,8]{1,0:T(8,128)S(1)} %fusion.ids_ref, s32[32]{0:T(128)S(1)} %copy-done.5, bf16[8,64,1152]{2,1,0:T(8,128)(2,1)S(1)} %all-to-all-done.got_ref), custom_call_target="tpu_custom_call" | custom-call | flops 1207959552 | bytes 6291456 | tf_op jit(solution)/shard_map/prefix_and_own/pallas_call | solution.py:206
  46.0 0.2 collective-permute-done.11.rest_4_
  46.2 0.7 collective-permute-done.9.rest_2_
  46.8 1.6 %collective-permute-start.10 = (bf16[4,256,256]{2,1,0:T(8,128)(2,1)S(1)}, bf16[4,256,256]{2,1,0:T(8,128)(2,1)S(1)}, u32[]{:S(2)}, u32[]{:S(2)}) collective-permute-start(bf16[4,256,256]{2,1,0:T(8,128)(2,1)S(1)} %collective-permute-done.9.rest_2_), channel_id=1, source_target_pairs={{0,32},{1,33},{2,34},{3,35},{4,36},{5,37},{6,38},{7,39},{8,40},{9,... | collective-permute-start | bytes 1572872 | tf_op jit(solution)/shard_map/ppermute | solution.py:41
  48.4 0.3 collective-permute-start.13
  48.7 2.4 %collective-permute-start.15 = (bf16[4,256,256]{2,1,0:T(8,128)(2,1)S(1)}, bf16[4,256,256]{2,1,0:T(8,128)(2,1)S(1)}, u32[]{:S(2)}, u32[]{:S(2)}) collective-permute-start(bf16[4,256,256]{2,1,0:T(8,128)(2,1)S(1)} %collective-permute-done.11.rest_4_), channel_id=1, source_target_pairs={{0,7},{1,0},{2,1},{3,2},{4,3},{5,4},{6,5},{7,6},{8,15},{9,8},{10,9... | collective-permute-start | bytes 1572872 | tf_op jit(solution)/shard_map/ppermute | solution.py:41
  51.1 10.5 %passages.4 = (f32[2112,256]{1,0:T(8,128)S(1)}, f32[2112,128]{1,0:T(8,128)S(1)}) custom-call(s32[2]{0:T(128)S(1)} %pad_add_fusion.spot_ref, s32[33]{0:T(128)S(1)} %get-tuple-element.33.count_ref, s32[33,32]{1,0:T(8,128)S(1)} %get-tuple-element.34.list_ref, ...), custom_call_target="tpu_custom_call", output_to_operand_aliasing={{0}: (4, {}), {1}: (5, {})} | custom-call | flops 8053063680 | bytes 6291456 | tf_op jit(solution)/shard_map/passages/pallas_call | solution.py:340
  61.6 0.9 collective-permute-done.13.rest_2_
  62.6 1.4 %collective-permute-start.14 = (bf16[4,256,256]{2,1,0:T(8,128)(2,1)S(1)}, bf16[4,256,256]{2,1,0:T(8,128)(2,1)S(1)}, u32[]{:S(2)}, u32[]{:S(2)}) collective-permute-start(bf16[4,256,256]{2,1,0:T(8,128)(2,1)S(1)} %collective-permute-done.13.rest_2_), channel_id=1, source_target_pairs={{0,32},{1,33},{2,34},{3,35},{4,36},{5,37},{6,38},{7,39},{8,40},{9,... | collective-permute-start | bytes 1572872 | tf_op jit(solution)/shard_map/ppermute | solution.py:41
  64.0 2.7 %collective-permute-start.17 = (bf16[4,256,256]{2,1,0:T(8,128)(2,1)S(1)}, bf16[4,256,256]{2,1,0:T(8,128)(2,1)S(1)}, u32[]{:S(2)}, u32[]{:S(2)}) collective-permute-start(bf16[4,256,256]{2,1,0:T(8,128)(2,1)S(1)} %broadcast_select_fusion), channel_id=1, source_target_pairs={{0,1},{1,2},{2,3},{3,4},{4,5},{5,6},{6,7},{7,0},{8,9},{9,10},{10,1... | collective-permute-start | bytes 1572872 | tf_op jit(solution)/shard_map/ppermute | solution.py:41
  66.8 4.5 %passages.5 = (f32[2112,256]{1,0:T(8,128)S(1)}, f32[2112,128]{1,0:T(8,128)S(1)}) custom-call(s32[2]{0:T(128)S(1)} %pad_add_fusion.spot_ref, s32[33]{0:T(128)S(1)} %get-tuple-element.33.count_ref, s32[33,32]{1,0:T(8,128)S(1)} %get-tuple-element.34.list_ref, ...), custom_call_target="tpu_custom_call", output_to_operand_aliasing={{0}: (4, {}), {1}: (5, {})} | custom-call | flops 5368709120 | bytes 6291456 | tf_op jit(solution)/shard_map/passages/pallas_call | solution.py:340
  71.3 6.3 %passages.6 = (f32[2112,256]{1,0:T(8,128)S(1)}, f32[2112,128]{1,0:T(8,128)S(1)}) custom-call(s32[2]{0:T(128)S(1)} %pad_add_fusion.spot_ref, s32[33]{0:T(128)S(1)} %get-tuple-element.33.count_ref, s32[33,32]{1,0:T(8,128)S(1)} %get-tuple-element.34.list_ref, ...), custom_call_target="tpu_custom_call", output_to_operand_aliasing={{0}: (4, {}), {1}: (5, {})} | custom-call | flops 5368709120 | bytes 6291456 | tf_op jit(solution)/shard_map/passages/pallas_call | solution.py:340
  77.7 1.9 %collective-permute-done.18.rest_3_ = bf16[4,256,256]{2,1,0:T(8,128)(2,1)S(1)} collective-permute-done((bf16[4,256,256]{2,1,0:T(8,128)(2,1)S(1)}, bf16[4,256,256]{2,1,0:T(8,128)(2,1)S(1)}, u32[]{:S(2)}, u32[]{:S(2)}) %collective-permute-start.18) | collective-permute-done | bytes 524320 | tf_op jit(solution)/shard_map/ppermute | solution.py:41
  79.5 2.9 %passages.7 = (f32[2112,256]{1,0:T(8,128)S(1)}, f32[2112,128]{1,0:T(8,128)S(1)}, bf16[512,512]{1,0:T(8,128)(2,1)S(1)}) custom-call(s32[2]{0:T(128)S(1)} %pad_add_fusion.spot_ref, s32[33]{0:T(128)S(1)} %get-tuple-element.33.count_ref, s32[33,32]{1,0:T(8,128)S(1)} %get-tuple-element.34.list_ref, ...), custom_call_target="tpu_custom_call", output_to_operand_aliasing={{0}: (4, {}), {1}: (5, {})} | custom-call | flops 2684354560 | bytes 6291456 | tf_op jit(solution)/shard_map/passages/pallas_call | solution.py:340
  82.5 14.7 %all_to_all.10 = bf16[8,64,512]{2,1,0:T(8,128)(2,1)S(1)} all-to-all(bf16[8,64,512]{2,1,0:T(8,128)(2,1)S(1)} %bitcast.31), channel_id=1, replica_groups={{0,8,64,72,128,136,192,200},{1,9,65,73,129,137,193,201},{2,10,66,74,130..., dimensions={0} | all-to-all | bytes 1048576 | tf_op jit(solution)/shard_map/all_to_all | solution.py:413
  97.2 0.3 copy.19
  97.5 1.0 %reshape.95 = bf16[4,16,4096]{2,1,0:T(8,128)(2,1)} reshape(bf16[64,8,512]{2,1,0:T(8,128)(2,1)S(1)} %copy.19) | data formatting | bytes 1048576 | tf_op jit(solution)/shard_map/reshape | solution.py:414
  (46 shorter events, 1.0 us)
Async XLA Ops:
  0.0 6.6 %copy-start.6 = (s32[4,8]{1,0:T(4,128)S(1)}, s32[4,8]{1,0:T(4,128)}, u32[]{:S(2)}) copy-start(s32[4,8]{1,0:T(4,128)} %param.16) | copy-start | bytes 388
  0.0 6.6 %copy-start.2 = (bf16[128,1024]{1,0:T(8,128)(2,1)S(1)}, bf16[128,1024]{1,0:T(8,128)(2,1)}, u32[]{:S(2)}) copy-start(bf16[128,1024]{1,0:T(8,128)(2,1)} %pv_hbm.1) | copy-start | bytes 786436
  0.0 6.6 %copy-start.1 = (bf16[128,1024]{1,0:T(8,128)(2,1)S(1)}, bf16[128,1024]{1,0:T(8,128)(2,1)}, u32[]{:S(2)}) copy-start(bf16[128,1024]{1,0:T(8,128)(2,1)} %pk_hbm.1) | copy-start | bytes 786436
  0.0 6.6 %copy-start.4 = (bf16[4,16,1024]{2,1,0:T(8,128)(2,1)S(1)}, bf16[4,16,1024]{2,1,0:T(8,128)(2,1)}, u32[]{:S(2)}) copy-start(bf16[4,16,1024]{2,1,0:T(8,128)(2,1)} %param.11) | copy-start | bytes 393220
  0.0 6.6 %copy-start.3 = (bf16[4,16,1024]{2,1,0:T(8,128)(2,1)S(1)}, bf16[4,16,1024]{2,1,0:T(8,128)(2,1)}, u32[]{:S(2)}) copy-start(bf16[4,16,1024]{2,1,0:T(8,128)(2,1)} %param.10) | copy-start | bytes 393220
  0.0 6.6 %copy-start = (bf16[4,16,4096]{2,1,0:T(8,128)(2,1)S(1)}, bf16[4,16,4096]{2,1,0:T(8,128)(2,1)}, u32[]{:S(2)}) copy-start(bf16[4,16,4096]{2,1,0:T(8,128)(2,1)} %param.9) | copy-start | bytes 1572868
  1.3 7.4 %collective-permute-start.2 = (bf16[256,256]{1,0:T(8,128)(2,1)S(1)}, bf16[256,256]{1,0:T(8,128)(2,1)S(1)}, u32[]{:S(2)}, u32[]{:S(2)}) collective-permute-start(bf16[256,256]{1,0:T(8,128)(2,1)S(1)} %get-tuple-element.53), channel_id=1, source_target_pairs={{0,16},{1,17},{2,18},{3,19},{4,20},{5,21},{6,22},{7,23},{8,24},{9,... | collective-permute-start | bytes 393224 | tf_op jit(solution)/shard_map/ppermute | solution.py:41
  5.1 6.1 %collective-permute-start.1 = (bf16[256,256]{1,0:T(8,128)(2,1)S(1)}, bf16[256,256]{1,0:T(8,128)(2,1)S(1)}, u32[]{:S(2)}, u32[]{:S(2)}) collective-permute-start(bf16[256,256]{1,0:T(8,128)(2,1)S(1)} %get-tuple-element.54), channel_id=1, source_target_pairs={{0,24},{1,25},{2,26},{3,27},{4,28},{5,29},{6,30},{7,31},{8,0},{9,1... | collective-permute-start | bytes 393224 | tf_op jit(solution)/shard_map/ppermute | solution.py:41
  5.9 7.2 %collective-permute-start = (bf16[256,256]{1,0:T(8,128)(2,1)S(1)}, bf16[256,256]{1,0:T(8,128)(2,1)S(1)}, u32[]{:S(2)}, u32[]{:S(2)}) collective-permute-start(bf16[256,256]{1,0:T(8,128)(2,1)S(1)} %get-tuple-element.54), channel_id=1, source_target_pairs={{0,8},{1,9},{2,10},{3,11},{4,12},{5,13},{6,14},{7,15},{8,16},{9,17... | collective-permute-start | bytes 393224 | tf_op jit(solution)/shard_map/ppermute | solution.py:41
  13.2 28.3 %copy-start.5 = (s32[32]{0:T(128)S(1)}, s32[32]{0:T(128)}, u32[]{:S(2)}) copy-start(s32[32]{0:T(128)} %at_ref.1) | copy-start | bytes 388
  13.2 12.9 %collective-permute-start.5 = (bf16[4,256,256]{2,1,0:T(8,128)(2,1)S(1)}, bf16[4,256,256]{2,1,0:T(8,128)(2,1)S(1)}, u32[]{:S(2)}, u32[]{:S(2)}) collective-permute-start(bf16[4,256,256]{2,1,0:T(8,128)(2,1)S(1)} %pad_maximum_fusion.rest_2_), channel_id=1, source_target_pairs={{0,7},{1,0},{2,1},{3,2},{4,3},{5,4},{6,5},{7,6},{8,15},{9,8},{10,9... | collective-permute-start | bytes 1572872 | tf_op jit(solution)/shard_map/ppermute | solution.py:41
  17.0 12.4 %collective-permute-start.3 = (bf16[4,256,256]{2,1,0:T(8,128)(2,1)S(1)}, bf16[4,256,256]{2,1,0:T(8,128)(2,1)}, u32[]{:S(2)}, u32[]{:S(2)}) collective-permute-start(bf16[4,256,256]{2,1,0:T(8,128)(2,1)S(1)} %pad_maximum_fusion.rest_2_), channel_id=1, source_target_pairs={{0,1},{1,2},{2,3},{3,4},{4,5},{5,6},{6,7},{7,0},{8,9},{9,10},{10,1... | collective-permute-start | bytes 1572872 | tf_op jit(solution)/shard_map/ppermute | solution.py:41
  17.0 22.5 %all-to-all-start = ((bf16[8,64,1152]{2,1,0:T(8,128)(2,1)}), bf16[8,64,1152]{2,1,0:T(8,128)(2,1)S(1)}, u32[]{:S(2)}, u32[]{:S(2)}) async-start(bf16[8,64,1152]{2,1,0:T(8,128)(2,1)} %parcel.1), calls=%async_computation | async-start | bytes 2359296 | tf_op jit(solution)/shard_map/all_to_all | solution.py:389
  26.1 13.4 %collective-permute-start.6 = (bf16[4,256,256]{2,1,0:T(8,128)(2,1)S(1)}, bf16[4,256,256]{2,1,0:T(8,128)(2,1)}, u32[]{:S(2)}, u32[]{:S(2)}) collective-permute-start(bf16[4,256,256]{2,1,0:T(8,128)(2,1)S(1)} %collective-permute-done.5.rest_6_), channel_id=1, source_target_pairs={{0,32},{1,33},{2,34},{3,35},{4,36},{5,37},{6,38},{7,39},{8,40},{9,... | collective-permute-start | bytes 1572872 | tf_op jit(solution)/shard_map/ppermute | solution.py:41
  29.4 10.1 %collective-permute-start.4 = (bf16[4,256,256]{2,1,0:T(8,128)(2,1)}, bf16[4,256,256]{2,1,0:T(8,128)(2,1)}, u32[]{:S(2)}, u32[]{:S(2)}) collective-permute-start(bf16[4,256,256]{2,1,0:T(8,128)(2,1)} %collective-permute-done.3.rest_4_), channel_id=1, source_target_pairs={{0,32},{1,33},{2,34},{3,35},{4,36},{5,37},{6,38},{7,39},{8,40},{9,... | collective-permute-start | bytes 1572872 | tf_op jit(solution)/shard_map/ppermute | solution.py:41
  32.6 13.6 %collective-permute-start.11 = (bf16[4,256,256]{2,1,0:T(8,128)(2,1)S(1)}, bf16[4,256,256]{2,1,0:T(8,128)(2,1)S(1)}, u32[]{:S(2)}, u32[]{:S(2)}) collective-permute-start(bf16[4,256,256]{2,1,0:T(8,128)(2,1)S(1)} %collective-permute-done.5.rest_6_), channel_id=1, source_target_pairs={{0,7},{1,0},{2,1},{3,2},{4,3},{5,4},{6,5},{7,6},{8,15},{9,8},{10,9... | collective-permute-start | bytes 1572872 | tf_op jit(solution)/shard_map/ppermute | solution.py:41
  32.6 14.2 %collective-permute-start.9 = (bf16[4,256,256]{2,1,0:T(8,128)(2,1)}, bf16[4,256,256]{2,1,0:T(8,128)(2,1)S(1)}, u32[]{:S(2)}, u32[]{:S(2)}) collective-permute-start(bf16[4,256,256]{2,1,0:T(8,128)(2,1)} %collective-permute-done.3.rest_4_), channel_id=1, source_target_pairs={{0,1},{1,2},{2,3},{3,4},{4,5},{5,6},{6,7},{7,0},{8,9},{9,10},{10,1... | collective-permute-start | bytes 1572872 | tf_op jit(solution)/shard_map/ppermute | solution.py:41
  39.5 11.6 %collective-permute-start.7 = (bf16[4,256,256]{2,1,0:T(8,128)(2,1)S(1)}, bf16[4,256,256]{2,1,0:T(8,128)(2,1)}, u32[]{:S(2)}, u32[]{:S(2)}) collective-permute-start(bf16[4,256,256]{2,1,0:T(8,128)(2,1)S(1)} %pad_maximum_fusion.rest_2_), channel_id=1, source_target_pairs={{0,32},{1,33},{2,34},{3,35},{4,36},{5,37},{6,38},{7,39},{8,40},{9,... | collective-permute-start | bytes 1572872 | tf_op jit(solution)/shard_map/ppermute | solution.py:41
  41.4 7.3 %collective-permute-start.8 = (bf16[2,256,256]{2,1,0:T(8,128)(2,1)S(1)}, bf16[2,256,256]{2,1,0:T(8,128)(2,1)S(1)}, u32[]{:S(2)}, u32[]{:S(2)}) collective-permute-start(bf16[2,256,256]{2,1,0:T(8,128)(2,1)S(1)} %bitcast.37), channel_id=1, source_target_pairs={{0,32},{1,33},{2,34},{3,35},{4,36},{5,37},{6,38},{7,39},{8,40},{9,... | collective-permute-start | bytes 786440 | tf_op jit(solution)/shard_map/ppermute | solution.py:41
  46.8 19.9 %collective-permute-start.10 = (bf16[4,256,256]{2,1,0:T(8,128)(2,1)S(1)}, bf16[4,256,256]{2,1,0:T(8,128)(2,1)S(1)}, u32[]{:S(2)}, u32[]{:S(2)}) collective-permute-start(bf16[4,256,256]{2,1,0:T(8,128)(2,1)S(1)} %collective-permute-done.9.rest_2_), channel_id=1, source_target_pairs={{0,32},{1,33},{2,34},{3,35},{4,36},{5,37},{6,38},{7,39},{8,40},{9,... | collective-permute-start | bytes 1572872 | tf_op jit(solution)/shard_map/ppermute | solution.py:41
  48.4 18.4 %collective-permute-start.12 = (bf16[4,256,256]{2,1,0:T(8,128)(2,1)S(1)}, bf16[4,256,256]{2,1,0:T(8,128)(2,1)S(1)}, u32[]{:S(2)}, u32[]{:S(2)}) collective-permute-start(bf16[4,256,256]{2,1,0:T(8,128)(2,1)S(1)} %collective-permute-done.11.rest_4_), channel_id=1, source_target_pairs={{0,32},{1,33},{2,34},{3,35},{4,36},{5,37},{6,38},{7,39},{8,40},{9,... | collective-permute-start | bytes 1572872 | tf_op jit(solution)/shard_map/ppermute | solution.py:41
  48.4 14.2 %collective-permute-start.13 = (bf16[4,256,256]{2,1,0:T(8,128)(2,1)S(1)}, bf16[4,256,256]{2,1,0:T(8,128)(2,1)S(1)}, u32[]{:S(2)}, u32[]{:S(2)}) collective-permute-start(bf16[4,256,256]{2,1,0:T(8,128)(2,1)S(1)} %collective-permute-done.9.rest_2_), channel_id=1, source_target_pairs={{0,1},{1,2},{2,3},{3,4},{4,5},{5,6},{6,7},{7,0},{8,9},{9,10},{10,1... | collective-permute-start | bytes 1572872 | tf_op jit(solution)/shard_map/ppermute | solution.py:41
  48.7 15.3 %collective-permute-start.15 = (bf16[4,256,256]{2,1,0:T(8,128)(2,1)S(1)}, bf16[4,256,256]{2,1,0:T(8,128)(2,1)S(1)}, u32[]{:S(2)}, u32[]{:S(2)}) collective-permute-start(bf16[4,256,256]{2,1,0:T(8,128)(2,1)S(1)} %collective-permute-done.11.rest_4_), channel_id=1, source_target_pairs={{0,7},{1,0},{2,1},{3,2},{4,3},{5,4},{6,5},{7,6},{8,15},{9,8},{10,9... | collective-permute-start | bytes 1572872 | tf_op jit(solution)/shard_map/ppermute | solution.py:41
  62.6 8.7 %collective-permute-start.14 = (bf16[4,256,256]{2,1,0:T(8,128)(2,1)S(1)}, bf16[4,256,256]{2,1,0:T(8,128)(2,1)S(1)}, u32[]{:S(2)}, u32[]{:S(2)}) collective-permute-start(bf16[4,256,256]{2,1,0:T(8,128)(2,1)S(1)} %collective-permute-done.13.rest_2_), channel_id=1, source_target_pairs={{0,32},{1,33},{2,34},{3,35},{4,36},{5,37},{6,38},{7,39},{8,40},{9,... | collective-permute-start | bytes 1572872 | tf_op jit(solution)/shard_map/ppermute | solution.py:41
  64.0 7.3 %collective-permute-start.16 = (bf16[4,256,256]{2,1,0:T(8,128)(2,1)S(1)}, bf16[4,256,256]{2,1,0:T(8,128)(2,1)S(1)}, u32[]{:S(2)}, u32[]{:S(2)}) collective-permute-start(bf16[4,256,256]{2,1,0:T(8,128)(2,1)S(1)} %collective-permute-done.15.rest_4_), channel_id=1, source_target_pairs={{0,32},{1,33},{2,34},{3,35},{4,36},{5,37},{6,38},{7,39},{8,40},{9,... | collective-permute-start | bytes 1572872 | tf_op jit(solution)/shard_map/ppermute | solution.py:41
  64.0 13.5 %collective-permute-start.17 = (bf16[4,256,256]{2,1,0:T(8,128)(2,1)S(1)}, bf16[4,256,256]{2,1,0:T(8,128)(2,1)S(1)}, u32[]{:S(2)}, u32[]{:S(2)}) collective-permute-start(bf16[4,256,256]{2,1,0:T(8,128)(2,1)S(1)} %broadcast_select_fusion), channel_id=1, source_target_pairs={{0,1},{1,2},{2,3},{3,4},{4,5},{5,6},{6,7},{7,0},{8,9},{9,10},{10,1... | collective-permute-start | bytes 1572872 | tf_op jit(solution)/shard_map/ppermute | solution.py:41
  77.6 2.0 %collective-permute-start.18 = (bf16[4,256,256]{2,1,0:T(8,128)(2,1)S(1)}, bf16[4,256,256]{2,1,0:T(8,128)(2,1)S(1)}, u32[]{:S(2)}, u32[]{:S(2)}) collective-permute-start(bf16[4,256,256]{2,1,0:T(8,128)(2,1)S(1)} %collective-permute-done.17.rest_2_), channel_id=1, source_target_pairs={{0,32},{1,33},{2,34},{3,35},{4,36},{5,37},{6,38},{7,39},{8,40},{9,... | collective-permute-start | bytes 1572872 | tf_op jit(solution)/shard_map/ppermute | solution.py:41

commit v5 on v4

--- a/solution.py
+++ b/solution.py
@@ -50,7 +50,7 @@
 
 
 def z_by(step):
-    return lambda x, c, y, z: (x, c, y, z + step)
+    return lambda x, c, y, z: (x, c, y, z + step * (1 - 2 * c))
 
 
 def other_core(x, c, y, z):
@@ -293,7 +293,7 @@
 def run_streams(streams, blocks, ones, spot_ref, count_ref, list_ref, q_ref, acc, m):
     def place_of(s, i):
         turn = any_turn(streams[s].base + i)
-        up = spot_ref[1] + streams[s].offset
+        up = spot_ref[1] + streams[s].offset * spot_ref[2]
         return ((spot_ref[0] + turn) & (NY - 1)) * NZ + (up & (NZ - 1))
 
     def batches(s):
@@ -367,7 +367,7 @@
     grp, dev = lax.axis_index("grp"), lax.axis_index("dev")
     x, c, y, z = grp >> 1, grp & 1, dev >> 3, dev & 7
     low = y & 1
-    spot = jnp.stack([y, z])
+    spot = jnp.stack([y, z, 1 - 2 * c])
 
     def two_heads(cache):
         return lax.dynamic_slice(cache[0], (c * 256, x * 2 * D), (256, 2 * D))
@@ -386,10 +386,13 @@
     def swap(block):
         return block, send(block, other_core)
 
+    def cross(up, down):
+        return [(up, send(down, other_core)), (down, send(up, other_core))]
+
     got = lax.all_to_all(after(parcel, column), AXES, 0, 0, tiled=True, axis_index_groups=head_groups())
     up1, down1 = send(column, z_by(1)), send(column, z_by(-1))
     up2, down2 = send(up1, z_by(1)), send(down1, z_by(-1))
-    one = [swap(up1), swap(down1)]
+    one = cross(up1, down1)
     got = after(got, one[0][1], one[1][1])
     here = swap(after(column, got))
     theirs = send(got[:, :, 768:1024].reshape(2, 256, 2 * D), other_core)
@@ -399,11 +402,11 @@
     state = (spot, counts_of, lists, q)
     seen = (m, one[0][1], one[1][1])
     up3, down3 = send(after(up2, *seen), z_by(1)), send(after(down2, *seen), z_by(-1))
-    two = [swap(after(up2, m)), swap(after(down2, m))]
+    two = cross(after(up2, m), after(down2, m))
     acc, m = passage_call(*state, acc, m, (split(0, 0), both(1, 1)), [here] + one, theirs)
     up3, down3 = after(up3, m), after(down3, m)
-    four = send(jnp.where(c == 0, up3, down3), lambda x, c, y, z: (x, c, y, z + 1 - 2 * c))
-    three = [swap(up3), swap(down3)]
+    four = send(up3, z_by(1))
+    three = cross(up3, down3)
     acc, m = passage_call(*state, acc, m, (both(0, 2),), two)
     acc, m = passage_call(*state, acc, m, (both(0, 3),), three)
     four = after(four, m)

time: 98.7 us -> 95.7 us (0.970)
  blocking collectives: 14.7 us -> 12.6 us
  Pallas kernels: 30.6 us -> 29.6 us
    all_to_all x1, blocking collectives: 14.7 us -> 12.6 us  [per_device(): lax.all_to_all(out, AXES, 0, 0, tiled=True, axis_index_groups=head_groups())]
    pallas_call x4, Pallas kernels: 24.2 us -> 23.2 us  [passage_call(): pl.pallas_call(functools.partial(passage_kernel, rounds, len(blocks), pre...]
  transfers between devices with their start and end apart: 20 -> 20, of which waited for: 9 -> 7; matrix products, arithmetic and copies ran while one was open for 0% -> 0% of each run, Pallas kernels for 28% -> 27%
where the time goes in v5:
time: 95.7 us; the launch traced here: 95.5 us
  starting transfers between devices  33.4 us (35%)
  Pallas kernels  29.6 us (31%)
  waiting for transfers between devices  16.9 us (18%)
  blocking collectives  12.6 us (13%)
  local copies, waits for them, and re-layouts  2.59 us (3%)
    ppermute x19, starting transfers between devices, send(): return lax.ppermute(block, AXES, moves(to))  27.7 us
    pallas_call x4, Pallas kernels, passage_call(): pl.pallas_call(functools.partial(passage_kernel, rounds, len(blocks), pre...  23.2 us
    all_to_all x1, blocking collectives, per_device(): lax.all_to_all(out, AXES, 0, 0, tiled=True, axis_index_groups=head_groups())  12.6 us
    ppermute x19, waiting for transfers between devices, send(): return lax.ppermute(block, AXES, moves(to))  12 us
    all_to_all x1, starting transfers between devices, per_device(): lax.all_to_all(after(parcel, column), AXES, 0, 0, tiled=True, axis_index_...  5.71 us
    all_to_all x1, waiting for transfers between devices, per_device(): lax.all_to_all(after(parcel, column), AXES, 0, 0, tiled=True, axis_index_...  4.83 us
    pallas_call x1, Pallas kernels, first_call(): pl.pallas_call(first_kernel, out_shape=(jax.ShapeDtypeStruct((n, D), jnp....  4.44 us
    pallas_call x1, Pallas kernels, parcel_call(): pl.pallas_call(parcel_kernel, out_shape=jax.ShapeDtypeStruct((KV, 64, 115...  1.93 us
  transfers between devices with their start and end apart: 20, of which 7 were waited for; matrix products, arithmetic and copies ran while one was open for 0% of the time, Pallas kernels for 27%

profile of v5, /device:TPU:1, one launch (start us, length us, event | category | flops | bytes accessed | tf_op | source)
XLA Modules:
  0.0 95.5 jit_solution(7904659489681798792)
XLA Ops:
  0.1 1.1 %dynamic-slice_bitcast_fusion = (bf16[256,256]{1,0:T(8,128)(2,1)S(1)}, bf16[256,256]{1,0:T(8,128)(2,1)S(1)}) fusion(bf16[1,512,1024]{2,1,0:T(8,128)(2,1)} %param.15, s32[]{:T(128)S(6)} %select_n.32, s32[]{:T(128)S(6)} %select_n.33, bf16[1,512,1024]{2,1,0:T(8,128)(2,1)} %param.14), kind=kLoop, calls=%fused_computation.4 | loop fusion | bytes 524296 | tf_op jit(solution)/shard_map/dynamic_slice | solution.py:373
  1.3 3.8 %collective-permute-start.2 = (bf16[256,256]{1,0:T(8,128)(2,1)S(1)}, bf16[256,256]{1,0:T(8,128)(2,1)S(1)}, u32[]{:S(2)}, u32[]{:S(2)}) collective-permute-start(bf16[256,256]{1,0:T(8,128)(2,1)S(1)} %get-tuple-element.53), channel_id=1, source_target_pairs={{0,16},{1,17},{2,18},{3,19},{4,20},{5,21},{6,22},{7,23},{8,24},{9,... | collective-permute-start | bytes 393224 | tf_op jit(solution)/shard_map/ppermute | solution.py:41
  5.1 0.8 collective-permute-start.1
  5.9 0.7 collective-permute-start
  6.7 1.9 %parcel.1 = bf16[8,64,1152]{2,1,0:T(8,128)(2,1)} custom-call(s32[1]{0:T(128)} %bitcast.5.low_ref, bf16[64,4096]{1,0:T(8,128)(2,1)S(1)} %bitcast.33, bf16[64,1024]{1,0:T(8,128)(2,1)S(1)} %bitcast.34, bf16[64,1024]{1,0:T(8,128)(2,1)S(1)} %bitcast.35, bf16[128,1024]{1,0:T(8,128)(2,1)S(1)} %copy-done.1, bf16[128,1024]{1,0:T(8,128)(2,1)S(1)} %copy-done.2, ...), custom_call_target="tpu_custom_call" | custom-call | bytes 6291456 | tf_op jit(solution)/shard_map/parcel/pallas_call | solution.py:114
  8.7 2.6 %collective-permute-done.1 = bf16[256,256]{1,0:T(8,128)(2,1)S(1)} collective-permute-done((bf16[256,256]{1,0:T(8,128)(2,1)S(1)}, bf16[256,256]{1,0:T(8,128)(2,1)S(1)}, u32[]{:S(2)}, u32[]{:S(2)}) %collective-permute-start.1) | collective-permute-done | bytes 131104 | tf_op jit(solution)/shard_map/ppermute | solution.py:41
  11.2 1.9 %collective-permute-done = bf16[256,256]{1,0:T(8,128)(2,1)S(1)} collective-permute-done((bf16[256,256]{1,0:T(8,128)(2,1)S(1)}, bf16[256,256]{1,0:T(8,128)(2,1)S(1)}, u32[]{:S(2)}, u32[]{:S(2)}) %collective-permute-start) | collective-permute-done | bytes 131104 | tf_op jit(solution)/shard_map/ppermute | solution.py:41
  13.2 3.8 %collective-permute-start.5 = (bf16[4,256,256]{2,1,0:T(8,128)(2,1)S(1)}, bf16[4,256,256]{2,1,0:T(8,128)(2,1)S(1)}, u32[]{:S(2)}, u32[]{:S(2)}) collective-permute-start(bf16[4,256,256]{2,1,0:T(8,128)(2,1)S(1)} %pad_maximum_fusion.rest_2_), channel_id=1, source_target_pairs={{0,1},{1,2},{2,3},{3,4},{4,5},{5,6},{6,7},{7,0},{8,9},{9,10},{10,1... | collective-permute-start | bytes 1572872 | tf_op jit(solution)/shard_map/ppermute | solution.py:41
  17.0 5.7 %all-to-all-start = ((bf16[8,64,1152]{2,1,0:T(8,128)(2,1)}), bf16[8,64,1152]{2,1,0:T(8,128)(2,1)S(1)}, u32[]{:S(2)}, u32[]{:S(2)}) async-start(bf16[8,64,1152]{2,1,0:T(8,128)(2,1)} %parcel.1), calls=%async_computation | async-start | bytes 2359296 | tf_op jit(solution)/shard_map/all_to_all | solution.py:392
  22.7 3.3 %collective-permute-done.5.rest_4_ = bf16[4,256,256]{2,1,0:T(8,128)(2,1)S(1)} collective-permute-done((bf16[4,256,256]{2,1,0:T(8,128)(2,1)S(1)}, bf16[4,256,256]{2,1,0:T(8,128)(2,1)S(1)}, u32[]{:S(2)}, u32[]{:S(2)}) %collective-permute-start.5) | collective-permute-done | bytes 524320 | tf_op jit(solution)/shard_map/ppermute | solution.py:41
  26.0 5.8 %collective-permute-start.6 = (bf16[4,256,256]{2,1,0:T(8,128)(2,1)S(1)}, bf16[4,256,256]{2,1,0:T(8,128)(2,1)}, u32[]{:S(2)}, u32[]{:S(2)}) collective-permute-start(bf16[4,256,256]{2,1,0:T(8,128)(2,1)S(1)} %collective-permute-done.5.rest_4_), channel_id=1, source_target_pairs={{0,32},{1,33},{2,34},{3,35},{4,36},{5,37},{6,38},{7,39},{8,40},{9,... | collective-permute-start | bytes 1572872 | tf_op jit(solution)/shard_map/ppermute | solution.py:41
  31.8 2.7 %collective-permute-start.9 = (bf16[4,256,256]{2,1,0:T(8,128)(2,1)S(1)}, bf16[4,256,256]{2,1,0:T(8,128)(2,1)S(1)}, u32[]{:S(2)}, u32[]{:S(2)}) collective-permute-start(bf16[4,256,256]{2,1,0:T(8,128)(2,1)S(1)} %collective-permute-done.5.rest_4_), channel_id=1, source_target_pairs={{0,1},{1,2},{2,3},{3,4},{4,5},{5,6},{6,7},{7,0},{8,9},{9,10},{10,1... | collective-permute-start | bytes 1572872 | tf_op jit(solution)/shard_map/ppermute | solution.py:41
  34.5 4.8 %all-to-all-done.got_ref = bf16[8,64,1152]{2,1,0:T(8,128)(2,1)S(1)} async-done(((bf16[8,64,1152]{2,1,0:T(8,128)(2,1)}), bf16[8,64,1152]{2,1,0:T(8,128)(2,1)S(1)}, u32[]{:S(2)}, u32[]{:S(2)}) %all-to-all-start) | async-done | bytes 1179680 | tf_op jit(solution)/shard_map/all_to_all | solution.py:392
  39.3 1.8 %collective-permute-start.7 = (bf16[4,256,256]{2,1,0:T(8,128)(2,1)S(1)}, bf16[4,256,256]{2,1,0:T(8,128)(2,1)}, u32[]{:S(2)}, u32[]{:S(2)}) collective-permute-start(bf16[4,256,256]{2,1,0:T(8,128)(2,1)S(1)} %pad_maximum_fusion.rest_2_), channel_id=1, source_target_pairs={{0,32},{1,33},{2,34},{3,35},{4,36},{5,37},{6,38},{7,39},{8,40},{9,... | collective-permute-start | bytes 1572872 | tf_op jit(solution)/shard_map/ppermute | solution.py:41
  41.1 0.1 pad_add_fusion.spot_ref
  41.3 0.1 collective-permute-start.8
  41.4 4.4 %prefix_and_own.1 = (bf16[2112,128]{1,0:T(8,128)(2,1)S(1)}, f32[2112,256]{1,0:T(8,128)S(1)}, f32[2112,128]{1,0:T(8,128)S(1)}, s32[33]{0:T(128)S(1)}, s32[33,32]{1,0:T(8,128)S(1)}) custom-call(s32[32,8]{1,0:T(8,128)S(1)} %fusion.ids_ref, s32[32]{0:T(128)S(1)} %copy-done.5, bf16[8,64,1152]{2,1,0:T(8,128)(2,1)S(1)} %all-to-all-done.got_ref), custom_call_target="tpu_custom_call" | custom-call | flops 1207959552 | bytes 6291456 | tf_op jit(solution)/shard_map/prefix_and_own/pallas_call | solution.py:206
  45.9 1.7 %collective-permute-start.12 = (bf16[4,256,256]{2,1,0:T(8,128)(2,1)S(1)}, bf16[4,256,256]{2,1,0:T(8,128)(2,1)S(1)}, u32[]{:S(2)}, u32[]{:S(2)}) collective-permute-start(bf16[4,256,256]{2,1,0:T(8,128)(2,1)S(1)} %collective-permute-done.9.rest_2_), channel_id=1, source_target_pairs={{0,32},{1,33},{2,34},{3,35},{4,36},{5,37},{6,38},{7,39},{8,40},{9,... | collective-permute-start | bytes 1572872 | tf_op jit(solution)/shard_map/ppermute | solution.py:41
  47.6 2.9 %collective-permute-start.13 = (bf16[4,256,256]{2,1,0:T(8,128)(2,1)S(1)}, bf16[4,256,256]{2,1,0:T(8,128)(2,1)S(1)}, u32[]{:S(2)}, u32[]{:S(2)}) collective-permute-start(bf16[4,256,256]{2,1,0:T(8,128)(2,1)S(1)} %collective-permute-done.9.rest_2_), channel_id=1, source_target_pairs={{0,1},{1,2},{2,3},{3,4},{4,5},{5,6},{6,7},{7,0},{8,9},{9,10},{10,1... | collective-permute-start | bytes 1572872 | tf_op jit(solution)/shard_map/ppermute | solution.py:41
  50.5 9.6 %passages.4 = (f32[2112,256]{1,0:T(8,128)S(1)}, f32[2112,128]{1,0:T(8,128)S(1)}) custom-call(s32[3]{0:T(128)S(1)} %pad_add_fusion.spot_ref, s32[33]{0:T(128)S(1)} %get-tuple-element.33.count_ref, s32[33,32]{1,0:T(8,128)S(1)} %get-tuple-element.34.list_ref, ...), custom_call_target="tpu_custom_call", output_to_operand_aliasing={{0}: (4, {}), {1}: (5, {})} | custom-call | flops 8053063680 | bytes 6291456 | tf_op jit(solution)/shard_map/passages/pallas_call | solution.py:340
  60.1 1.1 %collective-permute-done.13.rest_2_ = bf16[4,256,256]{2,1,0:T(8,128)(2,1)S(1)} collective-permute-done((bf16[4,256,256]{2,1,0:T(8,128)(2,1)S(1)}, bf16[4,256,256]{2,1,0:T(8,128)(2,1)S(1)}, u32[]{:S(2)}, u32[]{:S(2)}) %collective-permute-start.13) | collective-permute-done | bytes 524320 | tf_op jit(solution)/shard_map/ppermute | solution.py:41
  61.1 1.0 %collective-permute-start.16 = (bf16[4,256,256]{2,1,0:T(8,128)(2,1)S(1)}, bf16[4,256,256]{2,1,0:T(8,128)(2,1)S(1)}, u32[]{:S(2)}, u32[]{:S(2)}) collective-permute-start(bf16[4,256,256]{2,1,0:T(8,128)(2,1)S(1)} %collective-permute-done.13.rest_2_), channel_id=1, source_target_pairs={{0,32},{1,33},{2,34},{3,35},{4,36},{5,37},{6,38},{7,39},{8,40},{9,... | collective-permute-start | bytes 1572872 | tf_op jit(solution)/shard_map/ppermute | solution.py:41
  62.1 1.3 %collective-permute-done.14.rest_4_ = bf16[4,256,256]{2,1,0:T(8,128)(2,1)S(1)} collective-permute-done((bf16[4,256,256]{2,1,0:T(8,128)(2,1)S(1)}, bf16[4,256,256]{2,1,0:T(8,128)(2,1)S(1)}, u32[]{:S(2)}, u32[]{:S(2)}) %collective-permute-start.14) | collective-permute-done | bytes 524320 | tf_op jit(solution)/shard_map/ppermute | solution.py:41
  63.4 2.6 %collective-permute-start.17 = (bf16[4,256,256]{2,1,0:T(8,128)(2,1)S(1)}, bf16[4,256,256]{2,1,0:T(8,128)(2,1)S(1)}, u32[]{:S(2)}, u32[]{:S(2)}) collective-permute-start(bf16[4,256,256]{2,1,0:T(8,128)(2,1)S(1)} %collective-permute-done.13.rest_2_), channel_id=1, source_target_pairs={{0,1},{1,2},{2,3},{3,4},{4,5},{5,6},{6,7},{7,0},{8,9},{9,10},{10,1... | collective-permute-start | bytes 1572872 | tf_op jit(solution)/shard_map/ppermute | solution.py:41
  66.0 4.4 %passages.5 = (f32[2112,256]{1,0:T(8,128)S(1)}, f32[2112,128]{1,0:T(8,128)S(1)}) custom-call(s32[3]{0:T(128)S(1)} %pad_add_fusion.spot_ref, s32[33]{0:T(128)S(1)} %get-tuple-element.33.count_ref, s32[33,32]{1,0:T(8,128)S(1)} %get-tuple-element.34.list_ref, ...), custom_call_target="tpu_custom_call", output_to_operand_aliasing={{0}: (4, {}), {1}: (5, {})} | custom-call | flops 5368709120 | bytes 6291456 | tf_op jit(solution)/shard_map/passages/pallas_call | solution.py:340
  70.5 5.4 %passages.6 = (f32[2112,256]{1,0:T(8,128)S(1)}, f32[2112,128]{1,0:T(8,128)S(1)}) custom-call(s32[3]{0:T(128)S(1)} %pad_add_fusion.spot_ref, s32[33]{0:T(128)S(1)} %get-tuple-element.33.count_ref, s32[33,32]{1,0:T(8,128)S(1)} %get-tuple-element.34.list_ref, ...), custom_call_target="tpu_custom_call", output_to_operand_aliasing={{0}: (4, {}), {1}: (5, {})} | custom-call | flops 5368709120 | bytes 6291456 | tf_op jit(solution)/shard_map/passages/pallas_call | solution.py:340
  75.8 0.1 collective-permute-start.18
  75.9 1.9 %collective-permute-done.18.rest_3_ = bf16[4,256,256]{2,1,0:T(8,128)(2,1)S(1)} collective-permute-done((bf16[4,256,256]{2,1,0:T(8,128)(2,1)S(1)}, bf16[4,256,256]{2,1,0:T(8,128)(2,1)S(1)}, u32[]{:S(2)}, u32[]{:S(2)}) %collective-permute-start.18) | collective-permute-done | bytes 524320 | tf_op jit(solution)/shard_map/ppermute | solution.py:41
  77.8 3.8 %passages.7 = (f32[2112,256]{1,0:T(8,128)S(1)}, f32[2112,128]{1,0:T(8,128)S(1)}, bf16[512,512]{1,0:T(8,128)(2,1)S(1)}) custom-call(s32[3]{0:T(128)S(1)} %pad_add_fusion.spot_ref, s32[33]{0:T(128)S(1)} %get-tuple-element.33.count_ref, s32[33,32]{1,0:T(8,128)S(1)} %get-tuple-element.34.list_ref, ...), custom_call_target="tpu_custom_call", output_to_operand_aliasing={{0}: (4, {}), {1}: (5, {})} | custom-call | flops 2684354560 | bytes 6291456 | tf_op jit(solution)/shard_map/passages/pallas_call | solution.py:340
  81.6 12.6 %all_to_all.10 = bf16[8,64,512]{2,1,0:T(8,128)(2,1)S(1)} all-to-all(bf16[8,64,512]{2,1,0:T(8,128)(2,1)S(1)} %bitcast.32), channel_id=1, replica_groups={{0,8,64,72,128,136,192,200},{1,9,65,73,129,137,193,201},{2,10,66,74,130..., dimensions={0} | all-to-all | bytes 1048576 | tf_op jit(solution)/shard_map/all_to_all | solution.py:416
  94.2 0.3 copy.19
  94.5 1.0 %reshape.95 = bf16[4,16,4096]{2,1,0:T(8,128)(2,1)} reshape(bf16[64,8,512]{2,1,0:T(8,128)(2,1)S(1)} %copy.19) | data formatting | bytes 1048576 | tf_op jit(solution)/shard_map/reshape | solution.py:417
  (45 shorter events, 0.4 us)
Async XLA Ops:
  0.0 6.6 %copy-start.6 = (s32[4,8]{1,0:T(4,128)S(1)}, s32[4,8]{1,0:T(4,128)}, u32[]{:S(2)}) copy-start(s32[4,8]{1,0:T(4,128)} %param.16) | copy-start | bytes 388
  0.0 6.6 %copy-start.2 = (bf16[128,1024]{1,0:T(8,128)(2,1)S(1)}, bf16[128,1024]{1,0:T(8,128)(2,1)}, u32[]{:S(2)}) copy-start(bf16[128,1024]{1,0:T(8,128)(2,1)} %pv_hbm.1) | copy-start | bytes 786436
  0.0 6.6 %copy-start.1 = (bf16[128,1024]{1,0:T(8,128)(2,1)S(1)}, bf16[128,1024]{1,0:T(8,128)(2,1)}, u32[]{:S(2)}) copy-start(bf16[128,1024]{1,0:T(8,128)(2,1)} %pk_hbm.1) | copy-start | bytes 786436
  0.0 6.6 %copy-start.4 = (bf16[4,16,1024]{2,1,0:T(8,128)(2,1)S(1)}, bf16[4,16,1024]{2,1,0:T(8,128)(2,1)}, u32[]{:S(2)}) copy-start(bf16[4,16,1024]{2,1,0:T(8,128)(2,1)} %param.11) | copy-start | bytes 393220
  0.0 6.6 %copy-start.3 = (bf16[4,16,1024]{2,1,0:T(8,128)(2,1)S(1)}, bf16[4,16,1024]{2,1,0:T(8,128)(2,1)}, u32[]{:S(2)}) copy-start(bf16[4,16,1024]{2,1,0:T(8,128)(2,1)} %param.10) | copy-start | bytes 393220
  0.0 6.6 %copy-start = (bf16[4,16,4096]{2,1,0:T(8,128)(2,1)S(1)}, bf16[4,16,4096]{2,1,0:T(8,128)(2,1)}, u32[]{:S(2)}) copy-start(bf16[4,16,4096]{2,1,0:T(8,128)(2,1)} %param.9) | copy-start | bytes 1572868
  1.3 7.4 %collective-permute-start.2 = (bf16[256,256]{1,0:T(8,128)(2,1)S(1)}, bf16[256,256]{1,0:T(8,128)(2,1)S(1)}, u32[]{:S(2)}, u32[]{:S(2)}) collective-permute-start(bf16[256,256]{1,0:T(8,128)(2,1)S(1)} %get-tuple-element.53), channel_id=1, source_target_pairs={{0,16},{1,17},{2,18},{3,19},{4,20},{5,21},{6,22},{7,23},{8,24},{9,... | collective-permute-start | bytes 393224 | tf_op jit(solution)/shard_map/ppermute | solution.py:41
  5.1 6.1 %collective-permute-start.1 = (bf16[256,256]{1,0:T(8,128)(2,1)S(1)}, bf16[256,256]{1,0:T(8,128)(2,1)S(1)}, u32[]{:S(2)}, u32[]{:S(2)}) collective-permute-start(bf16[256,256]{1,0:T(8,128)(2,1)S(1)} %get-tuple-element.54), channel_id=1, source_target_pairs={{0,24},{1,25},{2,26},{3,27},{4,28},{5,29},{6,30},{7,31},{8,0},{9,1... | collective-permute-start | bytes 393224 | tf_op jit(solution)/shard_map/ppermute | solution.py:41
  5.9 7.2 %collective-permute-start = (bf16[256,256]{1,0:T(8,128)(2,1)S(1)}, bf16[256,256]{1,0:T(8,128)(2,1)S(1)}, u32[]{:S(2)}, u32[]{:S(2)}) collective-permute-start(bf16[256,256]{1,0:T(8,128)(2,1)S(1)} %get-tuple-element.54), channel_id=1, source_target_pairs={{0,8},{1,9},{2,10},{3,11},{4,12},{5,13},{6,14},{7,15},{8,16},{9,17... | collective-permute-start | bytes 393224 | tf_op jit(solution)/shard_map/ppermute | solution.py:41
  13.2 28.2 %copy-start.5 = (s32[32]{0:T(128)S(1)}, s32[32]{0:T(128)}, u32[]{:S(2)}) copy-start(s32[32]{0:T(128)} %at_ref.1) | copy-start | bytes 388
  13.2 12.8 %collective-permute-start.5 = (bf16[4,256,256]{2,1,0:T(8,128)(2,1)S(1)}, bf16[4,256,256]{2,1,0:T(8,128)(2,1)S(1)}, u32[]{:S(2)}, u32[]{:S(2)}) collective-permute-start(bf16[4,256,256]{2,1,0:T(8,128)(2,1)S(1)} %pad_maximum_fusion.rest_2_), channel_id=1, source_target_pairs={{0,1},{1,2},{2,3},{3,4},{4,5},{5,6},{6,7},{7,0},{8,9},{9,10},{10,1... | collective-permute-start | bytes 1572872 | tf_op jit(solution)/shard_map/ppermute | solution.py:41
  17.0 14.8 %collective-permute-start.3 = (bf16[4,256,256]{2,1,0:T(8,128)(2,1)S(1)}, bf16[4,256,256]{2,1,0:T(8,128)(2,1)}, u32[]{:S(2)}, u32[]{:S(2)}) collective-permute-start(bf16[4,256,256]{2,1,0:T(8,128)(2,1)S(1)} %pad_maximum_fusion.rest_2_), channel_id=1, source_target_pairs={{0,7},{1,0},{2,1},{3,2},{4,3},{5,4},{6,5},{7,6},{8,15},{9,8},{10,9... | collective-permute-start | bytes 1572872 | tf_op jit(solution)/shard_map/ppermute | solution.py:41
  17.0 22.3 %all-to-all-start = ((bf16[8,64,1152]{2,1,0:T(8,128)(2,1)}), bf16[8,64,1152]{2,1,0:T(8,128)(2,1)S(1)}, u32[]{:S(2)}, u32[]{:S(2)}) async-start(bf16[8,64,1152]{2,1,0:T(8,128)(2,1)} %parcel.1), calls=%async_computation | async-start | bytes 2359296 | tf_op jit(solution)/shard_map/all_to_all | solution.py:392
  26.0 13.3 %collective-permute-start.6 = (bf16[4,256,256]{2,1,0:T(8,128)(2,1)S(1)}, bf16[4,256,256]{2,1,0:T(8,128)(2,1)}, u32[]{:S(2)}, u32[]{:S(2)}) collective-permute-start(bf16[4,256,256]{2,1,0:T(8,128)(2,1)S(1)} %collective-permute-done.5.rest_4_), channel_id=1, source_target_pairs={{0,32},{1,33},{2,34},{3,35},{4,36},{5,37},{6,38},{7,39},{8,40},{9,... | collective-permute-start | bytes 1572872 | tf_op jit(solution)/shard_map/ppermute | solution.py:41
  31.8 7.5 %collective-permute-start.4 = (bf16[4,256,256]{2,1,0:T(8,128)(2,1)}, bf16[4,256,256]{2,1,0:T(8,128)(2,1)}, u32[]{:S(2)}, u32[]{:S(2)}) collective-permute-start(bf16[4,256,256]{2,1,0:T(8,128)(2,1)} %collective-permute-done.3.rest_6_), channel_id=1, source_target_pairs={{0,32},{1,33},{2,34},{3,35},{4,36},{5,37},{6,38},{7,39},{8,40},{9,... | collective-permute-start | bytes 1572872 | tf_op jit(solution)/shard_map/ppermute | solution.py:41
  31.8 14.0 %collective-permute-start.10 = (bf16[4,256,256]{2,1,0:T(8,128)(2,1)}, bf16[4,256,256]{2,1,0:T(8,128)(2,1)S(1)}, u32[]{:S(2)}, u32[]{:S(2)}) collective-permute-start(bf16[4,256,256]{2,1,0:T(8,128)(2,1)} %collective-permute-done.3.rest_6_), channel_id=1, source_target_pairs={{0,7},{1,0},{2,1},{3,2},{4,3},{5,4},{6,5},{7,6},{8,15},{9,8},{10,9... | collective-permute-start | bytes 1572872 | tf_op jit(solution)/shard_map/ppermute | solution.py:41
  31.8 14.0 %collective-permute-start.9 = (bf16[4,256,256]{2,1,0:T(8,128)(2,1)S(1)}, bf16[4,256,256]{2,1,0:T(8,128)(2,1)S(1)}, u32[]{:S(2)}, u32[]{:S(2)}) collective-permute-start(bf16[4,256,256]{2,1,0:T(8,128)(2,1)S(1)} %collective-permute-done.5.rest_4_), channel_id=1, source_target_pairs={{0,1},{1,2},{2,3},{3,4},{4,5},{5,6},{6,7},{7,0},{8,9},{9,10},{10,1... | collective-permute-start | bytes 1572872 | tf_op jit(solution)/shard_map/ppermute | solution.py:41
  39.3 11.1 %collective-permute-start.7 = (bf16[4,256,256]{2,1,0:T(8,128)(2,1)S(1)}, bf16[4,256,256]{2,1,0:T(8,128)(2,1)}, u32[]{:S(2)}, u32[]{:S(2)}) collective-permute-start(bf16[4,256,256]{2,1,0:T(8,128)(2,1)S(1)} %pad_maximum_fusion.rest_2_), channel_id=1, source_target_pairs={{0,32},{1,33},{2,34},{3,35},{4,36},{5,37},{6,38},{7,39},{8,40},{9,... | collective-permute-start | bytes 1572872 | tf_op jit(solution)/shard_map/ppermute | solution.py:41
  41.3 9.2 %collective-permute-start.8 = (bf16[2,256,256]{2,1,0:T(8,128)(2,1)S(1)}, bf16[2,256,256]{2,1,0:T(8,128)(2,1)S(1)}, u32[]{:S(2)}, u32[]{:S(2)}) collective-permute-start(bf16[2,256,256]{2,1,0:T(8,128)(2,1)S(1)} %bitcast.38), channel_id=1, source_target_pairs={{0,32},{1,33},{2,34},{3,35},{4,36},{5,37},{6,38},{7,39},{8,40},{9,... | collective-permute-start | bytes 786440 | tf_op jit(solution)/shard_map/ppermute | solution.py:41
  45.9 20.1 %collective-permute-start.12 = (bf16[4,256,256]{2,1,0:T(8,128)(2,1)S(1)}, bf16[4,256,256]{2,1,0:T(8,128)(2,1)S(1)}, u32[]{:S(2)}, u32[]{:S(2)}) collective-permute-start(bf16[4,256,256]{2,1,0:T(8,128)(2,1)S(1)} %collective-permute-done.9.rest_2_), channel_id=1, source_target_pairs={{0,32},{1,33},{2,34},{3,35},{4,36},{5,37},{6,38},{7,39},{8,40},{9,... | collective-permute-start | bytes 1572872 | tf_op jit(solution)/shard_map/ppermute | solution.py:41
  47.6 18.4 %collective-permute-start.11 = (bf16[4,256,256]{2,1,0:T(8,128)(2,1)S(1)}, bf16[4,256,256]{2,1,0:T(8,128)(2,1)S(1)}, u32[]{:S(2)}, u32[]{:S(2)}) collective-permute-start(bf16[4,256,256]{2,1,0:T(8,128)(2,1)S(1)} %collective-permute-done.10.rest_4_), channel_id=1, source_target_pairs={{0,32},{1,33},{2,34},{3,35},{4,36},{5,37},{6,38},{7,39},{8,40},{9,... | collective-permute-start | bytes 1572872 | tf_op jit(solution)/shard_map/ppermute | solution.py:41
  47.6 13.6 %collective-permute-start.13 = (bf16[4,256,256]{2,1,0:T(8,128)(2,1)S(1)}, bf16[4,256,256]{2,1,0:T(8,128)(2,1)S(1)}, u32[]{:S(2)}, u32[]{:S(2)}) collective-permute-start(bf16[4,256,256]{2,1,0:T(8,128)(2,1)S(1)} %collective-permute-done.9.rest_2_), channel_id=1, source_target_pairs={{0,1},{1,2},{2,3},{3,4},{4,5},{5,6},{6,7},{7,0},{8,9},{9,10},{10,1... | collective-permute-start | bytes 1572872 | tf_op jit(solution)/shard_map/ppermute | solution.py:41
  50.4 12.9 %collective-permute-start.14 = (bf16[4,256,256]{2,1,0:T(8,128)(2,1)S(1)}, bf16[4,256,256]{2,1,0:T(8,128)(2,1)S(1)}, u32[]{:S(2)}, u32[]{:S(2)}) collective-permute-start(bf16[4,256,256]{2,1,0:T(8,128)(2,1)S(1)} %collective-permute-done.10.rest_4_), channel_id=1, source_target_pairs={{0,7},{1,0},{2,1},{3,2},{4,3},{5,4},{6,5},{7,6},{8,15},{9,8},{10,9... | collective-permute-start | bytes 1572872 | tf_op jit(solution)/shard_map/ppermute | solution.py:41
  61.1 9.3 %collective-permute-start.16 = (bf16[4,256,256]{2,1,0:T(8,128)(2,1)S(1)}, bf16[4,256,256]{2,1,0:T(8,128)(2,1)S(1)}, u32[]{:S(2)}, u32[]{:S(2)}) collective-permute-start(bf16[4,256,256]{2,1,0:T(8,128)(2,1)S(1)} %collective-permute-done.13.rest_2_), channel_id=1, source_target_pairs={{0,32},{1,33},{2,34},{3,35},{4,36},{5,37},{6,38},{7,39},{8,40},{9,... | collective-permute-start | bytes 1572872 | tf_op jit(solution)/shard_map/ppermute | solution.py:41
  63.4 7.1 %collective-permute-start.15 = (bf16[4,256,256]{2,1,0:T(8,128)(2,1)S(1)}, bf16[4,256,256]{2,1,0:T(8,128)(2,1)S(1)}, u32[]{:S(2)}, u32[]{:S(2)}) collective-permute-start(bf16[4,256,256]{2,1,0:T(8,128)(2,1)S(1)} %collective-permute-done.14.rest_4_), channel_id=1, source_target_pairs={{0,32},{1,33},{2,34},{3,35},{4,36},{5,37},{6,38},{7,39},{8,40},{9,... | collective-permute-start | bytes 1572872 | tf_op jit(solution)/shard_map/ppermute | solution.py:41
  63.4 12.4 %collective-permute-start.17 = (bf16[4,256,256]{2,1,0:T(8,128)(2,1)S(1)}, bf16[4,256,256]{2,1,0:T(8,128)(2,1)S(1)}, u32[]{:S(2)}, u32[]{:S(2)}) collective-permute-start(bf16[4,256,256]{2,1,0:T(8,128)(2,1)S(1)} %collective-permute-done.13.rest_2_), channel_id=1, source_target_pairs={{0,1},{1,2},{2,3},{3,4},{4,5},{5,6},{6,7},{7,0},{8,9},{9,10},{10,1... | collective-permute-start | bytes 1572872 | tf_op jit(solution)/shard_map/ppermute | solution.py:41
  75.8 2.0 %collective-permute-start.18 = (bf16[4,256,256]{2,1,0:T(8,128)(2,1)S(1)}, bf16[4,256,256]{2,1,0:T(8,128)(2,1)S(1)}, u32[]{:S(2)}, u32[]{:S(2)}) collective-permute-start(bf16[4,256,256]{2,1,0:T(8,128)(2,1)S(1)} %collective-permute-done.17.rest_2_), channel_id=1, source_target_pairs={{0,32},{1,33},{2,34},{3,35},{4,36},{5,37},{6,38},{7,39},{8,40},{9,... | collective-permute-start | bytes 1572872 | tf_op jit(solution)/shard_map/ppermute | solution.py:41
